TPU v7x, 256 devices: a whole 4x4x8 slice. The times are simulated.
256 devices in a mesh: units: 256 (over y, x, z, core).
Axes of the slice: x: 4, y: 4, z: 8, core: 2. Of those that a mesh axis runs over, the one named last changes fastest.
Arguments:
- unit_data: bfloat16 [524288, 384], P('units'), may hold values from -6 to 6
- owner: int32 [1], replicated, may hold values from 0 to 255
Outputs:
- owner_grad: float32 [2048, 256], replicated
- local_grad: float32 [524288, 256], P('units')
All inputs are finite; a program needn't handle non-finite values.
Results may differ from a plain program's by a relative error of at most 0.0022.
Values may be sent and summed in bfloat16 or wider, within the bound.
No kernel may reach another device: no remote copies, remote signals or barrier semaphores. Data moves between devices by JAX's collectives and lax.ppermute only.
A program may use at most 64 MiB of HBM per device.

v0:
```python
import math

import jax
import jax.numpy as jnp
from jax import lax
from jax.sharding import PartitionSpec as P

D = 256
COLS = 64


def from_root(x, axis, root):
    mine = lax.axis_index(axis) == root
    return lax.psum(jnp.where(mine, x, jnp.zeros_like(x)), axis)


def pair_terms(owner_block, unit_block):
    owner_feat = owner_block[:, :D]
    owner_sol = owner_block[:, D : D + COLS]
    owner_probe = owner_block[:, D + COLS :]
    unit_feat = unit_block[:, :D]
    unit_sol = unit_block[:, D : D + COLS]
    unit_probe = unit_block[:, D + COLS :]
    owner_wide = owner_feat.astype(jnp.float32)
    unit_wide = unit_feat.astype(jnp.float32)
    owner_sq = jnp.sum(owner_wide * owner_wide, axis=1)
    unit_sq = jnp.sum(unit_wide * unit_wide, axis=1)
    contract_last = (((1,), (1,)), ((), ()))
    cross = lax.dot_general(
        owner_feat, unit_feat, contract_last, preferred_element_type=jnp.float32
    )
    kernel = jnp.exp(-(owner_sq[:, None] + unit_sq[None, :] - 2.0 * cross) / (2.0 * D))
    weight = lax.dot_general(
        owner_sol, unit_probe, contract_last, preferred_element_type=jnp.float32
    )
    weight = weight + lax.dot_general(
        owner_probe, unit_sol, contract_last, preferred_element_type=jnp.float32
    )
    weight = weight * (0.5 / math.sqrt(COLS))
    mixed = weight * kernel
    mixed_b = mixed.astype(jnp.bfloat16)
    owner_term = (
        jnp.dot(mixed_b, unit_feat, preferred_element_type=jnp.float32)
        - jnp.sum(mixed, axis=1)[:, None] * owner_wide
    )
    contract_first = (((0,), (0,)), ((), ()))
    local_term = (
        lax.dot_general(mixed_b, owner_feat, contract_first, preferred_element_type=jnp.float32)
        - jnp.sum(mixed, axis=0)[:, None] * unit_wide
    )
    return (owner_term, local_term)


def local(unit_data, owner):
    row_count = unit_data.shape[0]
    device_count = lax.axis_size("units")
    owner_block = from_root(unit_data, "units", owner[0])
    block_size = min(512, row_count)
    owner_parts = []
    local_total = jnp.zeros((row_count, D), jnp.float32)
    for block_index in range(row_count // block_size):
        owner_piece = owner_block[block_index * block_size : (block_index + 1) * block_size]
        owner_part, local_part = pair_terms(owner_piece, unit_data)
        owner_parts.append(owner_part)
        local_total = local_total + local_part
    owner_term = jnp.concatenate(owner_parts, axis=0)
    summed = lax.psum(owner_term, "units")
    owner_grad = summed * (1.0 / math.sqrt(row_count * device_count))
    local_grad = local_total * (1.0 / math.sqrt(row_count))
    return (owner_grad, local_grad)


def solution(mesh):
    in_specs = (P("units", None), P())
    out_specs = (P(), P("units", None))
    return jax.shard_map(local, mesh=mesh, in_specs=in_specs, out_specs=out_specs, check_vma=False)
```

profile of v0, /device:TPU:1, one launch (start us, length us, event | category | flops | bytes accessed | tf_op | source)
XLA Modules:
  0.0 569.0 jit_solution(11121365655887773946)
XLA Ops:
  7.9 1.3 broadcast_select_fusion
  10.2 265.2 %all-reduce.3.cloned.1.call-done = bf16[2048,384]{1,0:T(8,128)(2,1)} async-done(((bf16[2048,384]{1,0:T(8,128)(2,1)}), bf16[2048,384]{1,0:T(8,128)(2,1)}) %all-reduce.3.cloned.1.call-update) | async-done | bytes 1572880 | tf_op jit(solution)/shard_map/psum | solution.py:14
  275.4 1.8 fusion.30
  277.5 0.8 fusion.21
  278.3 0.7 fusion.33
  279.1 0.8 fusion.23
  279.9 0.7 fusion.36
  280.6 0.8 fusion.25
  281.4 0.7 fusion.39
  282.2 0.8 fusion.27
  283.0 2.4 fusion.57
  285.4 0.7 convolution_subtract_fusion.4
  286.7 2.2 fusion.58
  289.0 0.7 convolution_subtract_fusion.5
  290.3 2.2 fusion.59
  292.5 0.7 convolution_subtract_fusion.6
  293.8 2.2 fusion.60
  297.3 1.5 pad_maximum_fusion
  298.8 2.6 convolution_subtract_fusion.3
  301.5 1.1 fusion.2
  303.1 1.1 fusion.1
  304.6 2.5 fusion.3
  307.1 251.9 %all-reduce.5.cloned.1.call-done = f32[2048,256]{1,0:T(8,128)} async-done(((f32[2048,256]{1,0:T(8,128)}), f32[2048,256]{1,0:T(8,128)}) %all-reduce.5.cloned.1.call-update) | async-done | bytes 2097168 | tf_op jit(solution)/shard_map/psum | solution.py:67
  559.0 3.1 broadcast_multiply_fusion
  (25 shorter events, 5.6 us)
Async XLA Ops:
  7.2 268.2 %all-reduce.3.cloned.1.call-start = ((), (), s32[]{:S(2)}) async-start(), calls=%async_computation | async-start | bytes 3145728 | tf_op jit(solution)/shard_map/psum | solution.py:14
  7.9 2.0 copy-start
  9.2 549.8 %all-reduce.5.cloned.1.call-start = ((), (), s32[]{:S(2)}) async-start(), calls=%async_computation.1 | async-start | bytes 4194304 | tf_op jit(solution)/shard_map/psum | solution.py:67
  275.4 1.8 copy-start.1
  285.4 1.4 copy-start.2
  289.0 1.3 copy-start.4
  292.5 1.3 copy-start.6
  296.0 1.3 copy-start.8
  298.8 2.7 copy-start.7
  301.5 1.6 copy-start.5
  303.0 1.6 copy-start.3
Sparse Core Ops, SparseCore 0:
  13.9 261.3 all-reduce.2
  298.9 260.0 all-reduce.4
where the time goes:
time: 570 us; the launch traced here: 569 us
  waiting for transfers between devices  517 us (91%)
  matrix products  26.3 us (5%)
  between operations  14.9 us (3%)
  other arithmetic  6.55 us (1%)
    psum x1, waiting for transfers between devices, from_root(): return lax.psum(jnp.where(mine, x, jnp.zeros_like(x)), axis)  265 us
    psum x1, waiting for transfers between devices, local(): summed = lax.psum(owner_term, 'units')  252 us
  transfers between devices with their start and end apart: 2, of which 2 were waited for; matrix products, arithmetic and copies ran while one was open for 1% of the time, Pallas kernels for 0%

commit v1 on v0

v1 whole, which is shorter than its diff:
```python
import math

import jax
import jax.numpy as jnp
import numpy as np
from jax import lax
from jax.sharding import Mesh
from jax.sharding import PartitionSpec as P

D = 256
COLS = 64
PLANE = ("y", "x")
ALL = ("y", "x", "z", "c")
NY, NX, NZ, NC = 4, 4, 8, 2


def swap(v):
    return lax.ppermute(v, "c", [(0, 1), (1, 0)])


def exchange(v, axis):
    return lax.all_to_all(v, axis, 0, 0, tiled=True)


def pick(v, parts, index):
    rows = v.shape[0] // parts
    return lax.dynamic_slice_in_dim(v, index * rows, rows, 0)


def repeat(v, parts):
    return jnp.broadcast_to(v[None], (parts, *v.shape)).reshape(parts * v.shape[0], *v.shape[1:])


def broadcast_half(mine, theirs, owner):
    oc = owner % NC
    oz = owner // NC % NZ
    plane = owner // (NC * NZ)
    half = jnp.where(oc == lax.axis_index("c"), mine, theirs)
    piece = pick(exchange(half, PLANE), NY * NX, plane)
    piece = pick(exchange(repeat(piece, NZ), "z"), NZ, oz)
    return exchange(repeat(piece, NY * NX), PLANE)


def reduce_half(term):
    rows = term.shape[0] // (NY * NX)
    piece = jnp.sum(exchange(term, PLANE).reshape(NY * NX, rows, D), axis=0)
    piece = jnp.sum(exchange(repeat(piece, NZ), "z").reshape(NZ, rows, D), axis=0)
    return exchange(repeat(piece, NY * NX), PLANE)


def pair_terms(owner_block, unit_block):
    owner_feat = owner_block[:, :D]
    unit_feat = unit_block[:, :D]
    owner_wide = owner_feat.astype(jnp.float32)
    unit_wide = unit_feat.astype(jnp.float32)
    owner_sq = jnp.sum(owner_wide * owner_wide, axis=1)
    unit_sq = jnp.sum(unit_wide * unit_wide, axis=1)
    contract_last = (((1,), (1,)), ((), ()))
    cross = lax.dot_general(owner_feat, unit_feat, contract_last, preferred_element_type=jnp.float32)
    kernel = jnp.exp(-(owner_sq[:, None] + unit_sq[None, :] - 2.0 * cross) / (2.0 * D))
    swapped = jnp.concatenate([unit_block[:, D + COLS :], unit_block[:, D : D + COLS]], axis=1)
    weight = lax.dot_general(owner_block[:, D:], swapped, contract_last, preferred_element_type=jnp.float32)
    mixed = weight * (0.5 / math.sqrt(COLS)) * kernel
    mixed_b = mixed.astype(jnp.bfloat16)
    owner_term = (
        jnp.dot(mixed_b, unit_feat, preferred_element_type=jnp.float32)
        - jnp.sum(mixed, axis=1)[:, None] * owner_wide
    )
    contract_first = (((0,), (0,)), ((), ()))
    local_term = (
        lax.dot_general(mixed_b, owner_feat, contract_first, preferred_element_type=jnp.float32)
        - jnp.sum(mixed, axis=0)[:, None] * unit_wide
    )
    return (owner_term, local_term)


def local(unit_data, owner):
    rows = unit_data.shape[0]
    half_rows = rows // NC
    core = lax.axis_index("c")
    here = pick(unit_data, NC, core)
    there = pick(unit_data, NC, 1 - core)
    here_other = swap(there)
    there_other = swap(here)
    owner_half = broadcast_half(here, here_other, owner[0])
    both = jnp.concatenate([here, there, here_other, there_other], axis=0)
    owner_term, local_term = pair_terms(owner_half, both)
    summed = reduce_half(owner_term) * (1.0 / math.sqrt(rows * NY * NX * NZ * NC))
    summed_other = swap(summed)
    owner_grad = jnp.concatenate(
        [jnp.where(core == 0, summed, summed_other), jnp.where(core == 0, summed_other, summed)], axis=0
    )
    received = swap(local_term[rows:])
    local_sum = (local_term[:rows] + jnp.concatenate([received[half_rows:], received[:half_rows]], axis=0)) * (
        1.0 / math.sqrt(rows)
    )
    first = local_sum[:half_rows]
    second = local_sum[half_rows:]
    local_grad = jnp.concatenate(
        [jnp.where(core == 0, first, second), jnp.where(core == 0, second, first)], axis=0
    )
    return (owner_grad, local_grad)


def solution(mesh):
    grid = Mesh(np.asarray(mesh.devices).reshape(NY, NX, NZ, NC), ALL)
    in_specs = (P(ALL, None), P())
    out_specs = (P(), P(ALL, None))
    return jax.shard_map(local, mesh=grid, in_specs=in_specs, out_specs=out_specs, check_vma=False)
```

time: 570 us -> 164 us (0.29)
  waiting for transfers between devices: 517 us -> 37.2 us
  starting transfers between devices: 0.08 us -> 35.3 us
  blocking collectives: 0 us -> 35.2 us
  between operations: 14.9 us -> 1.49 us
  local copies, waits for them, and re-layouts: 4.03 us -> 11.3 us
  other arithmetic: 6.55 us -> 13.8 us
    psum x2 -> x0, waiting for transfers between devices: 517 us -> none  [the longest x1 265 us: from_root(): return lax.psum(jnp.where(mine, x, jnp.zeros_like(x)), axis)]
    all_to_all x0 -> x4, waiting for transfers between devices: none -> 35.9 us  [exchange(): return lax.all_to_all(v, axis, 0, 0, tiled=True)]
    all_to_all x0 -> x2, blocking collectives: none -> 35.2 us  [exchange(): return lax.all_to_all(v, axis, 0, 0, tiled=True)]
    all_to_all x0 -> x4, starting transfers between devices: none -> 23.4 us  [exchange(): return lax.all_to_all(v, axis, 0, 0, tiled=True)]
    ppermute x0 -> x4, starting transfers between devices: none -> 11.9 us  [swap(): return lax.ppermute(v, 'c', [(0, 1), (1, 0)])]
    dot_general x4 -> x1, matrix products: 4.03 us -> 9.93 us  [pair_terms(): lax.dot_general(owner_feat, unit_feat, contract_last, preferred_element_t...]
    dot_general x8 -> x1, matrix products: 12.1 us -> 9.77 us  [pair_terms(): lax.dot_general(owner_block[:, D:], swapped, contract_last, preferred_ele...]
  transfers between devices with their start and end apart: 2 -> 8, of which waited for: 2 -> 5; matrix products, arithmetic and copies ran while one was open for 1% -> 9% of each run, Pallas kernels for 0% -> 0%
where the time goes in v1:
time: 164 us; the launch traced here: 163 us
  waiting for transfers between devices  37.2 us (23%)
  starting transfers between devices  35.3 us (22%)
  blocking collectives  35.2 us (21%)
  matrix products  28.9 us (18%)
  other arithmetic  13.8 us (8%)
  local copies, waits for them, and re-layouts  11.3 us (7%)
    all_to_all x4, waiting for transfers between devices, exchange(): return lax.all_to_all(v, axis, 0, 0, tiled=True)  35.9 us
    all_to_all x2, blocking collectives, exchange(): return lax.all_to_all(v, axis, 0, 0, tiled=True)  35.2 us
    all_to_all x4, starting transfers between devices, exchange(): return lax.all_to_all(v, axis, 0, 0, tiled=True)  23.4 us
    ppermute x4, starting transfers between devices, swap(): return lax.ppermute(v, 'c', [(0, 1), (1, 0)])  11.9 us
    dot_general x1, matrix products, pair_terms(): lax.dot_general(owner_feat, unit_feat, contract_last, preferred_element_t...  9.93 us
    dot_general x1, matrix products, pair_terms(): lax.dot_general(owner_block[:, D:], swapped, contract_last, preferred_ele...  9.77 us
    dot_general x1, matrix products, pair_terms(): lax.dot_general(mixed_b, owner_feat, contract_first, preferred_element_ty...  5.41 us
    unnamed x12, local copies, waits for them, and re-layouts  3.98 us
  transfers between devices with their start and end apart: 8, of which 5 were waited for; matrix products, arithmetic and copies ran while one was open for 9% of the time, Pallas kernels for 0%

profile of v1, /device:TPU:1, one launch (start us, length us, event | category | flops | bytes accessed | tf_op | source)
XLA Modules:
  0.0 163.2 jit_solution(10392748986594429788)
XLA Ops:
  1.9 3.3 %collective-permute-start = (bf16[1024,384]{1,0:T(8,128)(2,1)S(1)}, bf16[1024,384]{1,0:T(8,128)(2,1)S(1)}, u32[]{:S(2)}, u32[]{:S(2)}) collective-permute-start(bf16[1024,384]{1,0:T(8,128)(2,1)S(1)} %constant_dynamic-slice_fusion.2), channel_id=1, source_target_pairs={{0,1},{1,0},{2,3},{3,2},{4,5},{5,4},{6,7},{7,6},{8,9},{9,8},{10,11... | collective-permute-start | bytes 2359304 | tf_op jit(solution)/shard_map/ppermute | solution.py:18
  7.1 2.6 %broadcast_select_fusion = (bf16[1024,384]{1,0:T(8,128)(2,1)}, bf16[1024,384]{1,0:T(8,128)(2,1)S(1)}) fusion(bf16[1024,384]{1,0:T(8,128)(2,1)S(1)} %collective-permute-done, pred[]{:T(512)S(6)} %eq.13, bf16[2048,384]{1,0:T(8,128)(2,1)} %param.2, s32[]{:T(128)S(6)} %select_n.61), kind=kLoop, calls=%fused_computation.26 | loop fusion | flops 393216 | bytes 3145733 | tf_op jit(solution)/shard_map/jit(_where)/select_n | solution.py:38
  9.7 5.0 %all-to-all-start = ((bf16[16,64,384]{2,1,0:T(8,128)(2,1)}), bf16[16,64,384]{2,1,0:T(8,128)(2,1)S(1)}, u32[]{:S(2)}, u32[]{:S(2)}) async-start(bf16[16,64,384]{2,1,0:T(8,128)(2,1)} %bitcast.1), calls=%async_computation | async-start | bytes 1572864 | tf_op jit(solution)/shard_map/all_to_all | solution.py:22
  15.4 12.8 %all-to-all-done = bf16[16,64,384]{2,1,0:T(8,128)(2,1)S(1)} async-done(((bf16[16,64,384]{2,1,0:T(8,128)(2,1)}), bf16[16,64,384]{2,1,0:T(8,128)(2,1)S(1)}, u32[]{:S(2)}, u32[]{:S(2)}) %all-to-all-start) | async-done | bytes 786464 | tf_op jit(solution)/shard_map/all_to_all | solution.py:22
  29.0 8.2 %all-to-all-start.1 = ((bf16[8,64,384]{2,1,0:T(8,128)(2,1)}), bf16[8,64,384]{2,1,0:T(8,128)(2,1)S(1)}, u32[]{:S(2)}, u32[]{:S(2)}) async-start(bf16[8,64,384]{2,1,0:T(8,128)(2,1)} %broadcast_in_dim.8), calls=%async_computation.1 | async-start | bytes 786432 | tf_op jit(solution)/shard_map/all_to_all | solution.py:22
  37.2 2.2 %pad_maximum_fusion = bf16[4096,384]{1,0:T(8,128)(2,1)S(1)} fusion(bf16[1024,384]{1,0:T(8,128)(2,1)} %collective-permute-done.1, bf16[1024,384]{1,0:T(8,128)(2,1)} %copy-done.3, bf16[1024,384]{1,0:T(8,128)(2,1)} %copy-done.2, bf16[1024,384]{1,0:T(8,128)(2,1)} %copy-done.4), kind=kLoop, calls=%fused_computation.9 | loop fusion | flops 12582912 | bytes 6291456 | tf_op jit(solution)/shard_map/concatenate | solution.py:86
  40.0 9.4 %all-to-all-done.1 = bf16[8,64,384]{2,1,0:T(8,128)(2,1)S(1)} async-done(((bf16[8,64,384]{2,1,0:T(8,128)(2,1)}), bf16[8,64,384]{2,1,0:T(8,128)(2,1)S(1)}, u32[]{:S(2)}, u32[]{:S(2)}) %all-to-all-start.1) | async-done | bytes 393248 | tf_op jit(solution)/shard_map/all_to_all | solution.py:22
  50.4 6.1 %all-to-all-start.2 = ((bf16[16,64,384]{2,1,0:T(8,128)(2,1)}), bf16[16,64,384]{2,1,0:T(8,128)(2,1)}, u32[]{:S(2)}, u32[]{:S(2)}) async-start(bf16[16,64,384]{2,1,0:T(8,128)(2,1)} %broadcast_in_dim.9), calls=%async_computation.2 | async-start | bytes 1572864 | tf_op jit(solution)/shard_map/all_to_all | solution.py:22
  56.5 1.8 %fusion.26 = (bf16[4096,64]{1,0:T(8,128)(2,1)}, bf16[4096,64]{1,0:T(8,128)(2,1)}) fusion(bf16[4096,384]{1,0:T(8,128)(2,1)S(1)} %pad_maximum_fusion), kind=kLoop, calls=%fused_computation.39 | loop fusion | bytes 2097152 | tf_op jit(solution)/shard_map/slice | solution.py:61
  58.3 10.9 %all-to-all-done.2 = bf16[16,64,384]{2,1,0:T(8,128)(2,1)} async-done(((bf16[16,64,384]{2,1,0:T(8,128)(2,1)}), bf16[16,64,384]{2,1,0:T(8,128)(2,1)}, u32[]{:S(2)}, u32[]{:S(2)}) %all-to-all-start.2) | async-done | bytes 786464 | tf_op jit(solution)/shard_map/all_to_all | solution.py:22
  70.5 9.8 %fusion.17 = f32[1024,4096]{1,0:T(8,128)} fusion(bf16[4096,64]{1,0:T(8,128)(2,1)} %get-tuple-element.7, bf16[4096,64]{1,0:T(8,128)(2,1)} %get-tuple-element.6, bf16[1024,384]{1,0:T(8,128)(2,1)} %bitcast.4), kind=kOutput, calls=%fused_computation.20 | convolution fusion | flops 1075838976 | bytes 19136512 | tf_op jit(solution)/shard_map/dot_general | solution.py:62
  80.3 9.9 %fusion.25 = (f32[4096]{0:T(1024)S(1)}, f32[1024]{0:T(1024)S(1)}, bf16[1024,4096]{1,0:T(8,128)(2,1)S(1)}) fusion(bf16[4096,384]{1,0:T(8,128)(2,1)S(1)} %pad_maximum_fusion, bf16[1024,384]{1,0:T(8,128)(2,1)} %bitcast.4, f32[4096]{0:T(1024)S(1)} %fusion, f32[1024]{0:T(1024)S(1)} %fusion.16, f32[1024,4096]{1,0:T(8,128)} %fusion.17), kind=kOutput, calls=%fused_computation.38 | convolution fusion | flops 2189421568 | bytes 27828224 | tf_op jit(solution)/shard_map/dot_general | solution.py:59
  90.2 3.8 %fusion.11 = f32[1024,256]{1,0:T(8,128)S(1)} fusion(bf16[4096,384]{1,0:T(8,128)(2,1)S(1)} %pad_maximum_fusion, bf16[1024,4096]{1,0:T(8,128)(2,1)S(1)} %get-tuple-element.14, f32[1024]{0:T(1024)S(1)} %get-tuple-element.3, bf16[1024,384]{1,0:T(8,128)(2,1)} %bitcast.4), kind=kOutput, calls=%fused_computation.18 | convolution fusion | flops 2148270080 | bytes 12062720 | tf_op jit(solution)/shard_map/dot_general | solution.py:66
  94.0 19.3 %all_to_all.51 = f32[16,64,256]{2,1,0:T(8,128)} all-to-all(f32[16,64,256]{2,1,0:T(8,128)S(1)} %bitcast.16), channel_id=1, replica_groups=mesh['y'=4,'x'=4,'z'=8,'c'=2] {'y','x'}, dimensions={0} | all-to-all | bytes 2097152 | tf_op jit(solution)/shard_map/all_to_all | solution.py:22
  115.4 4.1 %all-to-all-start.4 = ((f32[8,64,256]{2,1,0:T(8,128)}), f32[8,64,256]{2,1,0:T(8,128)}, u32[]{:S(2)}, u32[]{:S(2)}) async-start(f32[8,64,256]{2,1,0:T(8,128)} %broadcast_in_dim.10), calls=%async_computation.4 | async-start | bytes 1048576 | tf_op jit(solution)/shard_map/all_to_all | solution.py:22
  119.5 5.4 %fusion.1 = f32[4096,256]{1,0:T(8,128)S(1)} fusion(bf16[1024,4096]{1,0:T(8,128)(2,1)} %copy-done.5, f32[4096]{0:T(1024)S(1)} %get-tuple-element.2, bf16[4096,384]{1,0:T(8,128)(2,1)S(1)} %pad_maximum_fusion, bf16[1024,384]{1,0:T(8,128)(2,1)} %bitcast.4), kind=kOutput, calls=%fused_computation.4 | convolution fusion | flops 2150629376 | bytes 15220736 | tf_op jit(solution)/shard_map/dot_general | solution.py:71
  125.0 1.9 %copy-done = f32[4096,256]{1,0:T(8,128)} copy-done((f32[4096,256]{1,0:T(8,128)}, f32[4096,256]{1,0:T(8,128)S(1)}, u32[]{:S(2)}) %copy-start) | copy-done | bytes 4194328
  128.3 2.9 %collective-permute-start.3 = (f32[2048,256]{1,0:T(8,128)}, f32[2048,256]{1,0:T(8,128)S(1)}, u32[]{:S(2)}, u32[]{:S(2)}) collective-permute-start(f32[2048,256]{1,0:T(8,128)} %slice.50), channel_id=1, source_target_pairs={{0,1},{1,0},{2,3},{3,2},{4,5},{5,4},{6,7},{7,6},{8,9},{9,8},{10,11... | collective-permute-start | bytes 6291464 | tf_op jit(solution)/shard_map/ppermute | solution.py:18
  131.2 2.8 %all-to-all-done.4 = f32[8,64,256]{2,1,0:T(8,128)} async-done(((f32[8,64,256]{2,1,0:T(8,128)}), f32[8,64,256]{2,1,0:T(8,128)}, u32[]{:S(2)}, u32[]{:S(2)}) %all-to-all-start.4) | async-done | bytes 524320 | tf_op jit(solution)/shard_map/all_to_all | solution.py:22
  135.2 16.0 %all_to_all.52 = f32[16,64,256]{2,1,0:T(8,128)S(1)} all-to-all(f32[16,64,256]{2,1,0:T(8,128)S(1)} %broadcast_in_dim.11), channel_id=1, replica_groups=mesh['y'=4,'x'=4,'z'=8,'c'=2] {'y','x'}, dimensions={0} | all-to-all | bytes 2097152 | tf_op jit(solution)/shard_map/all_to_all | solution.py:22
  151.3 4.9 %collective-permute-start.2 = (f32[1024,256]{1,0:T(8,128)S(1)}, f32[1024,256]{1,0:T(8,128)}, u32[]{:S(2)}, u32[]{:S(2)}) collective-permute-start(f32[1024,256]{1,0:T(8,128)S(1)} %bitcast.15), channel_id=1, source_target_pairs={{0,1},{1,0},{2,3},{3,2},{4,5},{5,4},{6,7},{7,6},{8,9},{9,8},{10,11... | collective-permute-start | bytes 3145736 | tf_op jit(solution)/shard_map/ppermute | solution.py:18
  156.4 2.0 %copy-done.1 = f32[4096,256]{1,0:T(8,128)S(1)} copy-done((f32[4096,256]{1,0:T(8,128)S(1)}, f32[4096,256]{1,0:T(8,128)}, u32[]{:S(2)}) %copy-start.1) | copy-done | bytes 4194328
  158.7 1.6 slice_select_fusion.1
  160.3 1.5 pad_maximum_fusion.2
  (31 shorter events, 13.6 us)
Async XLA Ops:
  1.9 35.3 %copy-start.2 = (bf16[1024,384]{1,0:T(8,128)(2,1)}, bf16[1024,384]{1,0:T(8,128)(2,1)S(1)}, u32[]{:S(2)}) copy-start(bf16[1024,384]{1,0:T(8,128)(2,1)S(1)} %constant_dynamic-slice_fusion.2) | copy-start | bytes 2359300
  1.9 5.2 %collective-permute-start = (bf16[1024,384]{1,0:T(8,128)(2,1)S(1)}, bf16[1024,384]{1,0:T(8,128)(2,1)S(1)}, u32[]{:S(2)}, u32[]{:S(2)}) collective-permute-start(bf16[1024,384]{1,0:T(8,128)(2,1)S(1)} %constant_dynamic-slice_fusion.2), channel_id=1, source_target_pairs={{0,1},{1,0},{2,3},{3,2},{4,5},{5,4},{6,7},{7,6},{8,9},{9,8},{10,11... | collective-permute-start | bytes 2359304 | tf_op jit(solution)/shard_map/ppermute | solution.py:18
  7.1 30.1 %copy-start.3 = (bf16[1024,384]{1,0:T(8,128)(2,1)}, bf16[1024,384]{1,0:T(8,128)(2,1)S(1)}, u32[]{:S(2)}) copy-start(bf16[1024,384]{1,0:T(8,128)(2,1)S(1)} %collective-permute-done) | copy-start | bytes 2359300
  9.7 27.5 %copy-start.4 = (bf16[1024,384]{1,0:T(8,128)(2,1)}, bf16[1024,384]{1,0:T(8,128)(2,1)S(1)}, u32[]{:S(2)}) copy-start(bf16[1024,384]{1,0:T(8,128)(2,1)S(1)} %get-tuple-element.5) | copy-start | bytes 2359300
  9.7 18.5 %all-to-all-start = ((bf16[16,64,384]{2,1,0:T(8,128)(2,1)}), bf16[16,64,384]{2,1,0:T(8,128)(2,1)S(1)}, u32[]{:S(2)}, u32[]{:S(2)}) async-start(bf16[16,64,384]{2,1,0:T(8,128)(2,1)} %bitcast.1), calls=%async_computation | async-start | bytes 1572864 | tf_op jit(solution)/shard_map/all_to_all | solution.py:22
  14.7 22.5 %collective-permute-start.1 = (bf16[1024,384]{1,0:T(8,128)(2,1)S(1)}, bf16[1024,384]{1,0:T(8,128)(2,1)}, u32[]{:S(2)}, u32[]{:S(2)}) collective-permute-start(bf16[1024,384]{1,0:T(8,128)(2,1)S(1)} %get-tuple-element.5), channel_id=1, source_target_pairs={{0,1},{1,0},{2,3},{3,2},{4,5},{5,4},{6,7},{7,6},{8,9},{9,8},{10,11... | collective-permute-start | bytes 2359304 | tf_op jit(solution)/shard_map/ppermute | solution.py:18
  29.0 20.4 %all-to-all-start.1 = ((bf16[8,64,384]{2,1,0:T(8,128)(2,1)}), bf16[8,64,384]{2,1,0:T(8,128)(2,1)S(1)}, u32[]{:S(2)}, u32[]{:S(2)}) async-start(bf16[8,64,384]{2,1,0:T(8,128)(2,1)} %broadcast_in_dim.8), calls=%async_computation.1 | async-start | bytes 786432 | tf_op jit(solution)/shard_map/all_to_all | solution.py:22
  50.4 18.8 %all-to-all-start.2 = ((bf16[16,64,384]{2,1,0:T(8,128)(2,1)}), bf16[16,64,384]{2,1,0:T(8,128)(2,1)}, u32[]{:S(2)}, u32[]{:S(2)}) async-start(bf16[16,64,384]{2,1,0:T(8,128)(2,1)} %broadcast_in_dim.9), calls=%async_computation.2 | async-start | bytes 1572864 | tf_op jit(solution)/shard_map/all_to_all | solution.py:22
  90.2 3.8 %copy-start.5 = (bf16[1024,4096]{1,0:T(8,128)(2,1)}, bf16[1024,4096]{1,0:T(8,128)(2,1)S(1)}, u32[]{:S(2)}) copy-start(bf16[1024,4096]{1,0:T(8,128)(2,1)S(1)} %get-tuple-element.14) | copy-start | bytes 25165828
  115.4 18.6 %all-to-all-start.4 = ((f32[8,64,256]{2,1,0:T(8,128)}), f32[8,64,256]{2,1,0:T(8,128)}, u32[]{:S(2)}, u32[]{:S(2)}) async-start(f32[8,64,256]{2,1,0:T(8,128)} %broadcast_in_dim.10), calls=%async_computation.4 | async-start | bytes 1048576 | tf_op jit(solution)/shard_map/all_to_all | solution.py:22
  124.9 1.9 %copy-start = (f32[4096,256]{1,0:T(8,128)}, f32[4096,256]{1,0:T(8,128)S(1)}, u32[]{:S(2)}) copy-start(f32[4096,256]{1,0:T(8,128)S(1)} %fusion.1) | copy-start | bytes 12582916
  128.3 27.9 %collective-permute-start.3 = (f32[2048,256]{1,0:T(8,128)}, f32[2048,256]{1,0:T(8,128)S(1)}, u32[]{:S(2)}, u32[]{:S(2)}) collective-permute-start(f32[2048,256]{1,0:T(8,128)} %slice.50), channel_id=1, source_target_pairs={{0,1},{1,0},{2,3},{3,2},{4,5},{5,4},{6,7},{7,6},{8,9},{9,8},{10,11... | collective-permute-start | bytes 6291464 | tf_op jit(solution)/shard_map/ppermute | solution.py:18
  151.3 7.4 %collective-permute-start.2 = (f32[1024,256]{1,0:T(8,128)S(1)}, f32[1024,256]{1,0:T(8,128)}, u32[]{:S(2)}, u32[]{:S(2)}) collective-permute-start(f32[1024,256]{1,0:T(8,128)S(1)} %bitcast.15), channel_id=1, source_target_pairs={{0,1},{1,0},{2,3},{3,2},{4,5},{5,4},{6,7},{7,6},{8,9},{9,8},{10,11... | collective-permute-start | bytes 3145736 | tf_op jit(solution)/shard_map/ppermute | solution.py:18
  156.2 2.2 %copy-start.1 = (f32[4096,256]{1,0:T(8,128)S(1)}, f32[4096,256]{1,0:T(8,128)}, u32[]{:S(2)}) copy-start(f32[4096,256]{1,0:T(8,128)} %copy-done) | copy-start | bytes 12582916

commit v2 on v1

v2 whole, which is shorter than its diff:
```python
import functools
import math

import jax
import jax.numpy as jnp
import numpy as np
from jax import lax
from jax.experimental import pallas as pl
from jax.experimental.pallas import tpu as pltpu
from jax.sharding import Mesh
from jax.sharding import PartitionSpec as P

D = 256
COLS = 64
WIDE = D + 2 * COLS
PLANE = ("y", "x")
ALL = ("y", "x", "z", "c")
NY, NX, NZ, NC = 4, 4, 8, 2
NP = NY * NX
LOG2E = math.log2(math.e)
TILE_UNITS = 1024
TILE_OWNER = 256
SCALE_ROWS = 16


def swap(v):
    return lax.ppermute(v, "c", [(0, 1), (1, 0)])


def shift(v, k):
    return lax.ppermute(v, "z", [(i, (i + k) % NZ) for i in range(NZ)])


def exchange(v):
    return lax.all_to_all(v, PLANE, 0, 0, tiled=True)


def pick(v, parts, index):
    rows = v.shape[0] // parts
    return lax.dynamic_slice_in_dim(v, index * rows, rows, 0)


def repeat(v):
    return jnp.broadcast_to(v[None], (NP, *v.shape))


def along_z(v, root):
    away = (lax.axis_index("z") - root) % NZ
    v = jnp.where(away == 4, shift(v, 4), v)
    up, down, two = shift(v, 1), shift(v, -1), shift(v, 2)
    step = away % 4
    return jnp.where(step == 0, v, jnp.where(step == 1, up, jnp.where(step == 3, down, two)))


def sum_z(v):
    v = v + shift(v, 4)
    return (v + shift(v, 2)) + (shift(v, 1) + shift(v, -1))


def broadcast_half(block, owner):
    core = lax.axis_index("c")
    other = swap(pick(block, NC, 1 - core))
    half = jnp.where(owner % NC == core, pick(block, NC, core), other)
    piece = pick(exchange(half), NP, owner // (NC * NZ))
    piece = along_z(piece, owner // NC % NZ)
    return exchange(repeat(piece)).reshape(half.shape)


def pack(v):
    top = jnp.max(jnp.abs(v), axis=(-2, -1), keepdims=True)
    power = jnp.floor(jnp.log2(jnp.maximum(top, 1e-30))) - 13.0
    scaled = (v * jnp.exp2(-power)).astype(jnp.float16)
    extra = jnp.broadcast_to(power, (*v.shape[:-2], SCALE_ROWS, v.shape[-1])).astype(jnp.float16)
    return jnp.concatenate([scaled, extra], axis=-2)


def unpack(v, factor=1.0):
    scale = jnp.exp2(v[..., -SCALE_ROWS : 1 - SCALE_ROWS, :1].astype(jnp.float32)) * factor
    return v[..., :-SCALE_ROWS, :].astype(jnp.float32) * scale


def reduce_half(term, factor):
    rows = term.shape[0] // NP
    piece = jnp.sum(unpack(exchange(pack(term.reshape(NP, rows, D)))), axis=0)
    piece = sum_z(piece)
    mine = exchange(repeat(pack(piece)))
    other = swap(mine)
    first = lax.axis_index("c") == 0
    mine = unpack(mine, factor).reshape(term.shape)
    other = unpack(other, factor).reshape(term.shape)
    return jnp.concatenate([jnp.where(first, mine, other), jnp.where(first, other, mine)], axis=0)


def mix_kernel(own_ref, unit_ref, sq_ref, mix_ref, term_ref, col_ref, own_sq, row_sum, *, steps):
    j = pl.program_id(0)
    rows = own_ref.shape[0]
    spans = [slice(i, i + TILE_OWNER) for i in range(0, rows, TILE_OWNER)]

    @pl.when(j == 0)
    def _():
        term_ref[...] = jnp.zeros_like(term_ref)
        row_sum[...] = jnp.zeros_like(row_sum)
        for span in spans:
            feat = own_ref[span, :D].astype(jnp.float32)
            own_sq[span, :] = jnp.sum(feat * feat, axis=1, keepdims=True) * (LOG2E / (2.0 * D)) + math.log2(
                2.0 * math.sqrt(COLS)
            )

    feat = unit_ref[:, :D]
    swapped = jnp.concatenate([unit_ref[:, D + COLS :], unit_ref[:, D : D + COLS]], axis=1)
    col = jnp.zeros(col_ref.shape, jnp.float32)
    contract_last = (((1,), (1,)), ((), ()))
    for span in spans:
        cross = lax.dot_general(own_ref[span, :D], feat, contract_last, preferred_element_type=jnp.float32)
        weight = lax.dot_general(own_ref[span, D:], swapped, contract_last, preferred_element_type=jnp.float32)
        mixed = weight * jnp.exp2(cross * (LOG2E / D) - sq_ref[...] - own_sq[span, :])
        mixed_b = mixed.astype(jnp.bfloat16)
        mix_ref[span, :] = mixed_b
        term_ref[span, :] += jnp.dot(mixed_b, feat, preferred_element_type=jnp.float32)
        col = col + jnp.sum(mixed.reshape(-1, *col.shape), axis=0)
        lanes = mixed[:, :128]
        for start in range(128, mixed.shape[1], 128):
            lanes = lanes + mixed[:, start : start + 128]
        row_sum[span, :] += lanes
    col_ref[...] = col

    @pl.when(j == steps - 1)
    def _():
        for span in spans:
            total = jnp.sum(row_sum[span, :], axis=1, keepdims=True)
            term_ref[span, :] -= total * own_ref[span, :D].astype(jnp.float32)


def mix(own, units, unit_sq):
    rows, count = own.shape[0], units.shape[0]
    steps = count // TILE_UNITS
    return pl.pallas_call(
        functools.partial(mix_kernel, steps=steps),
        grid=(steps,),
        in_specs=[
            pl.BlockSpec((rows, WIDE), lambda j: (0, 0)),
            pl.BlockSpec((TILE_UNITS, WIDE), lambda j: (j, 0)),
            pl.BlockSpec((1, TILE_UNITS), lambda j: (0, j)),
        ],
        out_specs=[
            pl.BlockSpec((rows, TILE_UNITS), lambda j: (0, j)),
            pl.BlockSpec((rows, D), lambda j: (0, 0)),
            pl.BlockSpec((8, TILE_UNITS), lambda j: (0, j)),
        ],
        out_shape=[
            jax.ShapeDtypeStruct((rows, count), jnp.bfloat16),
            jax.ShapeDtypeStruct((rows, D), jnp.float32),
            jax.ShapeDtypeStruct((8, count), jnp.float32),
        ],
        scratch_shapes=[pltpu.VMEM((rows, 1), jnp.float32), pltpu.VMEM((rows, 128), jnp.float32)],
        compiler_params=pltpu.CompilerParams(
            vmem_limit_bytes=24 * 2**20, dimension_semantics=("arbitrary",)
        ),
        cost_estimate=pl.CostEstimate(
            flops=2 * rows * count * (WIDE + D),
            bytes_accessed=2 * rows * count + 2 * WIDE * (rows + count) + 4 * rows * D,
            transcendentals=rows * count,
        ),
    )(own, units, unit_sq)


def local(unit_data, owner):
    rows = unit_data.shape[0]
    owner_half = broadcast_half(unit_data, owner[0])
    both = jnp.concatenate([unit_data, swap(unit_data)], axis=0)
    both_wide = both[:, :D].astype(jnp.float32)
    unit_sq = jnp.sum(both_wide * both_wide, axis=1) * (LOG2E / (2.0 * D))
    mixed_b, owner_term, col_parts = mix(owner_half, both, unit_sq[None, :])
    owner_grad = reduce_half(owner_term, 1.0 / math.sqrt(rows * NP * NZ * NC))
    contract_first = (((0,), (0,)), ((), ()))
    local_term = (
        lax.dot_general(mixed_b, owner_half[:, :D], contract_first, preferred_element_type=jnp.float32)
        - jnp.sum(col_parts, axis=0)[:, None] * both_wide
    )
    local_grad = (local_term[:rows] + swap(local_term[rows:])) * (1.0 / math.sqrt(rows))
    return (owner_grad, local_grad)


def solution(mesh):
    grid = Mesh(np.asarray(mesh.devices).reshape(NY, NX, NZ, NC), ALL)
    in_specs = (P(ALL, None), P())
    out_specs = (P(), P(ALL, None))
    return jax.shard_map(local, mesh=grid, in_specs=in_specs, out_specs=out_specs, check_vma=False)
```

time: 164 us -> 145 us (0.88)
  matrix products: 28.9 us -> 5.4 us
  Pallas kernels: 0 us -> 10.6 us
  blocking collectives: 35.2 us -> 28.2 us
  waiting for transfers between devices: 37.2 us -> 31.8 us
  local copies, waits for them, and re-layouts: 11.3 us -> 15.7 us
  starting transfers between devices: 35.3 us -> 39.6 us
  other arithmetic: 13.8 us -> 10.2 us
    dot_general x4 -> x1, matrix products: 28.9 us -> 5.4 us  [local(): lax.dot_general(mixed_b, owner_half[:, :D], contract_first, preferred_ele...]
    ppermute x0 -> x8, starting transfers between devices: none -> 17.9 us  [shift(): return lax.ppermute(v, 'z', [(i, (i + k) % NZ) for i in range(NZ)])]
    all_to_all x4 -> x2, waiting for transfers between devices: 35.9 us -> 20.9 us  [exchange(): return lax.all_to_all(v, PLANE, 0, 0, tiled=True)]
    all_to_all x4 -> x2, starting transfers between devices: 23.4 us -> 9.54 us  [exchange(): return lax.all_to_all(v, PLANE, 0, 0, tiled=True)]
    pallas_call x0 -> x1, Pallas kernels: none -> 10.6 us  [mix(): pl.pallas_call(functools.partial(mix_kernel, steps=steps), grid=(steps,),...]
    ppermute x0 -> x8, waiting for transfers between devices: none -> 8.01 us  [shift(): return lax.ppermute(v, 'z', [(i, (i + k) % NZ) for i in range(NZ)])]
    all_to_all x2, blocking collectives: 35.2 us -> 28.2 us  [exchange(): return lax.all_to_all(v, PLANE, 0, 0, tiled=True)]
    unnamed x12 -> x14, local copies, waits for them, and re-layouts: 3.98 us -> 10 us
  transfers between devices with their start and end apart: 8 -> 14, of which waited for: 5 -> 8; matrix products, arithmetic and copies ran while one was open for 9% -> 10% of each run, Pallas kernels for 0% -> 0%
where the time goes in v2:
time: 145 us; the launch traced here: 144 us
  starting transfers between devices  39.6 us (27%)
  waiting for transfers between devices  31.8 us (22%)
  blocking collectives  28.2 us (19%)
  local copies, waits for them, and re-layouts  15.7 us (11%)
  Pallas kernels  10.6 us (7%)
  other arithmetic  10.2 us (7%)
  matrix products  5.4 us (4%)
  between operations  2.28 us (2%)
    all_to_all x2, blocking collectives, exchange(): return lax.all_to_all(v, PLANE, 0, 0, tiled=True)  28.2 us
    all_to_all x2, waiting for transfers between devices, exchange(): return lax.all_to_all(v, PLANE, 0, 0, tiled=True)  20.9 us
    ppermute x8, starting transfers between devices, shift(): return lax.ppermute(v, 'z', [(i, (i + k) % NZ) for i in range(NZ)])  17.9 us
    ppermute x4, starting transfers between devices, swap(): return lax.ppermute(v, 'c', [(0, 1), (1, 0)])  12.2 us
    pallas_call x1, Pallas kernels, mix(): pl.pallas_call(functools.partial(mix_kernel, steps=steps), grid=(steps,),...  10.6 us
    unnamed x14, local copies, waits for them, and re-layouts  10 us
    all_to_all x2, starting transfers between devices, exchange(): return lax.all_to_all(v, PLANE, 0, 0, tiled=True)  9.54 us
    ppermute x8, waiting for transfers between devices, shift(): return lax.ppermute(v, 'z', [(i, (i + k) % NZ) for i in range(NZ)])  8.01 us
  transfers between devices with their start and end apart: 14, of which 8 were waited for; matrix products, arithmetic and copies ran while one was open for 10% of the time, Pallas kernels for 0%

profile of v2, /device:TPU:1, one launch (start us, length us, event | category | flops | bytes accessed | tf_op | source)
XLA Modules:
  0.0 143.8 jit_solution(13714814911648079707)
XLA Ops:
  1.9 3.3 %collective-permute-start = (bf16[1024,384]{1,0:T(8,128)(2,1)S(1)}, bf16[1024,384]{1,0:T(8,128)(2,1)S(1)}, u32[]{:S(2)}, u32[]{:S(2)}) collective-permute-start(bf16[1024,384]{1,0:T(8,128)(2,1)S(1)} %constant_dynamic-slice_fusion.1), channel_id=1, source_target_pairs={{0,1},{1,0},{2,3},{3,2},{4,5},{5,4},{6,7},{7,6},{8,9},{9,8},{10,11... | collective-permute-start | bytes 2359304 | tf_op jit(solution)/shard_map/ppermute | solution.py:27
  7.1 2.2 %dynamic-slice_select_fusion = bf16[1024,384]{1,0:T(8,128)(2,1)} fusion(bf16[1024,384]{1,0:T(8,128)(2,1)S(1)} %collective-permute-done, bf16[2048,384]{1,0:T(8,128)(2,1)} %param.2, s32[]{:T(128)S(6)} %select_n.96, pred[]{:T(512)S(6)} %eq.26), kind=kLoop, calls=%fused_computation.14 | loop fusion | flops 393216 | bytes 2359301 | tf_op jit(solution)/shard_map/jit(_where)/select_n | solution.py:63
  9.3 5.0 %all-to-all-start = ((bf16[16,64,384]{2,1,0:T(8,128)(2,1)}), bf16[16,64,384]{2,1,0:T(8,128)(2,1)S(1)}, u32[]{:S(2)}, u32[]{:S(2)}) async-start(bf16[16,64,384]{2,1,0:T(8,128)(2,1)} %bitcast.1), calls=%async_computation | async-start | bytes 1572864 | tf_op jit(solution)/shard_map/all_to_all | solution.py:35
  15.1 12.8 %all-to-all-done = bf16[16,64,384]{2,1,0:T(8,128)(2,1)S(1)} async-done(((bf16[16,64,384]{2,1,0:T(8,128)(2,1)}), bf16[16,64,384]{2,1,0:T(8,128)(2,1)S(1)}, u32[]{:S(2)}, u32[]{:S(2)}) %all-to-all-start) | async-done | bytes 786464 | tf_op jit(solution)/shard_map/all_to_all | solution.py:35
  27.9 6.9 %collective-permute-start.1 = (bf16[64,384]{1,0:T(8,128)(2,1)S(1)}, bf16[64,384]{1,0:T(8,128)(2,1)S(1)}, u32[]{:S(2)}, u32[]{:S(2)}) collective-permute-start(bf16[64,384]{1,0:T(8,128)(2,1)S(1)} %constant_dynamic-slice_fusion), channel_id=1, source_target_pairs={{0,8},{2,10},{4,12},{6,14},{8,0},{10,2},{12,4},{14,6},{1,9},{3,11}... | collective-permute-start | bytes 147464 | tf_op jit(solution)/shard_map/ppermute | solution.py:31
  36.3 1.5 %collective-permute-start.4 = (bf16[64,384]{1,0:T(8,128)(2,1)S(1)}, bf16[64,384]{1,0:T(8,128)(2,1)S(1)}, u32[]{:S(2)}, u32[]{:S(2)}) collective-permute-start(bf16[64,384]{1,0:T(8,128)(2,1)S(1)} %broadcast_select_fusion), channel_id=1, source_target_pairs={{0,4},{2,6},{4,8},{6,10},{8,12},{10,14},{12,0},{14,2},{1,5},{3,7},... | collective-permute-start | bytes 147464 | tf_op jit(solution)/shard_map/ppermute | solution.py:31
  37.8 2.7 %collective-permute-start.3 = (bf16[64,384]{1,0:T(8,128)(2,1)S(1)}, bf16[64,384]{1,0:T(8,128)(2,1)S(1)}, u32[]{:S(2)}, u32[]{:S(2)}) collective-permute-start(bf16[64,384]{1,0:T(8,128)(2,1)S(1)} %broadcast_select_fusion), channel_id=1, source_target_pairs={{0,14},{2,0},{4,2},{6,4},{8,6},{10,8},{12,10},{14,12},{1,15},{3,1}... | collective-permute-start | bytes 147464 | tf_op jit(solution)/shard_map/ppermute | solution.py:31
  40.5 1.6 %constant_dynamic-update-slice_fusion.1 = bf16[4096,384]{1,0:T(8,128)(2,1)S(1)} fusion(bf16[2048,384]{1,0:T(8,128)(2,1)} %param.2), kind=kLoop, calls=%fused_computation.24 | loop fusion | bytes 3145728
  42.4 2.4 %collective-permute-done.2 = bf16[64,384]{1,0:T(8,128)(2,1)S(1)} collective-permute-done((bf16[64,384]{1,0:T(8,128)(2,1)S(1)}, bf16[64,384]{1,0:T(8,128)(2,1)S(1)}, u32[]{:S(2)}, u32[]{:S(2)}) %collective-permute-start.2) | collective-permute-done | bytes 49184 | tf_op jit(solution)/shard_map/ppermute | solution.py:31
  45.8 4.5 %all-to-all-start.1 = ((bf16[16,64,384]{2,1,0:T(8,128)(2,1)}), bf16[16,64,384]{2,1,0:T(8,128)(2,1)}, u32[]{:S(2)}, u32[]{:S(2)}) async-start(bf16[16,64,384]{2,1,0:T(8,128)(2,1)} %broadcast_in_dim.6), calls=%async_computation.1 | async-start | bytes 1572864 | tf_op jit(solution)/shard_map/all_to_all | solution.py:35
  50.3 1.7 %constant_dynamic-update-slice_fusion.unit_ref = bf16[4096,384]{1,0:T(8,128)(2,1)S(1)} fusion(bf16[4096,384]{1,0:T(8,128)(2,1)S(1)} %constant_dynamic-update-slice_fusion.1, bf16[2048,384]{1,0:T(8,128)(2,1)} %collective-permute-done.5), kind=kLoop, calls=%fused_computation.23 | loop fusion | bytes 3145728 | tf_op jit(solution)/shard_map/concatenate | solution.py:170
  52.7 8.1 %all-to-all-done.1 = bf16[16,64,384]{2,1,0:T(8,128)(2,1)} async-done(((bf16[16,64,384]{2,1,0:T(8,128)(2,1)}), bf16[16,64,384]{2,1,0:T(8,128)(2,1)}, u32[]{:S(2)}, u32[]{:S(2)}) %all-to-all-start.1) | async-done | bytes 786464 | tf_op jit(solution)/shard_map/all_to_all | solution.py:35
  60.8 10.6 %shard_map.41 = (bf16[1024,4096]{1,0:T(8,128)(2,1)S(1)}, f32[1024,256]{1,0:T(8,128)S(1)}, f32[8,4096]{1,0:T(8,128)S(1)}) custom-call(bf16[1024,384]{1,0:T(8,128)(2,1)} %bitcast.3.own_ref, bf16[4096,384]{1,0:T(8,128)(2,1)S(1)} %constant_dynamic-update-slice_fusion.unit_ref, f32[1,4096]{1,0:T(1,128)S(1)} %bitcast.20), custom_call_target="tpu_custom_call" | custom-call | flops 5368709120 | bytes 13369344 | tf_op jit(solution)/shard_map/pallas_call | solution.py:137
  71.5 3.2 %copy-done.1 = bf16[1024,4096]{1,0:T(8,128)(2,1)} copy-done((bf16[1024,4096]{1,0:T(8,128)(2,1)}, bf16[1024,4096]{1,0:T(8,128)(2,1)S(1)}, u32[]{:S(2)}) %copy-start.1) | copy-done | bytes 8388632
  77.7 12.6 %all_to_all.27 = f16[16,80,256]{2,1,0:T(8,128)(2,1)S(1)} all-to-all(f16[16,80,256]{2,1,0:T(8,128)(2,1)S(1)} %pad_maximum_fusion.1), channel_id=1, replica_groups=mesh['y'=4,'x'=4,'z'=8,'c'=2] {'y','x'}, dimensions={0} | all-to-all | bytes 1310720 | tf_op jit(solution)/shard_map/all_to_all | solution.py:35
  92.5 4.0 %collective-permute-start.6 = (f32[64,256]{1,0:T(8,128)S(1)}, f32[64,256]{1,0:T(8,128)S(1)}, u32[]{:S(2)}, u32[]{:S(2)}) collective-permute-start(f32[64,256]{1,0:T(8,128)S(1)} %multiply_reduce_fusion), channel_id=1, source_target_pairs={{0,8},{2,10},{4,12},{6,14},{8,0},{10,2},{12,4},{14,6},{1,9},{3,11}... | collective-permute-start | bytes 196616 | tf_op jit(solution)/shard_map/ppermute | solution.py:31
  96.6 3.8 %collective-permute-done.6 = f32[64,256]{1,0:T(8,128)S(1)} collective-permute-done((f32[64,256]{1,0:T(8,128)S(1)}, f32[64,256]{1,0:T(8,128)S(1)}, u32[]{:S(2)}, u32[]{:S(2)}) %collective-permute-start.6) | collective-permute-done | bytes 65568 | tf_op jit(solution)/shard_map/ppermute | solution.py:31
  100.5 1.6 %collective-permute-start.8 = (f32[64,256]{1,0:T(8,128)S(1)}, f32[64,256]{1,0:T(8,128)S(1)}, u32[]{:S(2)}, u32[]{:S(2)}) collective-permute-start(f32[64,256]{1,0:T(8,128)S(1)} %add.58), channel_id=1, source_target_pairs={{0,2},{2,4},{4,6},{6,8},{8,10},{10,12},{12,14},{14,0},{1,3},{3,5},... | collective-permute-start | bytes 196616 | tf_op jit(solution)/shard_map/ppermute | solution.py:31
  103.2 5.4 %convolution_subtract_fusion = f32[4096,256]{1,0:T(8,128)S(1)} fusion(bf16[1024,4096]{1,0:T(8,128)(2,1)} %copy-done.1, f32[4096]{0:T(1024)S(1)} %reduce_sum.29, bf16[4096,384]{1,0:T(8,128)(2,1)S(1)} %constant_dynamic-update-slice_fusion.unit_ref, bf16[1024,384]{1,0:T(8,128)(2,1)} %bitcast.3.own_ref), kind=kOutput, calls=%fused_computation.2 | convolution fusion | flops 2150629376 | bytes 15220736 | tf_op jit(solution)/shard_map/dot_general | solution.py:177
  108.6 1.9 %copy-done.2 = f32[4096,256]{1,0:T(8,128)} copy-done((f32[4096,256]{1,0:T(8,128)}, f32[4096,256]{1,0:T(8,128)S(1)}, u32[]{:S(2)}) %copy-start.2) | copy-done | bytes 4194328
  112.0 7.0 %collective-permute-start.11 = (f32[2048,256]{1,0:T(8,128)}, f32[2048,256]{1,0:T(8,128)S(1)}, u32[]{:S(2)}, u32[]{:S(2)}) collective-permute-start(f32[2048,256]{1,0:T(8,128)} %slice.49), channel_id=1, source_target_pairs={{0,1},{1,0},{2,3},{3,2},{4,5},{5,4},{6,7},{7,6},{8,9},{9,8},{10,11... | collective-permute-start | bytes 6291464 | tf_op jit(solution)/shard_map/ppermute | solution.py:27
  120.5 15.6 %all_to_all.28 = f16[16,80,256]{2,1,0:T(8,128)(2,1)S(1)} all-to-all(f16[16,80,256]{2,1,0:T(8,128)(2,1)S(1)} %broadcast_in_dim.8), channel_id=1, replica_groups=mesh['y'=4,'x'=4,'z'=8,'c'=2] {'y','x'}, dimensions={0} | all-to-all | bytes 1310720 | tf_op jit(solution)/shard_map/all_to_all | solution.py:35
  137.3 1.6 %collective-permute-done.10 = f16[16,80,256]{2,1,0:T(8,128)(2,1)S(1)} collective-permute-done((f16[16,80,256]{2,1,0:T(8,128)(2,1)S(1)}, f16[16,80,256]{2,1,0:T(8,128)(2,1)S(1)}, u32[]{:S(2)}, u32[]{:S(2)}) %collective-permute-start.10) | collective-permute-done | bytes 655392 | tf_op jit(solution)/shard_map/ppermute | solution.py:27
  142.0 1.8 %fusion.1 = f32[2048,256]{1,0:T(8,128)} fusion(f32[2048,256]{1,0:T(8,128)S(1)} %collective-permute-done.11, f32[4096,256]{1,0:T(8,128)S(1)} %copy-done.3), kind=kLoop, calls=%fused_computation.5 | loop fusion | flops 1048576 | bytes 6291456 | tf_op jit(solution)/shard_map/mul | solution.py:180
  (55 shorter events, 19.5 us)
Async XLA Ops:
  1.9 5.2 %collective-permute-start = (bf16[1024,384]{1,0:T(8,128)(2,1)S(1)}, bf16[1024,384]{1,0:T(8,128)(2,1)S(1)}, u32[]{:S(2)}, u32[]{:S(2)}) collective-permute-start(bf16[1024,384]{1,0:T(8,128)(2,1)S(1)} %constant_dynamic-slice_fusion.1), channel_id=1, source_target_pairs={{0,1},{1,0},{2,3},{3,2},{4,5},{5,4},{6,7},{7,6},{8,9},{9,8},{10,11... | collective-permute-start | bytes 2359304 | tf_op jit(solution)/shard_map/ppermute | solution.py:27
  9.3 18.5 %all-to-all-start = ((bf16[16,64,384]{2,1,0:T(8,128)(2,1)}), bf16[16,64,384]{2,1,0:T(8,128)(2,1)S(1)}, u32[]{:S(2)}, u32[]{:S(2)}) async-start(bf16[16,64,384]{2,1,0:T(8,128)(2,1)} %bitcast.1), calls=%async_computation | async-start | bytes 1572864 | tf_op jit(solution)/shard_map/all_to_all | solution.py:35
  14.3 36.0 %collective-permute-start.5 = (bf16[2048,384]{1,0:T(8,128)(2,1)}, bf16[2048,384]{1,0:T(8,128)(2,1)}, u32[]{:S(2)}, u32[]{:S(2)}) collective-permute-start(bf16[2048,384]{1,0:T(8,128)(2,1)} %param.2), channel_id=1, source_target_pairs={{0,1},{1,0},{2,3},{3,2},{4,5},{5,4},{6,7},{7,6},{8,9},{9,8},{10,11... | collective-permute-start | bytes 4718600 | tf_op jit(solution)/shard_map/ppermute | solution.py:27
  27.9 8.4 %collective-permute-start.1 = (bf16[64,384]{1,0:T(8,128)(2,1)S(1)}, bf16[64,384]{1,0:T(8,128)(2,1)S(1)}, u32[]{:S(2)}, u32[]{:S(2)}) collective-permute-start(bf16[64,384]{1,0:T(8,128)(2,1)S(1)} %constant_dynamic-slice_fusion), channel_id=1, source_target_pairs={{0,8},{2,10},{4,12},{6,14},{8,0},{10,2},{12,4},{14,6},{1,9},{3,11}... | collective-permute-start | bytes 147464 | tf_op jit(solution)/shard_map/ppermute | solution.py:31
  36.3 6.1 %collective-permute-start.4 = (bf16[64,384]{1,0:T(8,128)(2,1)S(1)}, bf16[64,384]{1,0:T(8,128)(2,1)S(1)}, u32[]{:S(2)}, u32[]{:S(2)}) collective-permute-start(bf16[64,384]{1,0:T(8,128)(2,1)S(1)} %broadcast_select_fusion), channel_id=1, source_target_pairs={{0,4},{2,6},{4,8},{6,10},{8,12},{10,14},{12,0},{14,2},{1,5},{3,7},... | collective-permute-start | bytes 147464 | tf_op jit(solution)/shard_map/ppermute | solution.py:31
  37.8 4.6 %collective-permute-start.3 = (bf16[64,384]{1,0:T(8,128)(2,1)S(1)}, bf16[64,384]{1,0:T(8,128)(2,1)S(1)}, u32[]{:S(2)}, u32[]{:S(2)}) collective-permute-start(bf16[64,384]{1,0:T(8,128)(2,1)S(1)} %broadcast_select_fusion), channel_id=1, source_target_pairs={{0,14},{2,0},{4,2},{6,4},{8,6},{10,8},{12,10},{14,12},{1,15},{3,1}... | collective-permute-start | bytes 147464 | tf_op jit(solution)/shard_map/ppermute | solution.py:31
  40.5 4.3 %collective-permute-start.2 = (bf16[64,384]{1,0:T(8,128)(2,1)S(1)}, bf16[64,384]{1,0:T(8,128)(2,1)S(1)}, u32[]{:S(2)}, u32[]{:S(2)}) collective-permute-start(bf16[64,384]{1,0:T(8,128)(2,1)S(1)} %broadcast_select_fusion), channel_id=1, source_target_pairs={{0,2},{2,4},{4,6},{6,8},{8,10},{10,12},{12,14},{14,0},{1,3},{3,5},... | collective-permute-start | bytes 147464 | tf_op jit(solution)/shard_map/ppermute | solution.py:31
  45.8 15.1 %all-to-all-start.1 = ((bf16[16,64,384]{2,1,0:T(8,128)(2,1)}), bf16[16,64,384]{2,1,0:T(8,128)(2,1)}, u32[]{:S(2)}, u32[]{:S(2)}) async-start(bf16[16,64,384]{2,1,0:T(8,128)(2,1)} %broadcast_in_dim.6), calls=%async_computation.1 | async-start | bytes 1572864 | tf_op jit(solution)/shard_map/all_to_all | solution.py:35
  71.5 3.2 %copy-start.1 = (bf16[1024,4096]{1,0:T(8,128)(2,1)}, bf16[1024,4096]{1,0:T(8,128)(2,1)S(1)}, u32[]{:S(2)}) copy-start(bf16[1024,4096]{1,0:T(8,128)(2,1)S(1)} %get-tuple-element.6) | copy-start | bytes 25165828
  74.7 1.0 copy-start
  90.4 0.8 copy-start.4
  92.5 7.8 %collective-permute-start.6 = (f32[64,256]{1,0:T(8,128)S(1)}, f32[64,256]{1,0:T(8,128)S(1)}, u32[]{:S(2)}, u32[]{:S(2)}) collective-permute-start(f32[64,256]{1,0:T(8,128)S(1)} %multiply_reduce_fusion), channel_id=1, source_target_pairs={{0,8},{2,10},{4,12},{6,14},{8,0},{10,2},{12,4},{14,6},{1,9},{3,11}... | collective-permute-start | bytes 196616 | tf_op jit(solution)/shard_map/ppermute | solution.py:31
  100.4 18.6 %collective-permute-start.9 = (f32[64,256]{1,0:T(8,128)S(1)}, f32[64,256]{1,0:T(8,128)S(1)}, u32[]{:S(2)}, u32[]{:S(2)}) collective-permute-start(f32[64,256]{1,0:T(8,128)S(1)} %add.58), channel_id=1, source_target_pairs={{0,14},{2,0},{4,2},{6,4},{8,6},{10,8},{12,10},{14,12},{1,15},{3,1}... | collective-permute-start | bytes 196616 | tf_op jit(solution)/shard_map/ppermute | solution.py:31
  100.5 18.5 %collective-permute-start.8 = (f32[64,256]{1,0:T(8,128)S(1)}, f32[64,256]{1,0:T(8,128)S(1)}, u32[]{:S(2)}, u32[]{:S(2)}) collective-permute-start(f32[64,256]{1,0:T(8,128)S(1)} %add.58), channel_id=1, source_target_pairs={{0,2},{2,4},{4,6},{6,8},{8,10},{10,12},{12,14},{14,0},{1,3},{3,5},... | collective-permute-start | bytes 196616 | tf_op jit(solution)/shard_map/ppermute | solution.py:31
  102.1 16.9 %collective-permute-start.7 = (f32[64,256]{1,0:T(8,128)S(1)}, f32[64,256]{1,0:T(8,128)S(1)}, u32[]{:S(2)}, u32[]{:S(2)}) collective-permute-start(f32[64,256]{1,0:T(8,128)S(1)} %add.58), channel_id=1, source_target_pairs={{0,4},{2,6},{4,8},{6,10},{8,12},{10,14},{12,0},{14,2},{1,5},{3,7},... | collective-permute-start | bytes 196616 | tf_op jit(solution)/shard_map/ppermute | solution.py:31
  108.6 1.9 %copy-start.2 = (f32[4096,256]{1,0:T(8,128)}, f32[4096,256]{1,0:T(8,128)S(1)}, u32[]{:S(2)}) copy-start(f32[4096,256]{1,0:T(8,128)S(1)} %convolution_subtract_fusion) | copy-start | bytes 12582916
  112.0 28.8 %collective-permute-start.11 = (f32[2048,256]{1,0:T(8,128)}, f32[2048,256]{1,0:T(8,128)S(1)}, u32[]{:S(2)}, u32[]{:S(2)}) collective-permute-start(f32[2048,256]{1,0:T(8,128)} %slice.49), channel_id=1, source_target_pairs={{0,1},{1,0},{2,3},{3,2},{4,5},{5,4},{6,7},{7,6},{8,9},{9,8},{10,11... | collective-permute-start | bytes 6291464 | tf_op jit(solution)/shard_map/ppermute | solution.py:27
  136.0 2.8 %collective-permute-start.10 = (f16[16,80,256]{2,1,0:T(8,128)(2,1)S(1)}, f16[16,80,256]{2,1,0:T(8,128)(2,1)S(1)}, u32[]{:S(2)}, u32[]{:S(2)}) collective-permute-start(f16[16,80,256]{2,1,0:T(8,128)(2,1)S(1)} %all_to_all.28), channel_id=1, source_target_pairs={{0,1},{1,0},{2,3},{3,2},{4,5},{5,4},{6,7},{7,6},{8,9},{9,8},{10,11... | collective-permute-start | bytes 1966088 | tf_op jit(solution)/shard_map/ppermute | solution.py:27
  139.0 3.0 %copy-start.3 = (f32[4096,256]{1,0:T(8,128)S(1)}, f32[4096,256]{1,0:T(8,128)}, u32[]{:S(2)}) copy-start(f32[4096,256]{1,0:T(8,128)} %copy-done.2) | copy-start | bytes 12582916

commit v3 on v2

--- a/solution.py
+++ b/solution.py
@@ -57,13 +57,29 @@
     return (v + shift(v, 2)) + (shift(v, 1) + shift(v, -1))
 
 
+def tie(*values):
+    return lax.optimization_barrier(values)
+
+
 def broadcast_half(block, owner):
     core = lax.axis_index("c")
-    other = swap(pick(block, NC, 1 - core))
-    half = jnp.where(owner % NC == core, pick(block, NC, core), other)
+    there = pick(block, NC, 1 - core)
+    here = pick(block, NC, core)
+    other = swap(there)
+    here, other = tie(here, other)
+    half = jnp.where(owner % NC == core, here, other)
     piece = pick(exchange(half), NP, owner // (NC * NZ))
+    piece, block = tie(piece, block)
+    partner = swap(block)
+    squares = jnp.concatenate([squared(block), squared(partner)])[None, :]
     piece = along_z(piece, owner // NC % NZ)
-    return exchange(repeat(piece)).reshape(half.shape)
+    piece, partner, squares = tie(piece, partner, squares)
+    return exchange(repeat(piece)).reshape(half.shape), partner, squares
+
+
+def squared(block):
+    wide = block[:, :D].astype(jnp.float32)
+    return jnp.sum(wide * wide, axis=1) * (LOG2E / (2.0 * D))
 
 
 def pack(v):
@@ -79,19 +95,7 @@
     return v[..., :-SCALE_ROWS, :].astype(jnp.float32) * scale
 
 
-def reduce_half(term, factor):
-    rows = term.shape[0] // NP
-    piece = jnp.sum(unpack(exchange(pack(term.reshape(NP, rows, D)))), axis=0)
-    piece = sum_z(piece)
-    mine = exchange(repeat(pack(piece)))
-    other = swap(mine)
-    first = lax.axis_index("c") == 0
-    mine = unpack(mine, factor).reshape(term.shape)
-    other = unpack(other, factor).reshape(term.shape)
-    return jnp.concatenate([jnp.where(first, mine, other), jnp.where(first, other, mine)], axis=0)
-
-
-def mix_kernel(own_ref, unit_ref, sq_ref, mix_ref, term_ref, col_ref, own_sq, row_sum, *, steps):
+def mix_kernel(own_ref, unit_ref, partner_ref, sq_ref, mix_ref, term_ref, col_ref, own_sq, row_sum, *, steps):
     j = pl.program_id(0)
     rows = own_ref.shape[0]
     spans = [slice(i, i + TILE_OWNER) for i in range(0, rows, TILE_OWNER)]
@@ -106,8 +110,9 @@
                 2.0 * math.sqrt(COLS)
             )
 
-    feat = unit_ref[:, :D]
-    swapped = jnp.concatenate([unit_ref[:, D + COLS :], unit_ref[:, D : D + COLS]], axis=1)
+    units = jnp.where(j < steps // 2, unit_ref[...], partner_ref[...])
+    feat = units[:, :D]
+    swapped = jnp.concatenate([units[:, D + COLS :], units[:, D : D + COLS]], axis=1)
     col = jnp.zeros(col_ref.shape, jnp.float32)
     contract_last = (((1,), (1,)), ((), ()))
     for span in spans:
@@ -131,15 +136,17 @@
             term_ref[span, :] -= total * own_ref[span, :D].astype(jnp.float32)
 
 
-def mix(own, units, unit_sq):
-    rows, count = own.shape[0], units.shape[0]
+def mix(own, units, partner, unit_sq):
+    rows, count = own.shape[0], units.shape[0] + partner.shape[0]
     steps = count // TILE_UNITS
+    half = steps // 2
     return pl.pallas_call(
         functools.partial(mix_kernel, steps=steps),
         grid=(steps,),
         in_specs=[
             pl.BlockSpec((rows, WIDE), lambda j: (0, 0)),
-            pl.BlockSpec((TILE_UNITS, WIDE), lambda j: (j, 0)),
+            pl.BlockSpec((TILE_UNITS, WIDE), lambda j: (jnp.minimum(j, half - 1), 0)),
+            pl.BlockSpec((TILE_UNITS, WIDE), lambda j: (jnp.maximum(j - half, 0), 0)),
             pl.BlockSpec((1, TILE_UNITS), lambda j: (0, j)),
         ],
         out_specs=[
@@ -148,7 +155,7 @@
             pl.BlockSpec((8, TILE_UNITS), lambda j: (0, j)),
         ],
         out_shape=[
-            jax.ShapeDtypeStruct((rows, count), jnp.bfloat16),
+            pltpu.HBM((rows, count), jnp.bfloat16),
             jax.ShapeDtypeStruct((rows, D), jnp.float32),
             jax.ShapeDtypeStruct((8, count), jnp.float32),
         ],
@@ -161,23 +168,68 @@
             bytes_accessed=2 * rows * count + 2 * WIDE * (rows + count) + 4 * rows * D,
             transcendentals=rows * count,
         ),
-    )(own, units, unit_sq)
+    )(own, units, partner, unit_sq)
+
+
+def local_kernel(mix_ref, own_ref, unit_ref, col_ref, *rest, scale):
+    contract_first = (((0,), (0,)), ((), ()))
+    out = lax.dot_general(mix_ref[...], own_ref[:, :D], contract_first, preferred_element_type=jnp.float32)
+    total = jnp.sum(col_ref[...].T, axis=1, keepdims=True)
+    out = out - total * unit_ref[:, :D].astype(jnp.float32)
+    if len(rest) == 2:
+        out = (out + rest[0][...]) * scale
+    rest[-1][...] = out
+
+
+def local_terms(mixed, own, units, col, first, received=None, scale=1.0):
+    rows, count = own.shape[0], units.shape[0]
+    base = first // TILE_UNITS
+    specs = [
+        pl.BlockSpec((rows, TILE_UNITS), lambda j: (0, j + base)),
+        pl.BlockSpec((rows, WIDE), lambda j: (0, 0)),
+        pl.BlockSpec((TILE_UNITS, WIDE), lambda j: (j, 0)),
+        pl.BlockSpec((8, TILE_UNITS), lambda j: (0, j + base)),
+    ]
+    args = [pltpu.with_memory_space_constraint(mixed, pltpu.HBM), own, units, col]
+    if received is not None:
+        specs.append(pl.BlockSpec((TILE_UNITS, D), lambda j: (j, 0)))
+        args.append(received)
+    return pl.pallas_call(
+        functools.partial(local_kernel, scale=scale),
+        grid=(count // TILE_UNITS,),
+        in_specs=specs,
+        out_specs=pl.BlockSpec((TILE_UNITS, D), lambda j: (j, 0)),
+        out_shape=jax.ShapeDtypeStruct((count, D), jnp.float32),
+        compiler_params=pltpu.CompilerParams(
+            vmem_limit_bytes=24 * 2**20, dimension_semantics=("arbitrary",)
+        ),
+        cost_estimate=pl.CostEstimate(
+            flops=2 * rows * count * D, bytes_accessed=2 * rows * count + 8 * count * D, transcendentals=0
+        ),
+    )(*args)
 
 
 def local(unit_data, owner):
     rows = unit_data.shape[0]
-    owner_half = broadcast_half(unit_data, owner[0])
-    both = jnp.concatenate([unit_data, swap(unit_data)], axis=0)
-    both_wide = both[:, :D].astype(jnp.float32)
-    unit_sq = jnp.sum(both_wide * both_wide, axis=1) * (LOG2E / (2.0 * D))
-    mixed_b, owner_term, col_parts = mix(owner_half, both, unit_sq[None, :])
-    owner_grad = reduce_half(owner_term, 1.0 / math.sqrt(rows * NP * NZ * NC))
-    contract_first = (((0,), (0,)), ((), ()))
-    local_term = (
-        lax.dot_general(mixed_b, owner_half[:, :D], contract_first, preferred_element_type=jnp.float32)
-        - jnp.sum(col_parts, axis=0)[:, None] * both_wide
-    )
-    local_grad = (local_term[:rows] + swap(local_term[rows:])) * (1.0 / math.sqrt(rows))
+    own, partner, squares = broadcast_half(unit_data, owner[0])
+    half_rows = own.shape[0]
+    piece_rows = half_rows // NP
+    mixed, term, col = mix(own, unit_data, partner, squares)
+    pieces = exchange(pack(term.reshape(NP, piece_rows, D)))
+    away = local_terms(mixed, own, partner, col, rows)
+    pieces, away = tie(pieces, away)
+    received = swap(away)
+    piece = sum_z(jnp.sum(unpack(pieces), axis=0))
+    piece, received = tie(piece, received)
+    mine = exchange(repeat(pack(piece)))
+    local_grad = local_terms(mixed, own, unit_data, col, 0, received, 1.0 / math.sqrt(rows))
+    mine, local_grad = tie(mine, local_grad)
+    other = swap(mine)
+    factor = 1.0 / math.sqrt(rows * NP * NZ * NC)
+    first = lax.axis_index("c") == 0
+    mine = unpack(mine, factor).reshape(half_rows, D)
+    other = unpack(other, factor).reshape(half_rows, D)
+    owner_grad = jnp.concatenate([jnp.where(first, mine, other), jnp.where(first, other, mine)], axis=0)
     return (owner_grad, local_grad)
 
 

time: 145 us -> 143 us (0.986)
  blocking collectives: 28.2 us -> 14.9 us
  waiting for transfers between devices: 31.8 us -> 40.1 us
  Pallas kernels: 10.6 us -> 18.6 us
  matrix products: 5.4 us -> 0 us
  other arithmetic: 10.2 us -> 7.11 us
  starting transfers between devices: 39.6 us -> 42.4 us
    all_to_all x2 -> x1, blocking collectives: 28.2 us -> 14.9 us  [exchange(): return lax.all_to_all(v, PLANE, 0, 0, tiled=True)]
    optimization_barrier x0 -> x2, local copies, waits for them, and re-layouts: none -> 9.18 us  [tie(): return lax.optimization_barrier(values)]
    ppermute x8, waiting for transfers between devices: 8.01 us -> 16.4 us  [shift(): return lax.ppermute(v, 'z', [(i, (i + k) % NZ) for i in range(NZ)])]
    pallas_call x0 -> x2, Pallas kernels: none -> 8.31 us  [local_terms(): pl.pallas_call(functools.partial(local_kernel, scale=scale), grid=(count...]
    unnamed x14 -> x11, local copies, waits for them, and re-layouts: 10 us -> 3.96 us
    dot_general x1 -> x0, matrix products: 5.4 us -> none  [local(): lax.dot_general(mixed_b, owner_half[:, :D], contract_first, preferred_ele...]
    all_to_all x2 -> x3, starting transfers between devices: 9.54 us -> 12.2 us  [exchange(): return lax.all_to_all(v, PLANE, 0, 0, tiled=True)]
    mul x2, other arithmetic: 1.85 us -> 0.01 us  [squared(): return jnp.sum(wide * wide, axis=1) * (LOG2E / (2.0 * D))]
  transfers between devices with their start and end apart: 14 -> 15, of which waited for: 8 -> 11; matrix products, arithmetic and copies ran while one was open for 10% -> 8% of each run, Pallas kernels for 0% -> 6%
where the time goes in v3:
time: 143 us; the launch traced here: 142 us
  starting transfers between devices  42.4 us (30%)
  waiting for transfers between devices  40.1 us (28%)
  Pallas kernels  18.6 us (13%)
  local copies, waits for them, and re-layouts  16.7 us (12%)
  blocking collectives  14.9 us (10%)
  other arithmetic  7.11 us (5%)
  between operations  2.29 us (2%)
    all_to_all x3, waiting for transfers between devices, exchange(): return lax.all_to_all(v, PLANE, 0, 0, tiled=True)  22.2 us
    ppermute x8, starting transfers between devices, shift(): return lax.ppermute(v, 'z', [(i, (i + k) % NZ) for i in range(NZ)])  17.1 us
    ppermute x8, waiting for transfers between devices, shift(): return lax.ppermute(v, 'z', [(i, (i + k) % NZ) for i in range(NZ)])  16.4 us
    all_to_all x1, blocking collectives, exchange(): return lax.all_to_all(v, PLANE, 0, 0, tiled=True)  14.9 us
    ppermute x4, starting transfers between devices, swap(): return lax.ppermute(v, 'c', [(0, 1), (1, 0)])  13.1 us
    all_to_all x3, starting transfers between devices, exchange(): return lax.all_to_all(v, PLANE, 0, 0, tiled=True)  12.2 us
    pallas_call x1, Pallas kernels, mix(): pl.pallas_call(functools.partial(mix_kernel, steps=steps), grid=(steps,),...  10.3 us
    optimization_barrier x2, local copies, waits for them, and re-layouts, tie(): return lax.optimization_barrier(values)  9.18 us
  transfers between devices with their start and end apart: 15, of which 11 were waited for; matrix products, arithmetic and copies ran while one was open for 8% of the time, Pallas kernels for 6%

profile of v3, /device:TPU:1, one launch (start us, length us, event | category | flops | bytes accessed | tf_op | source)
XLA Modules:
  0.0 142.2 jit_solution(17863922771913831250)
XLA Ops:
  0.6 2.4 %constant_dynamic-slice_fusion.1 = (bf16[1024,384]{1,0:T(8,128)(2,1)}, bf16[1024,384]{1,0:T(8,128)(2,1)S(1)}) fusion(bf16[2048,384]{1,0:T(8,128)(2,1)} %unit_ref.3, s32[]{:T(128)S(6)} %select_n.97, s32[]{:T(128)S(6)} %select_n.96), kind=kLoop, calls=%fused_computation.21 | loop fusion | bytes 3145736 | tf_op jit(solution)/shard_map/dynamic_slice | solution.py:40
  3.1 3.2 %collective-permute-start = (bf16[1024,384]{1,0:T(8,128)(2,1)}, bf16[1024,384]{1,0:T(8,128)(2,1)S(1)}, u32[]{:S(2)}, u32[]{:S(2)}) collective-permute-start(bf16[1024,384]{1,0:T(8,128)(2,1)} %get-tuple-element.34), channel_id=1, source_target_pairs={{0,1},{1,0},{2,3},{3,2},{4,5},{5,4},{6,7},{7,6},{8,9},{9,8},{10,11... | collective-permute-start | bytes 2359304 | tf_op jit(solution)/shard_map/ppermute | solution.py:27
  9.4 5.0 %all-to-all-start = ((bf16[16,64,384]{2,1,0:T(8,128)(2,1)}), bf16[16,64,384]{2,1,0:T(8,128)(2,1)S(1)}, u32[]{:S(2)}, u32[]{:S(2)}) async-start(bf16[16,64,384]{2,1,0:T(8,128)(2,1)} %bitcast.1), calls=%async_computation | async-start | bytes 1572864 | tf_op jit(solution)/shard_map/all_to_all | solution.py:35
  14.4 13.5 %all-to-all-done = bf16[16,64,384]{2,1,0:T(8,128)(2,1)S(1)} async-done(((bf16[16,64,384]{2,1,0:T(8,128)(2,1)}), bf16[16,64,384]{2,1,0:T(8,128)(2,1)S(1)}, u32[]{:S(2)}, u32[]{:S(2)}) %all-to-all-start) | async-done | bytes 786464 | tf_op jit(solution)/shard_map/all_to_all | solution.py:35
  27.9 1.9 %collective-permute-start.5 = (bf16[2048,384]{1,0:T(8,128)(2,1)S(1)}, bf16[2048,384]{1,0:T(8,128)(2,1)S(1)}, u32[]{:S(2)}, u32[]{:S(2)}) collective-permute-start(bf16[2048,384]{1,0:T(8,128)(2,1)S(1)} %copy-done), channel_id=1, source_target_pairs={{0,1},{1,0},{2,3},{3,2},{4,5},{5,4},{6,7},{7,6},{8,9},{9,8},{10,11... | collective-permute-start | bytes 4718600 | tf_op jit(solution)/shard_map/ppermute | solution.py:27
  29.8 6.9 %collective-permute-start.1 = (bf16[64,384]{1,0:T(8,128)(2,1)S(1)}, bf16[64,384]{1,0:T(8,128)(2,1)S(1)}, u32[]{:S(2)}, u32[]{:S(2)}) collective-permute-start(bf16[64,384]{1,0:T(8,128)(2,1)S(1)} %constant_dynamic-slice_fusion), channel_id=1, source_target_pairs={{0,8},{2,10},{4,12},{6,14},{8,0},{10,2},{12,4},{14,6},{1,9},{3,11}... | collective-permute-start | bytes 147464 | tf_op jit(solution)/shard_map/ppermute | solution.py:31
  39.7 2.8 %collective-permute-start.3 = (bf16[64,384]{1,0:T(8,128)(2,1)S(1)}, bf16[64,384]{1,0:T(8,128)(2,1)S(1)}, u32[]{:S(2)}, u32[]{:S(2)}) collective-permute-start(bf16[64,384]{1,0:T(8,128)(2,1)S(1)} %broadcast_select_fusion.1), channel_id=1, source_target_pairs={{0,14},{2,0},{4,2},{6,4},{8,6},{10,8},{12,10},{14,12},{1,15},{3,1}... | collective-permute-start | bytes 147464 | tf_op jit(solution)/shard_map/ppermute | solution.py:31
  42.5 1.8 %collective-permute-done.4 = bf16[64,384]{1,0:T(8,128)(2,1)S(1)} collective-permute-done((bf16[64,384]{1,0:T(8,128)(2,1)S(1)}, bf16[64,384]{1,0:T(8,128)(2,1)S(1)}, u32[]{:S(2)}, u32[]{:S(2)}) %collective-permute-start.4) | collective-permute-done | bytes 49184 | tf_op jit(solution)/shard_map/ppermute | solution.py:31
  44.4 3.0 %collective-permute-done.2 = bf16[64,384]{1,0:T(8,128)(2,1)S(1)} collective-permute-done((bf16[64,384]{1,0:T(8,128)(2,1)S(1)}, bf16[64,384]{1,0:T(8,128)(2,1)S(1)}, u32[]{:S(2)}, u32[]{:S(2)}) %collective-permute-start.2) | collective-permute-done | bytes 49184 | tf_op jit(solution)/shard_map/ppermute | solution.py:31
  49.0 14.9 %all_to_all.27 = bf16[16,64,384]{2,1,0:T(8,128)(2,1)S(1)} all-to-all(bf16[16,64,384]{2,1,0:T(8,128)(2,1)S(1)} %broadcast_in_dim.9), channel_id=1, replica_groups=mesh['y'=4,'x'=4,'z'=8,'c'=2] {'y','x'}, dimensions={0} | all-to-all | bytes 1572864 | tf_op jit(solution)/shard_map/all_to_all | solution.py:35
  63.9 10.3 %shard_map.41 = (bf16[1024,4096]{1,0:T(8,128)(2,1)}, f32[1024,256]{1,0:T(8,128)S(1)}, f32[8,4096]{1,0:T(8,128)S(1)}) custom-call(bf16[1024,384]{1,0:T(8,128)(2,1)S(1)} %bitcast.18, bf16[2048,384]{1,0:T(8,128)(2,1)S(1)} %copy-done, bf16[2048,384]{1,0:T(8,128)(2,1)S(1)} %copy-done.2, f32[1,4096]{1,0:T(1,128)S(1)} %bitcast.22), custom_call_target="tpu_custom_call" | custom-call | flops 5368709120 | bytes 13369344 | tf_op jit(solution)/shard_map/pallas_call | solution.py:143
  75.9 3.6 %all-to-all-start.2 = ((f16[16,80,256]{2,1,0:T(8,128)(2,1)}), f16[16,80,256]{2,1,0:T(8,128)(2,1)S(1)}, u32[]{:S(2)}, u32[]{:S(2)}) async-start(f16[16,80,256]{2,1,0:T(8,128)(2,1)} %pad_maximum_fusion.1), calls=%async_computation.2 | async-start | bytes 1310720 | tf_op jit(solution)/shard_map/all_to_all | solution.py:35
  80.9 3.5 %shard_map.42 = f32[2048,256]{1,0:T(8,128)S(1)} custom-call(bf16[1024,4096]{1,0:T(8,128)(2,1)} %get-tuple-element.26.mix_ref, bf16[1024,384]{1,0:T(8,128)(2,1)S(1)} %bitcast.19, bf16[2048,384]{1,0:T(8,128)(2,1)S(1)} %copy-done.3, f32[8,4096]{1,0:T(8,128)S(1)} %get-tuple-element.27.col_ref), custom_call_target="tpu_custom_call" | custom-call | flops 1073741824 | bytes 8388608 | tf_op jit(solution)/shard_map/pallas_call | solution.py:197
  85.7 3.6 %all-to-all-done.2 = f16[16,80,256]{2,1,0:T(8,128)(2,1)S(1)} async-done(((f16[16,80,256]{2,1,0:T(8,128)(2,1)}), f16[16,80,256]{2,1,0:T(8,128)(2,1)S(1)}, u32[]{:S(2)}, u32[]{:S(2)}) %all-to-all-start.2) | async-done | bytes 655392 | tf_op jit(solution)/shard_map/all_to_all | solution.py:35
  89.3 4.1 %collective-permute-start.10 = (f32[2048,256]{1,0:T(8,128)}, f32[2048,256]{1,0:T(8,128)}, u32[]{:S(2)}, u32[]{:S(2)}) collective-permute-start(f32[2048,256]{1,0:T(8,128)} %copy-done.4), channel_id=1, source_target_pairs={{0,1},{1,0},{2,3},{3,2},{4,5},{5,4},{6,7},{7,6},{8,9},{9,8},{10,11... | collective-permute-start | bytes 6291464 | tf_op jit(solution)/shard_map/ppermute | solution.py:27
  93.4 4.6 %copy.7 = f16[16,80,256]{0,2,1:T(8,128)(2,1)} copy(f16[16,80,256]{2,1,0:T(8,128)(2,1)S(1)} %all-to-all-done.2) | data formatting | bytes 1310720 | tf_op jit(solution)/shard_map/optimization_barrier | solution.py:61
  98.9 4.7 %collective-permute-start.6 = (f32[64,256]{1,0:T(8,128)S(1)}, f32[64,256]{1,0:T(8,128)S(1)}, u32[]{:S(2)}, u32[]{:S(2)}) collective-permute-start(f32[64,256]{1,0:T(8,128)S(1)} %multiply_reduce_fusion.2), channel_id=1, source_target_pairs={{0,8},{2,10},{4,12},{6,14},{8,0},{10,2},{12,4},{14,6},{1,9},{3,11}... | collective-permute-start | bytes 196616 | tf_op jit(solution)/shard_map/ppermute | solution.py:31
  103.7 4.4 %collective-permute-done.6 = f32[64,256]{1,0:T(8,128)S(1)} collective-permute-done((f32[64,256]{1,0:T(8,128)S(1)}, f32[64,256]{1,0:T(8,128)S(1)}, u32[]{:S(2)}, u32[]{:S(2)}) %collective-permute-start.6) | collective-permute-done | bytes 65568 | tf_op jit(solution)/shard_map/ppermute | solution.py:31
  112.7 2.6 %collective-permute-done.7 = f32[64,256]{1,0:T(8,128)S(1)} collective-permute-done((f32[64,256]{1,0:T(8,128)S(1)}, f32[64,256]{1,0:T(8,128)S(1)}, u32[]{:S(2)}, u32[]{:S(2)}) %collective-permute-start.7) | collective-permute-done | bytes 65568 | tf_op jit(solution)/shard_map/ppermute | solution.py:31
  117.6 3.6 %all-to-all-start.3 = ((f16[16,80,256]{2,1,0:T(8,128)(2,1)}), f16[16,80,256]{2,1,0:T(8,128)(2,1)S(1)}, u32[]{:S(2)}, u32[]{:S(2)}) async-start(f16[16,80,256]{2,1,0:T(8,128)(2,1)} %broadcast_in_dim.11), calls=%async_computation.3 | async-start | bytes 1310720 | tf_op jit(solution)/shard_map/all_to_all | solution.py:35
  121.2 4.8 %shard_map.43 = f32[2048,256]{1,0:T(8,128)} custom-call(bf16[1024,4096]{1,0:T(8,128)(2,1)} %get-tuple-element.26.mix_ref, bf16[1024,384]{1,0:T(8,128)(2,1)S(1)} %bitcast.20, bf16[2048,384]{1,0:T(8,128)(2,1)S(1)} %copy-done, f32[8,4096]{1,0:T(8,128)S(1)} %get-tuple-element.27.col_ref, f32[2048,256]{1,0:T(8,128)} %collective-permute-done.10.rest_0_), custom_call_target="tpu_custom_call" | custom-call | flops 1073741824 | bytes 8388608 | tf_op jit(solution)/shard_map/pallas_call | solution.py:197
  126.0 5.1 %all-to-all-done.3 = f16[16,80,256]{2,1,0:T(8,128)(2,1)S(1)} async-done(((f16[16,80,256]{2,1,0:T(8,128)(2,1)}), f16[16,80,256]{2,1,0:T(8,128)(2,1)S(1)}, u32[]{:S(2)}, u32[]{:S(2)}) %all-to-all-start.3) | async-done | bytes 655392 | tf_op jit(solution)/shard_map/all_to_all | solution.py:35
  131.2 3.9 %collective-permute-start.11 = (f16[16,80,256]{2,1,0:T(8,128)(2,1)S(1)}, f16[16,80,256]{2,1,0:T(8,128)(2,1)S(1)}, u32[]{:S(2)}, u32[]{:S(2)}) collective-permute-start(f16[16,80,256]{2,1,0:T(8,128)(2,1)S(1)} %all-to-all-done.3), channel_id=1, source_target_pairs={{0,1},{1,0},{2,3},{3,2},{4,5},{5,4},{6,7},{7,6},{8,9},{9,8},{10,11... | collective-permute-start | bytes 1966088 | tf_op jit(solution)/shard_map/ppermute | solution.py:27
  135.1 4.5 %copy.8 = f16[16,80,256]{0,2,1:T(8,128)(2,1)} copy(f16[16,80,256]{2,1,0:T(8,128)(2,1)S(1)} %all-to-all-done.3) | data formatting | bytes 1310720 | tf_op jit(solution)/shard_map/optimization_barrier | solution.py:61
  (54 shorter events, 21.0 us)
Async XLA Ops:
  3.0 24.9 %copy-start = (bf16[2048,384]{1,0:T(8,128)(2,1)S(1)}, bf16[2048,384]{1,0:T(8,128)(2,1)}, u32[]{:S(2)}) copy-start(bf16[2048,384]{1,0:T(8,128)(2,1)} %unit_ref.3) | copy-start | bytes 4718596
  3.1 5.4 %collective-permute-start = (bf16[1024,384]{1,0:T(8,128)(2,1)}, bf16[1024,384]{1,0:T(8,128)(2,1)S(1)}, u32[]{:S(2)}, u32[]{:S(2)}) collective-permute-start(bf16[1024,384]{1,0:T(8,128)(2,1)} %get-tuple-element.34), channel_id=1, source_target_pairs={{0,1},{1,0},{2,3},{3,2},{4,5},{5,4},{6,7},{7,6},{8,9},{9,8},{10,11... | collective-permute-start | bytes 2359304 | tf_op jit(solution)/shard_map/ppermute | solution.py:27
  9.4 18.5 %all-to-all-start = ((bf16[16,64,384]{2,1,0:T(8,128)(2,1)}), bf16[16,64,384]{2,1,0:T(8,128)(2,1)S(1)}, u32[]{:S(2)}, u32[]{:S(2)}) async-start(bf16[16,64,384]{2,1,0:T(8,128)(2,1)} %bitcast.1), calls=%async_computation | async-start | bytes 1572864 | tf_op jit(solution)/shard_map/all_to_all | solution.py:35
  27.9 19.4 %collective-permute-start.5 = (bf16[2048,384]{1,0:T(8,128)(2,1)S(1)}, bf16[2048,384]{1,0:T(8,128)(2,1)S(1)}, u32[]{:S(2)}, u32[]{:S(2)}) collective-permute-start(bf16[2048,384]{1,0:T(8,128)(2,1)S(1)} %copy-done), channel_id=1, source_target_pairs={{0,1},{1,0},{2,3},{3,2},{4,5},{5,4},{6,7},{7,6},{8,9},{9,8},{10,11... | collective-permute-start | bytes 4718600 | tf_op jit(solution)/shard_map/ppermute | solution.py:27
  29.8 8.9 %collective-permute-start.1 = (bf16[64,384]{1,0:T(8,128)(2,1)S(1)}, bf16[64,384]{1,0:T(8,128)(2,1)S(1)}, u32[]{:S(2)}, u32[]{:S(2)}) collective-permute-start(bf16[64,384]{1,0:T(8,128)(2,1)S(1)} %constant_dynamic-slice_fusion), channel_id=1, source_target_pairs={{0,8},{2,10},{4,12},{6,14},{8,0},{10,2},{12,4},{14,6},{1,9},{3,11}... | collective-permute-start | bytes 147464 | tf_op jit(solution)/shard_map/ppermute | solution.py:31
  38.8 5.6 %collective-permute-start.4 = (bf16[64,384]{1,0:T(8,128)(2,1)S(1)}, bf16[64,384]{1,0:T(8,128)(2,1)S(1)}, u32[]{:S(2)}, u32[]{:S(2)}) collective-permute-start(bf16[64,384]{1,0:T(8,128)(2,1)S(1)} %broadcast_select_fusion.1), channel_id=1, source_target_pairs={{0,4},{2,6},{4,8},{6,10},{8,12},{10,14},{12,0},{14,2},{1,5},{3,7},... | collective-permute-start | bytes 147464 | tf_op jit(solution)/shard_map/ppermute | solution.py:31
  39.7 4.6 %collective-permute-start.3 = (bf16[64,384]{1,0:T(8,128)(2,1)S(1)}, bf16[64,384]{1,0:T(8,128)(2,1)S(1)}, u32[]{:S(2)}, u32[]{:S(2)}) collective-permute-start(bf16[64,384]{1,0:T(8,128)(2,1)S(1)} %broadcast_select_fusion.1), channel_id=1, source_target_pairs={{0,14},{2,0},{4,2},{6,4},{8,6},{10,8},{12,10},{14,12},{1,15},{3,1}... | collective-permute-start | bytes 147464 | tf_op jit(solution)/shard_map/ppermute | solution.py:31
  42.5 4.8 %collective-permute-start.2 = (bf16[64,384]{1,0:T(8,128)(2,1)S(1)}, bf16[64,384]{1,0:T(8,128)(2,1)S(1)}, u32[]{:S(2)}, u32[]{:S(2)}) collective-permute-start(bf16[64,384]{1,0:T(8,128)(2,1)S(1)} %broadcast_select_fusion.1), channel_id=1, source_target_pairs={{0,2},{2,4},{4,6},{6,8},{8,10},{10,12},{12,14},{14,0},{1,3},{3,5},... | collective-permute-start | bytes 147464 | tf_op jit(solution)/shard_map/ppermute | solution.py:31
  47.7 1.1 copy-start.1
  48.9 15.0 %copy-start.2 = (bf16[2048,384]{1,0:T(8,128)(2,1)S(1)}, bf16[2048,384]{1,0:T(8,128)(2,1)}, u32[]{:S(2)}) copy-start(bf16[2048,384]{1,0:T(8,128)(2,1)} %copy-done.1) | copy-start | bytes 4718596
  75.9 13.4 %all-to-all-start.2 = ((f16[16,80,256]{2,1,0:T(8,128)(2,1)}), f16[16,80,256]{2,1,0:T(8,128)(2,1)S(1)}, u32[]{:S(2)}, u32[]{:S(2)}) async-start(f16[16,80,256]{2,1,0:T(8,128)(2,1)} %pad_maximum_fusion.1), calls=%async_computation.2 | async-start | bytes 1310720 | tf_op jit(solution)/shard_map/all_to_all | solution.py:35
  79.5 1.4 copy-start.3
  84.4 1.3 copy-start.4
  89.3 26.0 %collective-permute-start.10 = (f32[2048,256]{1,0:T(8,128)}, f32[2048,256]{1,0:T(8,128)}, u32[]{:S(2)}, u32[]{:S(2)}) collective-permute-start(f32[2048,256]{1,0:T(8,128)} %copy-done.4), channel_id=1, source_target_pairs={{0,1},{1,0},{2,3},{3,2},{4,5},{5,4},{6,7},{7,6},{8,9},{9,8},{10,11... | collective-permute-start | bytes 6291464 | tf_op jit(solution)/shard_map/ppermute | solution.py:27
  98.9 9.1 %collective-permute-start.6 = (f32[64,256]{1,0:T(8,128)S(1)}, f32[64,256]{1,0:T(8,128)S(1)}, u32[]{:S(2)}, u32[]{:S(2)}) collective-permute-start(f32[64,256]{1,0:T(8,128)S(1)} %multiply_reduce_fusion.2), channel_id=1, source_target_pairs={{0,8},{2,10},{4,12},{6,14},{8,0},{10,2},{12,4},{14,6},{1,9},{3,11}... | collective-permute-start | bytes 196616 | tf_op jit(solution)/shard_map/ppermute | solution.py:31
  108.1 3.4 %collective-permute-start.9 = (f32[64,256]{1,0:T(8,128)S(1)}, f32[64,256]{1,0:T(8,128)S(1)}, u32[]{:S(2)}, u32[]{:S(2)}) collective-permute-start(f32[64,256]{1,0:T(8,128)S(1)} %add.55), channel_id=1, source_target_pairs={{0,14},{2,0},{4,2},{6,4},{8,6},{10,8},{12,10},{14,12},{1,15},{3,1}... | collective-permute-start | bytes 196616 | tf_op jit(solution)/shard_map/ppermute | solution.py:31
  108.3 4.4 %collective-permute-start.8 = (f32[64,256]{1,0:T(8,128)S(1)}, f32[64,256]{1,0:T(8,128)S(1)}, u32[]{:S(2)}, u32[]{:S(2)}) collective-permute-start(f32[64,256]{1,0:T(8,128)S(1)} %add.55), channel_id=1, source_target_pairs={{0,2},{2,4},{4,6},{6,8},{8,10},{10,12},{12,14},{14,0},{1,3},{3,5},... | collective-permute-start | bytes 196616 | tf_op jit(solution)/shard_map/ppermute | solution.py:31
  109.8 5.5 %collective-permute-start.7 = (f32[64,256]{1,0:T(8,128)S(1)}, f32[64,256]{1,0:T(8,128)S(1)}, u32[]{:S(2)}, u32[]{:S(2)}) collective-permute-start(f32[64,256]{1,0:T(8,128)S(1)} %add.55), channel_id=1, source_target_pairs={{0,4},{2,6},{4,8},{6,10},{8,12},{10,14},{12,0},{14,2},{1,5},{3,7},... | collective-permute-start | bytes 196616 | tf_op jit(solution)/shard_map/ppermute | solution.py:31
  117.6 13.6 %all-to-all-start.3 = ((f16[16,80,256]{2,1,0:T(8,128)(2,1)}), f16[16,80,256]{2,1,0:T(8,128)(2,1)S(1)}, u32[]{:S(2)}, u32[]{:S(2)}) async-start(f16[16,80,256]{2,1,0:T(8,128)(2,1)} %broadcast_in_dim.11), calls=%async_computation.3 | async-start | bytes 1310720 | tf_op jit(solution)/shard_map/all_to_all | solution.py:35
  131.2 9.1 %collective-permute-start.11 = (f16[16,80,256]{2,1,0:T(8,128)(2,1)S(1)}, f16[16,80,256]{2,1,0:T(8,128)(2,1)S(1)}, u32[]{:S(2)}, u32[]{:S(2)}) collective-permute-start(f16[16,80,256]{2,1,0:T(8,128)(2,1)S(1)} %all-to-all-done.3), channel_id=1, source_target_pairs={{0,1},{1,0},{2,3},{3,2},{4,5},{5,4},{6,7},{7,6},{8,9},{9,8},{10,11... | collective-permute-start | bytes 1966088 | tf_op jit(solution)/shard_map/ppermute | solution.py:27

commit v4 on v3

v4 whole, which is shorter than its diff:
```python
import functools
import math

import jax
import jax.numpy as jnp
import numpy as np
from jax import lax
from jax.experimental import pallas as pl
from jax.experimental.pallas import tpu as pltpu
from jax.sharding import Mesh
from jax.sharding import PartitionSpec as P

D = 256
COLS = 64
WIDE = D + 2 * COLS
PLANE = ("y", "x", "v")
ALL = ("y", "x", "w", "v", "c")
NY, NX, NW, NV, NC = 4, 4, 4, 2, 2
NP = NY * NX * NV
TILE_UNITS = 1024
TILE_OWNER = 256
SCALE_ROWS = 8
SMALL = 4 * 2**20


def swap(v):
    return lax.ppermute(v, "c", [(0, 1), (1, 0)])


def shift(v, k):
    return lax.ppermute(v, "w", [(i, (i + k) % NW) for i in range(NW)])


def exchange(v):
    return lax.all_to_all(v, PLANE, 0, 0, tiled=True)


def pick(v, parts, index):
    rows = v.shape[0] // parts
    return lax.dynamic_slice_in_dim(v, index * rows, rows, 0)


def repeat(v):
    return jnp.broadcast_to(v[None], (NP, *v.shape))


def along_w(v, root):
    away = (lax.axis_index("w") - root) % NW
    up, down, two = shift(v, 1), shift(v, -1), shift(v, 2)
    return jnp.where(away == 0, v, jnp.where(away == 1, up, jnp.where(away == 3, down, two)))


def all_w(v):
    return v, shift(v, 2), shift(v, 1), shift(v, -1)


def in_hbm(v):
    return pltpu.with_memory_space_constraint(v, pltpu.HBM)


def tie(*values):
    return lax.optimization_barrier(values)


def split_kernel(block_ref, here_ref, there_ref, sems):
    rows = here_ref.shape[0]
    core = lax.axis_index("c")
    copies = [
        pltpu.make_async_copy(
            block_ref.at[pl.ds(pl.multiple_of(index * rows, rows), rows)], target, sems.at[slot]
        )
        for slot, (index, target) in enumerate(((1 - core, there_ref), (core, here_ref)))
    ]
    for copy in copies:
        copy.start()
    for copy in copies:
        copy.wait()


def split(block):
    half = jax.ShapeDtypeStruct((block.shape[0] // NC, block.shape[1]), block.dtype)
    return pl.pallas_call(
        split_kernel,
        in_specs=[pl.BlockSpec(memory_space=pl.ANY)],
        out_specs=[pl.BlockSpec(memory_space=pltpu.VMEM)] * 2,
        out_shape=[half, half],
        scratch_shapes=[pltpu.SemaphoreType.DMA((2,))],
        compiler_params=pltpu.CompilerParams(vmem_limit_bytes=SMALL),
    )(in_hbm(block))


def broadcast_half(block, owner):
    here, there = split(block)
    level = owner // NC % (NW * NV)
    place = owner // (NC * NW * NV) * NV + level % NV
    here, other, level, place = tie(here, swap(there), level, place)
    half = jnp.where(owner % NC == lax.axis_index("c"), here, other)
    piece = pick(exchange(half), NP, place)
    piece, block = tie(piece, block)
    partner = swap(block)
    squares = jnp.concatenate([squared(block), squared(partner)])[None, :]
    piece = along_w(piece, level // NV)
    piece, partner, squares = tie(piece, partner, squares)
    return exchange(repeat(piece)).reshape(half.shape), partner, squares


def squared(block):
    wide = block[:, :D].astype(jnp.float32)
    return jnp.sum(wide * wide, axis=1) * (0.5 / D)


def scaled(v):
    top = jnp.max(jnp.abs(v), axis=(0, 1), keepdims=True)
    power = jnp.floor(jnp.log2(jnp.maximum(top, 1e-30))) - 13.0
    return jnp.concatenate([v * jnp.exp(power * -math.log(2.0)), jnp.broadcast_to(power, (SCALE_ROWS, D))], axis=0)


def unpack(v, factor=1.0):
    groups = v.reshape(v.shape[0], -1, SCALE_ROWS, D).astype(jnp.float32)
    wide = groups[:, :-1] * (jnp.exp2(groups[:, -1:]) * factor)
    return wide.reshape(v.shape[0], -1, D)


def join_kernel(*refs):
    refs[-1][...] = scaled((refs[0][...] + refs[1][...]) + (refs[2][...] + refs[3][...]))


def join(*parts):
    rows = parts[0].shape[0]
    return pl.pallas_call(
        join_kernel,
        out_shape=jax.ShapeDtypeStruct((rows + SCALE_ROWS, D), jnp.float32),
        compiler_params=pltpu.CompilerParams(vmem_limit_bytes=SMALL),
    )(*parts)


def mix_kernel(own_ref, unit_ref, partner_ref, sq_ref, mix_ref, term_ref, col_ref, total, own_sq, row_sum, *, steps):
    j = pl.program_id(0)
    rows = own_ref.shape[0]
    spans = [slice(i, i + TILE_OWNER) for i in range(0, rows, TILE_OWNER)]

    @pl.when(j == 0)
    def _():
        total[...] = jnp.zeros_like(total)
        row_sum[...] = jnp.zeros_like(row_sum)
        for span in spans:
            feat = own_ref[span, :D].astype(jnp.float32)
            own_sq[span, :] = jnp.sum(feat * feat, axis=1, keepdims=True) * (0.5 / D) + math.log(2.0 * math.sqrt(COLS))

    units = jnp.where(j < steps // 2, unit_ref[...], partner_ref[...])
    feat = units[:, :D]
    swapped = jnp.concatenate([units[:, D + COLS :], units[:, D : D + COLS]], axis=1)
    col = jnp.zeros(col_ref.shape, jnp.float32)
    contract_last = (((1,), (1,)), ((), ()))
    for span in spans:
        cross = lax.dot_general(own_ref[span, :D], feat, contract_last, preferred_element_type=jnp.float32)
        weight = lax.dot_general(own_ref[span, D:], swapped, contract_last, preferred_element_type=jnp.float32)
        mixed = weight * jnp.exp(cross * (1.0 / D) - sq_ref[...] - own_sq[span, :])
        mixed_b = mixed.astype(jnp.bfloat16)
        mix_ref[span, :] = mixed_b
        total[span, :] += jnp.dot(mixed_b, feat, preferred_element_type=jnp.float32)
        col = col + jnp.sum(mixed.reshape(-1, *col.shape), axis=0)
        lanes = mixed[:, :128]
        for start in range(128, mixed.shape[1], 128):
            lanes = lanes + mixed[:, start : start + 128]
        row_sum[span, :] += lanes
    col_ref[...] = col

    @pl.when(j == steps - 1)
    def _():
        piece_rows = rows // NP
        for p in range(NP):
            span = slice(p * piece_rows, (p + 1) * piece_rows)
            row_total = jnp.sum(row_sum[span, :], axis=1, keepdims=True)
            term_ref[p] = scaled(total[span, :] - row_total * own_ref[span, :D].astype(jnp.float32))


def mix(own, units, partner, unit_sq):
    rows, count = own.shape[0], units.shape[0] + partner.shape[0]
    steps = count // TILE_UNITS
    half = steps // 2
    packed_rows = rows // NP + SCALE_ROWS
    return pl.pallas_call(
        functools.partial(mix_kernel, steps=steps),
        grid=(steps,),
        in_specs=[
            pl.BlockSpec((rows, WIDE), lambda j: (0, 0)),
            pl.BlockSpec((TILE_UNITS, WIDE), lambda j: (jnp.minimum(j, half - 1), 0)),
            pl.BlockSpec((TILE_UNITS, WIDE), lambda j: (jnp.maximum(j - half, 0), 0)),
            pl.BlockSpec((1, TILE_UNITS), lambda j: (0, j)),
        ],
        out_specs=[
            pl.BlockSpec((rows, TILE_UNITS), lambda j: (0, j)),
            pl.BlockSpec((NP, packed_rows, D), lambda j: (0, 0, 0)),
            pl.BlockSpec((8, TILE_UNITS), lambda j: (0, j)),
        ],
        out_shape=[
            pltpu.HBM((rows, count), jnp.bfloat16),
            jax.ShapeDtypeStruct((NP, packed_rows, D), jnp.float32),
            jax.ShapeDtypeStruct((8, count), jnp.float32),
        ],
        scratch_shapes=[pltpu.VMEM((rows, D), jnp.float32), pltpu.VMEM((rows, 1), jnp.float32), pltpu.VMEM((rows, 128), jnp.float32)],
        compiler_params=pltpu.CompilerParams(
            vmem_limit_bytes=24 * 2**20, dimension_semantics=("arbitrary",)
        ),
        cost_estimate=pl.CostEstimate(
            flops=2 * rows * count * (WIDE + D),
            bytes_accessed=2 * rows * count + 2 * WIDE * (rows + count) + 4 * rows * D,
            transcendentals=rows * count,
        ),
    )(own, in_hbm(units), partner, unit_sq)


def local_kernel(mix_ref, own_ref, unit_ref, col_ref, *rest, scale):
    contract_first = (((0,), (0,)), ((), ()))
    out = lax.dot_general(mix_ref[...], own_ref[:, :D], contract_first, preferred_element_type=jnp.float32)
    total = jnp.sum(col_ref[...].T, axis=1, keepdims=True)
    out = out - total * unit_ref[:, :D].astype(jnp.float32)
    if len(rest) == 2:
        out = (out + rest[0][...]) * scale
    rest[-1][...] = out


def local_terms(mixed, own, units, col, first, received=None, scale=1.0):
    rows, count = own.shape[0], units.shape[0]
    base = first // TILE_UNITS
    specs = [
        pl.BlockSpec((rows, TILE_UNITS), lambda j: (0, j + base)),
        pl.BlockSpec((rows, WIDE), lambda j: (0, 0)),
        pl.BlockSpec((TILE_UNITS, WIDE), lambda j: (j, 0)),
        pl.BlockSpec((8, TILE_UNITS), lambda j: (0, j + base)),
    ]
    args = [in_hbm(mixed), own, units, col]
    if received is not None:
        specs.append(pl.BlockSpec((TILE_UNITS, D), lambda j: (j, 0)))
        args.append(received)
    return pl.pallas_call(
        functools.partial(local_kernel, scale=scale),
        grid=(count // TILE_UNITS,),
        in_specs=specs,
        out_specs=pl.BlockSpec((TILE_UNITS, D), lambda j: (j, 0)),
        out_shape=pltpu.HBM((count, D), jnp.float32),
        compiler_params=pltpu.CompilerParams(
            vmem_limit_bytes=24 * 2**20, dimension_semantics=("arbitrary",)
        ),
        cost_estimate=pl.CostEstimate(
            flops=2 * rows * count * D, bytes_accessed=2 * rows * count + 8 * count * D, transcendentals=0
        ),
    )(*args)


def local(unit_data, owner):
    rows = unit_data.shape[0]
    own, partner, squares = broadcast_half(unit_data, owner[0])
    half_rows = own.shape[0]
    mixed, term, col = mix(own, unit_data, partner, squares)
    pieces = exchange(term.astype(jnp.float16))
    away = local_terms(mixed, own, partner, col, rows)
    pieces, away = tie(pieces, away)
    received = swap(away)
    piece = join(*all_w(jnp.sum(unpack(pieces), axis=0)))
    mine = exchange(repeat(piece.astype(jnp.float16)))
    local_grad = local_terms(mixed, own, in_hbm(unit_data), col, 0, received, 1.0 / math.sqrt(rows))
    mine, local_grad = tie(mine, local_grad)
    other = swap(mine)
    first = lax.axis_index("c") == 0
    packed = jnp.concatenate([jnp.where(first, mine, other), jnp.where(first, other, mine)], axis=0)
    owner_grad = unpack(packed, 1.0 / math.sqrt(rows * NP * NW * NC)).reshape(rows, D)
    return (owner_grad, local_grad)


def solution(mesh):
    grid = Mesh(np.asarray(mesh.devices).reshape(NY, NX, NW, NV, NC), ALL)
    in_specs = (P(ALL, None), P())
    out_specs = (P(), P(ALL, None))
    return jax.shard_map(local, mesh=grid, in_specs=in_specs, out_specs=out_specs, check_vma=False)
```

time: 143 us -> 128 us (0.90)
  local copies, waits for them, and re-layouts: 16.7 us -> 0.96 us
  waiting for transfers between devices: 40.1 us -> 35.7 us
  Pallas kernels: 18.6 us -> 22.4 us
  blocking collectives: 14.9 us -> 16.4 us
  other arithmetic: 7.11 us -> 8.55 us
    ppermute x8 -> x6, waiting for transfers between devices: 16.4 us -> 4.56 us  [shift(): return lax.ppermute(v, 'w', [(i, (i + k) % NW) for i in range(NW)])]
    optimization_barrier x2 -> x0, local copies, waits for them, and re-layouts: 9.18 us -> none  [tie(): return lax.optimization_barrier(values)]
    all_to_all x3, waiting for transfers between devices: 22.2 us -> 28 us  [exchange(): return lax.all_to_all(v, PLANE, 0, 0, tiled=True)]
    unnamed x11 -> x0, local copies, waits for them, and re-layouts: 3.96 us -> none
    all_to_all x3, starting transfers between devices: 12.2 us -> 15.9 us  [exchange(): return lax.all_to_all(v, PLANE, 0, 0, tiled=True)]
    concatenate x2 -> x0, other arithmetic: 2.45 us -> none  [the longest x1 1.46 us: local(): jnp.concatenate([jnp.where(first, mine, other), jnp.where(first, other, m...]
    dynamic_slice x2 -> x1, local copies, waits for them, and re-layouts: 2.42 us -> 0.01 us  [pick(): return lax.dynamic_slice_in_dim(v, index * rows, rows, 0)]
    convert_element_type x2 -> x4, other arithmetic: 0.18 us -> 2.33 us  [the longest x2 1.39 us: unpack(): groups = v.reshape(v.shape[0], -1, SCALE_ROWS, D).astype(jnp.float32)]
  transfers between devices with their start and end apart: 15 -> 13, of which waited for: 11 -> 8; matrix products, arithmetic and copies ran while one was open for 8% -> 3% of each run, Pallas kernels for 6% -> 7%
where the time goes in v4:
time: 128 us
  starting transfers between devices  42.2 us (33%)
  waiting for transfers between devices  35.7 us (28%)
  Pallas kernels  22.4 us (18%)
  blocking collectives  16.4 us (13%)
  other arithmetic  8.55 us (7%)
  between operations  1.53 us (1%)
    all_to_all x3, waiting for transfers between devices, exchange(): return lax.all_to_all(v, PLANE, 0, 0, tiled=True)  28 us
    all_to_all x1, blocking collectives, exchange(): return lax.all_to_all(v, PLANE, 0, 0, tiled=True)  16.4 us
    all_to_all x3, starting transfers between devices, exchange(): return lax.all_to_all(v, PLANE, 0, 0, tiled=True)  15.9 us
    ppermute x6, starting transfers between devices, shift(): return lax.ppermute(v, 'w', [(i, (i + k) % NW) for i in range(NW)])  15 us
    pallas_call x1, Pallas kernels, mix(): pl.pallas_call(functools.partial(mix_kernel, steps=steps), grid=(steps,),...  11.7 us
    ppermute x4, starting transfers between devices, swap(): return lax.ppermute(v, 'c', [(0, 1), (1, 0)])  11.3 us
    pallas_call x2, Pallas kernels, local_terms(): pl.pallas_call(functools.partial(local_kernel, scale=scale), grid=(count...  9.19 us
    ppermute x6, waiting for transfers between devices, shift(): return lax.ppermute(v, 'w', [(i, (i + k) % NW) for i in range(NW)])  4.56 us
  transfers between devices with their start and end apart: 13, of which 8 were waited for; matrix products, arithmetic and copies ran while one was open for 3% of the time, Pallas kernels for 7%

profile of v4, /device:TPU:1, one launch (start us, length us, event | category | flops | bytes accessed | tf_op | source)
XLA Modules:
  0.0 127.8 jit_solution(9887301965496693717)
XLA Ops:
  0.6 1.4 %shard_map.41 = (bf16[1024,384]{1,0:T(8,128)(2,1)S(1)}, bf16[1024,384]{1,0:T(8,128)(2,1)S(1)}) custom-call(bf16[2048,384]{1,0:T(8,128)(2,1)} %unit_ref.3), custom_call_target="tpu_custom_call" | custom-call | tf_op jit(solution)/shard_map/pallas_call | solution.py:82
  2.0 3.3 %collective-permute-start = (bf16[1024,384]{1,0:T(8,128)(2,1)S(1)}, bf16[1024,384]{1,0:T(8,128)(2,1)S(1)}, u32[]{:S(2)}, u32[]{:S(2)}) collective-permute-start(bf16[1024,384]{1,0:T(8,128)(2,1)S(1)} %get-tuple-element.21), channel_id=1, source_target_pairs={{0,1},{1,0},{2,3},{3,2},{4,5},{5,4},{6,7},{7,6},{8,9},{9,8},{10,11... | collective-permute-start | bytes 2359304 | tf_op jit(solution)/shard_map/ppermute | solution.py:27
  8.2 6.7 %all-to-all-start = ((bf16[32,32,384]{2,1,0:T(8,128)(2,1)}), bf16[32,32,384]{2,1,0:T(8,128)(2,1)S(1)}, u32[]{:S(2)}, u32[]{:S(2)}) async-start(bf16[32,32,384]{2,1,0:T(8,128)(2,1)} %bitcast.1), calls=%async_computation | async-start | bytes 1572864 | tf_op jit(solution)/shard_map/all_to_all | solution.py:35
  14.9 14.2 %all-to-all-done = bf16[32,32,384]{2,1,0:T(8,128)(2,1)S(1)} async-done(((bf16[32,32,384]{2,1,0:T(8,128)(2,1)}), bf16[32,32,384]{2,1,0:T(8,128)(2,1)S(1)}, u32[]{:S(2)}, u32[]{:S(2)}) %all-to-all-start) | async-done | bytes 786464 | tf_op jit(solution)/shard_map/all_to_all | solution.py:35
  29.1 1.8 %collective-permute-start.4 = (bf16[2048,384]{1,0:T(8,128)(2,1)}, bf16[2048,384]{1,0:T(8,128)(2,1)S(1)}, u32[]{:S(2)}, u32[]{:S(2)}) collective-permute-start(bf16[2048,384]{1,0:T(8,128)(2,1)} %unit_ref.3), channel_id=1, source_target_pairs={{0,1},{1,0},{2,3},{3,2},{4,5},{5,4},{6,7},{7,6},{8,9},{9,8},{10,11... | collective-permute-start | bytes 4718600 | tf_op jit(solution)/shard_map/ppermute | solution.py:27
  30.9 6.0 %collective-permute-start.3 = (bf16[32,384]{1,0:T(8,128)(2,1)S(1)}, bf16[32,384]{1,0:T(8,128)(2,1)S(1)}, u32[]{:S(2)}, u32[]{:S(2)}) collective-permute-start(bf16[32,384]{1,0:T(8,128)(2,1)S(1)} %constant_dynamic-slice_fusion), channel_id=1, source_target_pairs={{0,8},{4,12},{8,0},{12,4},{1,9},{5,13},{9,1},{13,5},{2,10},{6,14},... | collective-permute-start | bytes 73736 | tf_op jit(solution)/shard_map/ppermute | solution.py:31
  37.2 2.1 %collective-permute-start.1 = (bf16[32,384]{1,0:T(8,128)(2,1)S(1)}, bf16[32,384]{1,0:T(8,128)(2,1)S(1)}, u32[]{:S(2)}, u32[]{:S(2)}) collective-permute-start(bf16[32,384]{1,0:T(8,128)(2,1)S(1)} %constant_dynamic-slice_fusion), channel_id=1, source_target_pairs={{0,4},{4,8},{8,12},{12,0},{1,5},{5,9},{9,13},{13,1},{2,6},{6,10},{... | collective-permute-start | bytes 73736 | tf_op jit(solution)/shard_map/ppermute | solution.py:31
  39.3 1.6 %multiply_reduce_fusion.1 = f32[2048]{0:T(1024)S(1)} fusion(bf16[2048,384]{1,0:T(8,128)(2,1)} %unit_ref.3), kind=kLoop, calls=%fused_computation.2 | loop fusion | flops 1570816 | bytes 1056768 | tf_op jit(solution)/shard_map/reduce_sum | solution.py:109
  42.5 16.4 %all_to_all.27 = bf16[32,32,384]{2,1,0:T(8,128)(2,1)S(1)} all-to-all(bf16[32,32,384]{2,1,0:T(8,128)(2,1)S(1)} %broadcast_in_dim.7), channel_id=1, replica_groups=mesh['y'=4,'x'=4,'w'=4,'v'=2,'c'=2] {'y','x','v'}, dimensions={0} | all-to-all | bytes 1572864 | tf_op jit(solution)/shard_map/all_to_all | solution.py:35
  58.9 11.7 %shard_map.42 = (bf16[1024,4096]{1,0:T(8,128)(2,1)}, f32[32,40,256]{2,1,0:T(8,128)S(1)}, f32[8,4096]{1,0:T(8,128)S(1)}) custom-call(bf16[1024,384]{1,0:T(8,128)(2,1)S(1)} %bitcast.23, bf16[2048,384]{1,0:T(8,128)(2,1)} %unit_ref.3, bf16[2048,384]{1,0:T(8,128)(2,1)S(1)} %collective-permute-done.4.partner_ref.unit_ref, f32[1,4096]{1,0:T(1,128)S(1)} %bitcast.30), custom_call_target="tpu_custom_call" | custom-call | flops 5368709120 | bytes 13369344 | tf_op jit(solution)/shard_map/pallas_call | solution.py:183
  71.5 4.6 %all-to-all-start.2 = ((f16[32,40,256]{2,1,0:T(8,128)(2,1)}), f16[32,40,256]{2,1,0:T(8,128)(2,1)}, u32[]{:S(2)}, u32[]{:S(2)}) async-start(f16[32,40,256]{2,1,0:T(8,128)(2,1)} %convert_element_type.26), calls=%async_computation.2 | async-start | bytes 1310720 | tf_op jit(solution)/shard_map/all_to_all | solution.py:35
  76.1 4.4 %shard_map.43 = f32[2048,256]{1,0:T(8,128)} custom-call(bf16[1024,4096]{1,0:T(8,128)(2,1)} %get-tuple-element.32.mix_ref, bf16[1024,384]{1,0:T(8,128)(2,1)S(1)} %bitcast.24, bf16[2048,384]{1,0:T(8,128)(2,1)S(1)} %collective-permute-done.4.partner_ref.unit_ref, f32[8,4096]{1,0:T(8,128)S(1)} %get-tuple-element.33.col_ref), custom_call_target="tpu_custom_call" | custom-call | flops 1073741824 | bytes 8388608 | tf_op jit(solution)/shard_map/pallas_call | solution.py:237
  80.6 6.5 %all-to-all-done.2 = f16[32,40,256]{2,1,0:T(8,128)(2,1)} async-done(((f16[32,40,256]{2,1,0:T(8,128)(2,1)}), f16[32,40,256]{2,1,0:T(8,128)(2,1)}, u32[]{:S(2)}, u32[]{:S(2)}) %all-to-all-start.2) | async-done | bytes 655392 | tf_op jit(solution)/shard_map/all_to_all | solution.py:35
  87.1 3.7 %collective-permute-start.8 = (f32[2048,256]{1,0:T(8,128)}, f32[2048,256]{1,0:T(8,128)S(1)}, u32[]{:S(2)}, u32[]{:S(2)}) collective-permute-start(f32[2048,256]{1,0:T(8,128)} %shard_map.43), channel_id=1, source_target_pairs={{0,1},{1,0},{2,3},{3,2},{4,5},{5,4},{6,7},{7,6},{8,9},{9,8},{10,11... | collective-permute-start | bytes 6291464 | tf_op jit(solution)/shard_map/ppermute | solution.py:27
  92.1 3.4 %collective-permute-start.7 = (f32[32,256]{1,0:T(8,128)S(1)}, f32[32,256]{1,0:T(8,128)S(1)}, u32[]{:S(2)}, u32[]{:S(2)}) collective-permute-start(f32[32,256]{1,0:T(8,128)S(1)} %bitcast.26), channel_id=1, source_target_pairs={{0,12},{4,0},{8,4},{12,8},{1,13},{5,1},{9,5},{13,9},{2,14},{6,2},{... | collective-permute-start | bytes 98312 | tf_op jit(solution)/shard_map/ppermute | solution.py:31
  95.5 3.2 %collective-permute-start.5 = (f32[32,256]{1,0:T(8,128)S(1)}, f32[32,256]{1,0:T(8,128)S(1)}, u32[]{:S(2)}, u32[]{:S(2)}) collective-permute-start(f32[32,256]{1,0:T(8,128)S(1)} %bitcast.28), channel_id=1, source_target_pairs={{0,8},{4,12},{8,0},{12,4},{1,9},{5,13},{9,1},{13,5},{2,10},{6,14},... | collective-permute-start | bytes 98312 | tf_op jit(solution)/shard_map/ppermute | solution.py:31
  98.8 1.7 %collective-permute-done.6.refs_2_ = f32[32,256]{1,0:T(8,128)S(1)} collective-permute-done((f32[32,256]{1,0:T(8,128)S(1)}, f32[32,256]{1,0:T(8,128)S(1)}, u32[]{:S(2)}, u32[]{:S(2)}) %collective-permute-start.6) | collective-permute-done | bytes 32800 | tf_op jit(solution)/shard_map/ppermute | solution.py:31
  100.5 1.7 %collective-permute-done.5.refs_1_ = f32[32,256]{1,0:T(8,128)S(1)} collective-permute-done((f32[32,256]{1,0:T(8,128)S(1)}, f32[32,256]{1,0:T(8,128)S(1)}, u32[]{:S(2)}, u32[]{:S(2)}) %collective-permute-start.5) | collective-permute-done | bytes 32800 | tf_op jit(solution)/shard_map/ppermute | solution.py:31
  103.3 4.6 %all-to-all-start.3 = ((f16[32,40,256]{2,1,0:T(8,128)(2,1)}), f16[32,40,256]{2,1,0:T(8,128)(2,1)}, u32[]{:S(2)}, u32[]{:S(2)}) async-start(f16[32,40,256]{2,1,0:T(8,128)(2,1)} %broadcast_in_dim.8), calls=%async_computation.3 | async-start | bytes 1310720 | tf_op jit(solution)/shard_map/all_to_all | solution.py:35
  107.9 4.8 %shard_map.45 = f32[2048,256]{1,0:T(8,128)} custom-call(bf16[1024,4096]{1,0:T(8,128)(2,1)} %get-tuple-element.32.mix_ref, bf16[1024,384]{1,0:T(8,128)(2,1)S(1)} %bitcast.25, bf16[2048,384]{1,0:T(8,128)(2,1)} %unit_ref.3, f32[8,4096]{1,0:T(8,128)S(1)} %get-tuple-element.33.col_ref, f32[2048,256]{1,0:T(8,128)S(1)} %collective-permute-done.8.rest_0_), custom_call_target="tpu_custom_call" | custom-call | flops 1073741824 | bytes 8388608 | tf_op jit(solution)/shard_map/pallas_call | solution.py:237
  112.7 7.4 %all-to-all-done.3 = f16[32,40,256]{2,1,0:T(8,128)(2,1)} async-done(((f16[32,40,256]{2,1,0:T(8,128)(2,1)}), f16[32,40,256]{2,1,0:T(8,128)(2,1)}, u32[]{:S(2)}, u32[]{:S(2)}) %all-to-all-start.3) | async-done | bytes 655392 | tf_op jit(solution)/shard_map/all_to_all | solution.py:35
  120.0 2.5 %collective-permute-start.9 = (f16[32,40,256]{2,1,0:T(8,128)(2,1)}, f16[32,40,256]{2,1,0:T(8,128)(2,1)S(1)}, u32[]{:S(2)}, u32[]{:S(2)}) collective-permute-start(f16[32,40,256]{2,1,0:T(8,128)(2,1)} %all-to-all-done.3), channel_id=1, source_target_pairs={{0,1},{1,0},{2,3},{3,2},{4,5},{5,4},{6,7},{7,6},{8,9},{9,8},{10,11... | collective-permute-start | bytes 1966088 | tf_op jit(solution)/shard_map/ppermute | solution.py:27
  122.5 1.9 %collective-permute-done.9 = f16[32,40,256]{2,1,0:T(8,128)(2,1)S(1)} collective-permute-done((f16[32,40,256]{2,1,0:T(8,128)(2,1)}, f16[32,40,256]{2,1,0:T(8,128)(2,1)S(1)}, u32[]{:S(2)}, u32[]{:S(2)}) %collective-permute-start.9) | collective-permute-done | bytes 655392 | tf_op jit(solution)/shard_map/ppermute | solution.py:27
  126.2 1.7 %slice_multiply_fusion = f32[64,4,8,256]{3,2,1,0:T(8,128)} fusion(f32[64,5,8,256]{3,2,1,0:T(8,128)S(1)} %fusion, f32[64,8,256]{2,1,0:T(8,128)S(1)} %fusion.4), kind=kLoop, calls=%fused_computation | loop fusion | flops 524288 | bytes 4718592 | tf_op jit(solution)/shard_map/mul | solution.py:120
  (27 shorter events, 9.0 us)
Async XLA Ops:
  2.0 5.2 %collective-permute-start = (bf16[1024,384]{1,0:T(8,128)(2,1)S(1)}, bf16[1024,384]{1,0:T(8,128)(2,1)S(1)}, u32[]{:S(2)}, u32[]{:S(2)}) collective-permute-start(bf16[1024,384]{1,0:T(8,128)(2,1)S(1)} %get-tuple-element.21), channel_id=1, source_target_pairs={{0,1},{1,0},{2,3},{3,2},{4,5},{5,4},{6,7},{7,6},{8,9},{9,8},{10,11... | collective-permute-start | bytes 2359304 | tf_op jit(solution)/shard_map/ppermute | solution.py:27
  8.2 20.8 %all-to-all-start = ((bf16[32,32,384]{2,1,0:T(8,128)(2,1)}), bf16[32,32,384]{2,1,0:T(8,128)(2,1)S(1)}, u32[]{:S(2)}, u32[]{:S(2)}) async-start(bf16[32,32,384]{2,1,0:T(8,128)(2,1)} %bitcast.1), calls=%async_computation | async-start | bytes 1572864 | tf_op jit(solution)/shard_map/all_to_all | solution.py:35
  29.1 12.9 %collective-permute-start.4 = (bf16[2048,384]{1,0:T(8,128)(2,1)}, bf16[2048,384]{1,0:T(8,128)(2,1)S(1)}, u32[]{:S(2)}, u32[]{:S(2)}) collective-permute-start(bf16[2048,384]{1,0:T(8,128)(2,1)} %unit_ref.3), channel_id=1, source_target_pairs={{0,1},{1,0},{2,3},{3,2},{4,5},{5,4},{6,7},{7,6},{8,9},{9,8},{10,11... | collective-permute-start | bytes 4718600 | tf_op jit(solution)/shard_map/ppermute | solution.py:27
  30.9 10.0 %collective-permute-start.3 = (bf16[32,384]{1,0:T(8,128)(2,1)S(1)}, bf16[32,384]{1,0:T(8,128)(2,1)S(1)}, u32[]{:S(2)}, u32[]{:S(2)}) collective-permute-start(bf16[32,384]{1,0:T(8,128)(2,1)S(1)} %constant_dynamic-slice_fusion), channel_id=1, source_target_pairs={{0,8},{4,12},{8,0},{12,4},{1,9},{5,13},{9,1},{13,5},{2,10},{6,14},... | collective-permute-start | bytes 73736 | tf_op jit(solution)/shard_map/ppermute | solution.py:31
  36.9 4.0 %collective-permute-start.2 = (bf16[32,384]{1,0:T(8,128)(2,1)S(1)}, bf16[32,384]{1,0:T(8,128)(2,1)S(1)}, u32[]{:S(2)}, u32[]{:S(2)}) collective-permute-start(bf16[32,384]{1,0:T(8,128)(2,1)S(1)} %constant_dynamic-slice_fusion), channel_id=1, source_target_pairs={{0,12},{4,0},{8,4},{12,8},{1,13},{5,1},{9,5},{13,9},{2,14},{6,2},{... | collective-permute-start | bytes 73736 | tf_op jit(solution)/shard_map/ppermute | solution.py:31
  37.2 4.8 %collective-permute-start.1 = (bf16[32,384]{1,0:T(8,128)(2,1)S(1)}, bf16[32,384]{1,0:T(8,128)(2,1)S(1)}, u32[]{:S(2)}, u32[]{:S(2)}) collective-permute-start(bf16[32,384]{1,0:T(8,128)(2,1)S(1)} %constant_dynamic-slice_fusion), channel_id=1, source_target_pairs={{0,4},{4,8},{8,12},{12,0},{1,5},{5,9},{9,13},{13,1},{2,6},{6,10},{... | collective-permute-start | bytes 73736 | tf_op jit(solution)/shard_map/ppermute | solution.py:31
  71.5 15.6 %all-to-all-start.2 = ((f16[32,40,256]{2,1,0:T(8,128)(2,1)}), f16[32,40,256]{2,1,0:T(8,128)(2,1)}, u32[]{:S(2)}, u32[]{:S(2)}) async-start(f16[32,40,256]{2,1,0:T(8,128)(2,1)} %convert_element_type.26), calls=%async_computation.2 | async-start | bytes 1310720 | tf_op jit(solution)/shard_map/all_to_all | solution.py:35
  87.1 20.8 %collective-permute-start.8 = (f32[2048,256]{1,0:T(8,128)}, f32[2048,256]{1,0:T(8,128)S(1)}, u32[]{:S(2)}, u32[]{:S(2)}) collective-permute-start(f32[2048,256]{1,0:T(8,128)} %shard_map.43), channel_id=1, source_target_pairs={{0,1},{1,0},{2,3},{3,2},{4,5},{5,4},{6,7},{7,6},{8,9},{9,8},{10,11... | collective-permute-start | bytes 6291464 | tf_op jit(solution)/shard_map/ppermute | solution.py:27
  92.1 6.7 %collective-permute-start.7 = (f32[32,256]{1,0:T(8,128)S(1)}, f32[32,256]{1,0:T(8,128)S(1)}, u32[]{:S(2)}, u32[]{:S(2)}) collective-permute-start(f32[32,256]{1,0:T(8,128)S(1)} %bitcast.26), channel_id=1, source_target_pairs={{0,12},{4,0},{8,4},{12,8},{1,13},{5,1},{9,5},{13,9},{2,14},{6,2},{... | collective-permute-start | bytes 98312 | tf_op jit(solution)/shard_map/ppermute | solution.py:31
  95.5 5.0 %collective-permute-start.6 = (f32[32,256]{1,0:T(8,128)S(1)}, f32[32,256]{1,0:T(8,128)S(1)}, u32[]{:S(2)}, u32[]{:S(2)}) collective-permute-start(f32[32,256]{1,0:T(8,128)S(1)} %bitcast.27), channel_id=1, source_target_pairs={{0,4},{4,8},{8,12},{12,0},{1,5},{5,9},{9,13},{13,1},{2,6},{6,10},{... | collective-permute-start | bytes 98312 | tf_op jit(solution)/shard_map/ppermute | solution.py:31
  95.5 6.7 %collective-permute-start.5 = (f32[32,256]{1,0:T(8,128)S(1)}, f32[32,256]{1,0:T(8,128)S(1)}, u32[]{:S(2)}, u32[]{:S(2)}) collective-permute-start(f32[32,256]{1,0:T(8,128)S(1)} %bitcast.28), channel_id=1, source_target_pairs={{0,8},{4,12},{8,0},{12,4},{1,9},{5,13},{9,1},{13,5},{2,10},{6,14},... | collective-permute-start | bytes 98312 | tf_op jit(solution)/shard_map/ppermute | solution.py:31
  103.3 16.8 %all-to-all-start.3 = ((f16[32,40,256]{2,1,0:T(8,128)(2,1)}), f16[32,40,256]{2,1,0:T(8,128)(2,1)}, u32[]{:S(2)}, u32[]{:S(2)}) async-start(f16[32,40,256]{2,1,0:T(8,128)(2,1)} %broadcast_in_dim.8), calls=%async_computation.3 | async-start | bytes 1310720 | tf_op jit(solution)/shard_map/all_to_all | solution.py:35
  120.0 4.4 %collective-permute-start.9 = (f16[32,40,256]{2,1,0:T(8,128)(2,1)}, f16[32,40,256]{2,1,0:T(8,128)(2,1)S(1)}, u32[]{:S(2)}, u32[]{:S(2)}) collective-permute-start(f16[32,40,256]{2,1,0:T(8,128)(2,1)} %all-to-all-done.3), channel_id=1, source_target_pairs={{0,1},{1,0},{2,3},{3,2},{4,5},{5,4},{6,7},{7,6},{8,9},{9,8},{10,11... | collective-permute-start | bytes 1966088 | tf_op jit(solution)/shard_map/ppermute | solution.py:27

commit v5 on v4

v5 whole, which is shorter than its diff:
```python
import functools
import math

import jax
import jax.numpy as jnp
import numpy as np
from jax import lax
from jax.experimental import pallas as pl
from jax.experimental.pallas import tpu as pltpu
from jax.sharding import Mesh
from jax.sharding import PartitionSpec as P

D = 256
COLS = 64
WIDE = D + 2 * COLS
PLANE = ("y", "x", "v")
ALL = ("y", "x", "w", "v", "c")
NY, NX, NW, NV, NC = 4, 4, 4, 2, 2
NP = NY * NX * NV
TILE_OWNER = 256
SCALE_ROWS = 8
SMALL = 4 * 2**20


def swap(v):
    return lax.ppermute(v, "c", [(0, 1), (1, 0)])


def shift(v, k):
    return lax.ppermute(v, "w", [(i, (i + k) % NW) for i in range(NW)])


def exchange(v):
    return lax.all_to_all(v, PLANE, 0, 0, tiled=True)


def pick(v, parts, start):
    rows = v.shape[0] // parts
    return lax.dynamic_slice(v, (start, 0), (rows, v.shape[1]), allow_negative_indices=False)


def repeat(v):
    return jnp.broadcast_to(v[None], (NP, *v.shape))


def along_w(v, root):
    away = (lax.axis_index("w") - root) % NW
    up, down, two = shift(v, 1), shift(v, -1), shift(v, 2)
    return jnp.where(away == 0, v, jnp.where(away == 1, up, jnp.where(away == 3, down, two)))


def all_w(v):
    return v, shift(v, 2), shift(v, 1), shift(v, -1)


def in_hbm(v):
    return pltpu.with_memory_space_constraint(v, pltpu.HBM)


def tie(*values):
    return lax.optimization_barrier(values)


def split_kernel(block_ref, here_ref, there_ref, sems):
    rows = here_ref.shape[0]
    core = lax.axis_index("c")
    copies = [
        pltpu.make_async_copy(
            block_ref.at[pl.ds(pl.multiple_of(index * rows, rows), rows)], target, sems.at[slot]
        )
        for slot, (index, target) in enumerate(((1 - core, there_ref), (core, here_ref)))
    ]
    for copy in copies:
        copy.start()
    for copy in copies:
        copy.wait()


def split(block):
    half = jax.ShapeDtypeStruct((block.shape[0] // NC, block.shape[1]), block.dtype)
    return pl.pallas_call(
        split_kernel,
        in_specs=[pl.BlockSpec(memory_space=pl.ANY)],
        out_specs=[pl.BlockSpec(memory_space=pltpu.VMEM)] * 2,
        out_shape=[half, half],
        scratch_shapes=[pltpu.SemaphoreType.DMA((2,))],
        compiler_params=pltpu.CompilerParams(vmem_limit_bytes=SMALL),
    )(in_hbm(block))


def broadcast_half(block, owner):
    here, there = split(block)
    level = owner // NC % (NW * NV)
    start = (owner // (NC * NW * NV) * NV + level % NV) * (here.shape[0] // NP)
    here, other, level, start = tie(here, swap(there), level, start)
    half = jnp.where(owner % NC == lax.axis_index("c"), here, other)
    piece = pick(exchange(half), NP, start)
    parts = (here, there, other, swap(here))
    piece = along_w(piece, level // NV)
    squares = jnp.concatenate([squared(part) for part in parts])[None, :]
    piece, squares, *parts = tie(piece, squares, *parts)
    return exchange(repeat(piece)).reshape(half.shape), parts, squares


def squared(block):
    wide = block[:, :D].astype(jnp.float32)
    return jnp.sum(wide * wide, axis=1) * (0.5 / D)


def scaling(top):
    power = jnp.floor(jnp.log2(jnp.maximum(jnp.max(top, axis=(0, 1), keepdims=True), 1e-30))) - 13.0
    return power, jnp.exp(power * -math.log(2.0))


def sum_pieces(v):
    groups = v.reshape(v.shape[0], -1, SCALE_ROWS, D).astype(jnp.float32)
    powers = groups[:, -1]
    piece = jnp.sum(groups[:, :-1] * jnp.exp2(powers)[:, None], axis=0)
    return jnp.concatenate([piece, jnp.max(powers, axis=0)[None]], axis=0).reshape(-1, D)


def join_kernel(*refs):
    parts, piece_ref, power_ref = refs[:-2], refs[-2], refs[-1]
    rows = piece_ref.shape[0]
    piece = (parts[0][:rows] + parts[1][:rows]) + (parts[2][:rows] + parts[3][:rows])
    power = jnp.maximum(
        jnp.maximum(parts[0][rows:], parts[1][rows:]), jnp.maximum(parts[2][rows:], parts[3][rows:])
    ) + math.log2(NP * NW)
    factor = jnp.exp(power * -math.log(2.0))
    piece_ref[...] = (piece.reshape(-1, SCALE_ROWS, D) * factor[None]).reshape(rows, D)
    power_ref[...] = power


def join(*parts):
    rows = parts[0].shape[0] - SCALE_ROWS
    return pl.pallas_call(
        join_kernel,
        out_shape=[
            jax.ShapeDtypeStruct((rows, D), jnp.float32),
            jax.ShapeDtypeStruct((SCALE_ROWS, D), jnp.float32),
        ],
        compiler_params=pltpu.CompilerParams(vmem_limit_bytes=SMALL),
    )(*parts)


def unscale(v, power, factor):
    groups = v.reshape(-1, SCALE_ROWS, D).astype(jnp.float32) * (jnp.exp2(power) * factor)
    return groups.reshape(-1, D)


def choose(step, refs):
    picked = refs[-1][...]
    for index in range(len(refs) - 1):
        picked = jnp.where(step == index, refs[index][...], picked)
    return picked


def mix_kernel(own_ref, a_ref, b_ref, c_ref, d_ref, sq_ref, mix_ref, term_ref, col_ref, total, own_sq, row_sum, *, steps):
    j = pl.program_id(0)
    rows = own_ref.shape[0]
    spans = [slice(i, i + TILE_OWNER) for i in range(0, rows, TILE_OWNER)]

    @pl.when(j == 0)
    def _():
        total[...] = jnp.zeros_like(total)
        row_sum[...] = jnp.zeros_like(row_sum)
        for span in spans:
            feat = own_ref[span, :D].astype(jnp.float32)
            own_sq[span, :] = jnp.sum(feat * feat, axis=1, keepdims=True) * (0.5 / D) + math.log(2.0 * math.sqrt(COLS))

    units = choose(j, (a_ref, b_ref, c_ref, d_ref))
    feat = units[:, :D]
    swapped = jnp.concatenate([units[:, D + COLS :], units[:, D : D + COLS]], axis=1)
    col = jnp.zeros(col_ref.shape, jnp.float32)
    contract_last = (((1,), (1,)), ((), ()))
    for span in spans:
        cross = lax.dot_general(own_ref[span, :D], feat, contract_last, preferred_element_type=jnp.float32)
        weight = lax.dot_general(own_ref[span, D:], swapped, contract_last, preferred_element_type=jnp.float32)
        mixed = weight * jnp.exp(cross * (1.0 / D) - sq_ref[...] - own_sq[span, :])
        mixed_b = mixed.astype(jnp.bfloat16)
        mix_ref[span, :] = mixed_b
        total[span, :] += jnp.dot(mixed_b, feat, preferred_element_type=jnp.float32)
        col = col + jnp.sum(mixed.reshape(-1, *col.shape), axis=0)
        lanes = mixed[:, :128]
        for start in range(128, mixed.shape[1], 128):
            lanes = lanes + mixed[:, start : start + 128]
        row_sum[span, :] += lanes
    col_ref[...] = col

    @pl.when(j == steps - 1)
    def _():
        top = jnp.zeros((8, D), jnp.float32)
        for span in spans:
            row_total = jnp.sum(row_sum[span, :], axis=1, keepdims=True)
            part = total[span, :] - row_total * own_ref[span, :D].astype(jnp.float32)
            total[span, :] = part
            top = jnp.maximum(top, jnp.max(jnp.abs(part).reshape(-1, 8, D), axis=0))
        power, factor = scaling(top)
        piece_rows = rows // NP
        for p in range(NP):
            term_ref[p, :piece_rows] = total[p * piece_rows : (p + 1) * piece_rows, :] * factor
            term_ref[p, piece_rows:] = jnp.broadcast_to(power, (SCALE_ROWS, D))


def mix(own, parts, unit_sq):
    rows, tile = own.shape[0], parts[0].shape[0]
    steps = len(parts)
    count = steps * tile
    packed_rows = rows // NP + SCALE_ROWS
    return pl.pallas_call(
        functools.partial(mix_kernel, steps=steps),
        grid=(steps,),
        in_specs=[pl.BlockSpec(memory_space=pltpu.VMEM)] * (1 + steps) + [pl.BlockSpec((1, tile), lambda j: (0, j))],
        out_specs=[
            pl.BlockSpec((rows, tile), lambda j: (0, j)),
            pl.BlockSpec((NP, packed_rows, D), lambda j: (0, 0, 0)),
            pl.BlockSpec((8, tile), lambda j: (0, j)),
        ],
        out_shape=[
            pltpu.HBM((rows, count), jnp.bfloat16),
            jax.ShapeDtypeStruct((NP, packed_rows, D), jnp.float32),
            jax.ShapeDtypeStruct((8, count), jnp.float32),
        ],
        scratch_shapes=[pltpu.VMEM((rows, D), jnp.float32), pltpu.VMEM((rows, 1), jnp.float32), pltpu.VMEM((rows, 128), jnp.float32)],
        compiler_params=pltpu.CompilerParams(
            vmem_limit_bytes=24 * 2**20, dimension_semantics=("arbitrary",)
        ),
        cost_estimate=pl.CostEstimate(
            flops=2 * rows * count * (WIDE + D),
            bytes_accessed=2 * rows * count + 2 * WIDE * (rows + count) + 4 * rows * D,
            transcendentals=rows * count,
        ),
    )(own, *parts, unit_sq)


def local_kernel(core_ref, mix_ref, own_ref, a_ref, b_ref, col_ref, *rest, scale):
    contract_first = (((0,), (0,)), ((), ()))
    out = lax.dot_general(mix_ref[...], own_ref[:, :D], contract_first, preferred_element_type=jnp.float32)
    total = jnp.sum(col_ref[...].T, axis=1, keepdims=True)
    units = choose(pl.program_id(0), (a_ref, b_ref))
    out = out - total * units[:, :D].astype(jnp.float32)
    if len(rest) == 2:
        out = (out + rest[0][...]) * scale
    rest[-1][...] = out


def local_terms(core, mixed, own, parts, col, first, received=None, scale=1.0):
    rows, tile = own.shape[0], parts[0].shape[0]
    count = len(parts) * tile
    whole = pl.BlockSpec(memory_space=pltpu.VMEM)
    ordered = pl.BlockSpec((tile, D), lambda j, core: (jnp.where(j == 0, core[0], 1 - core[0]), 0))
    more = [] if received is None else [received]
    return pl.pallas_call(
        functools.partial(local_kernel, scale=scale),
        grid_spec=pltpu.PrefetchScalarGridSpec(
            num_scalar_prefetch=1,
            grid=(len(parts),),
            in_specs=[
                pl.BlockSpec((rows, tile), lambda j, core: (0, j + first)),
                whole,
                whole,
                whole,
                pl.BlockSpec((8, tile), lambda j, core: (0, j + first)),
            ]
            + [ordered] * len(more),
            out_specs=ordered,
        ),
        out_shape=pltpu.HBM((count, D), jnp.float32),
        compiler_params=pltpu.CompilerParams(
            vmem_limit_bytes=24 * 2**20, dimension_semantics=("arbitrary",)
        ),
        cost_estimate=pl.CostEstimate(
            flops=2 * rows * count * D, bytes_accessed=2 * rows * count + 8 * count * D, transcendentals=0
        ),
    )(core, in_hbm(mixed), own, *parts, col, *more)


def place_kernel(mine_ref, other_ref, out_ref, sems):
    rows = mine_ref.shape[0]
    core = lax.axis_index("c")
    copies = [
        pltpu.make_async_copy(source, out_ref.at[pl.ds(pl.multiple_of(index * rows, rows), rows)], sems.at[slot])
        for slot, (index, source) in enumerate(((core, mine_ref), (1 - core, other_ref)))
    ]
    for copy in copies:
        copy.start()
    for copy in copies:
        copy.wait()


def place(mine, other):
    return pl.pallas_call(
        place_kernel,
        in_specs=[pl.BlockSpec(memory_space=pltpu.VMEM)] * 2,
        out_specs=pl.BlockSpec(memory_space=pl.ANY),
        out_shape=jax.ShapeDtypeStruct((NC * mine.shape[0], mine.shape[1]), mine.dtype),
        scratch_shapes=[pltpu.SemaphoreType.DMA((2,))],
        compiler_params=pltpu.CompilerParams(vmem_limit_bytes=SMALL),
    )(mine, other)


def local(unit_data, owner):
    rows = unit_data.shape[0]
    core = lax.axis_index("c").astype(jnp.int32).reshape(1)
    own, parts, squares = broadcast_half(unit_data, owner[0])
    mixed, term, col = mix(own, parts, squares)
    pieces = exchange(term.astype(jnp.float16))
    away = local_terms(core, mixed, own, parts[2:], col, 2)
    pieces, away = tie(pieces, away)
    received = swap(away)
    piece, power = join(*all_w(sum_pieces(pieces)))
    power_other = swap(power)
    mine = exchange(repeat(piece.astype(jnp.float16)))
    local_grad = local_terms(core, mixed, own, parts[:2], col, 0, received, 1.0 / math.sqrt(rows))
    mine, local_grad = tie(mine, local_grad)
    other = swap(mine)
    factor = 1.0 / math.sqrt(rows * NP * NW * NC)
    owner_grad = place(unscale(mine, power, factor), unscale(other, power_other, factor))
    return (owner_grad, local_grad)


def solution(mesh):
    grid = Mesh(np.asarray(mesh.devices).reshape(NY, NX, NW, NV, NC), ALL)
    in_specs = (P(ALL, None), P())
    out_specs = (P(), P(ALL, None))
    return jax.shard_map(local, mesh=grid, in_specs=in_specs, out_specs=out_specs, check_vma=False)
```

time: 128 us -> 123 us (0.961)
  waiting for transfers between devices: 35.7 us -> 28.1 us
  starting transfers between devices: 42.2 us -> 46 us
  other arithmetic: 8.55 us -> 5.11 us
  local copies, waits for them, and re-layouts: 0.96 us -> 3.77 us
  blocking collectives: 16.4 us -> 14.9 us
    all_to_all x3, waiting for transfers between devices: 28 us -> 20 us  [exchange(): return lax.all_to_all(v, PLANE, 0, 0, tiled=True)]
    ppermute x6, starting transfers between devices: 15 us -> 17.7 us  [shift(): return lax.ppermute(v, 'w', [(i, (i + k) % NW) for i in range(NW)])]
    unnamed x0 -> x6, local copies, waits for them, and re-layouts: none -> 2.01 us
    all_to_all x1, blocking collectives: 16.4 us -> 14.9 us  [exchange(): return lax.all_to_all(v, PLANE, 0, 0, tiled=True)]
    mul x3 -> x5, other arithmetic: 1.8 us -> 0.29 us  [the longest x2 0.22 us: unscale(): v.reshape(-1, SCALE_ROWS, D).astype(jnp.float32)]
    select_n x1 -> x0, other arithmetic: 1.39 us -> none  [local(): jnp.where(first, mine, other)]
    pallas_call x3 -> x4, Pallas kernels: 9.33 us -> 10.7 us  [the longest x2 9.34 us: local_terms(): pl.pallas_call(functools.partial(local_kernel, scale=scale), grid_spec=pl...]
    ppermute x4 -> x5, waiting for transfers between devices: 3.13 us -> 4.11 us  [swap(): return lax.ppermute(v, 'c', [(0, 1), (1, 0)])]
  transfers between devices with their start and end apart: 13 -> 14, of which waited for: 8 -> 8; matrix products, arithmetic and copies ran while one was open for 3% -> 3% of each run, Pallas kernels for 7% -> 8%
where the time goes in v5:
time: 123 us; the launch traced here: 122 us
  starting transfers between devices  46 us (37%)
  waiting for transfers between devices  28.1 us (23%)
  Pallas kernels  22.7 us (18%)
  blocking collectives  14.9 us (12%)
  other arithmetic  5.11 us (4%)
  local copies, waits for them, and re-layouts  3.77 us (3%)
  between operations  1.7 us (1%)
    all_to_all x3, waiting for transfers between devices, exchange(): return lax.all_to_all(v, PLANE, 0, 0, tiled=True)  20 us
    ppermute x6, starting transfers between devices, shift(): return lax.ppermute(v, 'w', [(i, (i + k) % NW) for i in range(NW)])  17.7 us
    all_to_all x3, starting transfers between devices, exchange(): return lax.all_to_all(v, PLANE, 0, 0, tiled=True)  16.7 us
    all_to_all x1, blocking collectives, exchange(): return lax.all_to_all(v, PLANE, 0, 0, tiled=True)  14.9 us
    ppermute x5, starting transfers between devices, swap(): return lax.ppermute(v, 'c', [(0, 1), (1, 0)])  11.6 us
    pallas_call x1, Pallas kernels, mix(): pl.pallas_call(functools.partial(mix_kernel, steps=steps), grid=(steps,),...  10.6 us
    pallas_call x2, Pallas kernels, local_terms(): pl.pallas_call(functools.partial(local_kernel, scale=scale), grid_spec=pl...  9.34 us
    ppermute x5, waiting for transfers between devices, swap(): return lax.ppermute(v, 'c', [(0, 1), (1, 0)])  4.11 us
  transfers between devices with their start and end apart: 14, of which 8 were waited for; matrix products, arithmetic and copies ran while one was open for 3% of the time, Pallas kernels for 8%

profile of v5, /device:TPU:1, one launch (start us, length us, event | category | flops | bytes accessed | tf_op | source)
XLA Modules:
  0.0 122.2 jit_solution(6386517230336467799)
XLA Ops:
  0.6 1.4 %shard_map.41 = (bf16[1024,384]{1,0:T(8,128)(2,1)S(1)}, bf16[1024,384]{1,0:T(8,128)(2,1)S(1)}) custom-call(bf16[2048,384]{1,0:T(8,128)(2,1)} %block_ref.1), custom_call_target="tpu_custom_call" | custom-call | tf_op jit(solution)/shard_map/pallas_call | solution.py:81
  2.0 3.3 %collective-permute-start = (bf16[1024,384]{1,0:T(8,128)(2,1)S(1)}, bf16[1024,384]{1,0:T(8,128)(2,1)S(1)}, u32[]{:S(2)}, u32[]{:S(2)}) collective-permute-start(bf16[1024,384]{1,0:T(8,128)(2,1)S(1)} %get-tuple-element.31.b_ref), channel_id=1, source_target_pairs={{0,1},{1,0},{2,3},{3,2},{4,5},{5,4},{6,7},{7,6},{8,9},{9,8},{10,11... | collective-permute-start | bytes 2359304 | tf_op jit(solution)/shard_map/ppermute | solution.py:26
  8.2 6.8 %all-to-all-start = ((bf16[32,32,384]{2,1,0:T(8,128)(2,1)}), bf16[32,32,384]{2,1,0:T(8,128)(2,1)}, u32[]{:S(2)}, u32[]{:S(2)}) async-start(bf16[32,32,384]{2,1,0:T(8,128)(2,1)} %bitcast.1), calls=%async_computation | async-start | bytes 1572864 | tf_op jit(solution)/shard_map/all_to_all | solution.py:34
  16.4 1.5 %collective-permute-done.4.d_ref.b_ref = bf16[1024,384]{1,0:T(8,128)(2,1)S(1)} collective-permute-done((bf16[1024,384]{1,0:T(8,128)(2,1)S(1)}, bf16[1024,384]{1,0:T(8,128)(2,1)S(1)}, u32[]{:S(2)}, u32[]{:S(2)}) %collective-permute-start.4) | collective-permute-done | bytes 786464 | tf_op jit(solution)/shard_map/ppermute | solution.py:26
  19.0 10.2 %all-to-all-done = bf16[32,32,384]{2,1,0:T(8,128)(2,1)} async-done(((bf16[32,32,384]{2,1,0:T(8,128)(2,1)}), bf16[32,32,384]{2,1,0:T(8,128)(2,1)}, u32[]{:S(2)}, u32[]{:S(2)}) %all-to-all-start) | async-done | bytes 786464 | tf_op jit(solution)/shard_map/all_to_all | solution.py:34
  30.0 3.1 %collective-permute-start.1 = (bf16[32,384]{1,0:T(8,128)(2,1)S(1)}, bf16[32,384]{1,0:T(8,128)(2,1)S(1)}, u32[]{:S(2)}, u32[]{:S(2)}) collective-permute-start(bf16[32,384]{1,0:T(8,128)(2,1)S(1)} %constant_dynamic-slice_fusion), channel_id=1, source_target_pairs={{0,4},{4,8},{8,12},{12,0},{1,5},{5,9},{9,13},{13,1},{2,6},{6,10},{... | collective-permute-start | bytes 73736 | tf_op jit(solution)/shard_map/ppermute | solution.py:30
  33.1 2.2 %collective-permute-start.2 = (bf16[32,384]{1,0:T(8,128)(2,1)S(1)}, bf16[32,384]{1,0:T(8,128)(2,1)S(1)}, u32[]{:S(2)}, u32[]{:S(2)}) collective-permute-start(bf16[32,384]{1,0:T(8,128)(2,1)S(1)} %constant_dynamic-slice_fusion), channel_id=1, source_target_pairs={{0,12},{4,0},{8,4},{12,8},{1,13},{5,1},{9,5},{13,9},{2,14},{6,2},{... | collective-permute-start | bytes 73736 | tf_op jit(solution)/shard_map/ppermute | solution.py:30
  35.3 4.4 %collective-permute-start.3 = (bf16[32,384]{1,0:T(8,128)(2,1)S(1)}, bf16[32,384]{1,0:T(8,128)(2,1)S(1)}, u32[]{:S(2)}, u32[]{:S(2)}) collective-permute-start(bf16[32,384]{1,0:T(8,128)(2,1)S(1)} %constant_dynamic-slice_fusion), channel_id=1, source_target_pairs={{0,8},{4,12},{8,0},{12,4},{1,9},{5,13},{9,1},{13,5},{2,10},{6,14},... | collective-permute-start | bytes 73736 | tf_op jit(solution)/shard_map/ppermute | solution.py:30
  39.7 2.5 %collective-permute-done.3 = bf16[32,384]{1,0:T(8,128)(2,1)S(1)} collective-permute-done((bf16[32,384]{1,0:T(8,128)(2,1)S(1)}, bf16[32,384]{1,0:T(8,128)(2,1)S(1)}, u32[]{:S(2)}, u32[]{:S(2)}) %collective-permute-start.3) | collective-permute-done | bytes 24608 | tf_op jit(solution)/shard_map/ppermute | solution.py:30
  43.0 14.9 %all_to_all.27 = bf16[32,32,384]{2,1,0:T(8,128)(2,1)S(1)} all-to-all(bf16[32,32,384]{2,1,0:T(8,128)(2,1)S(1)} %broadcast_in_dim.9), channel_id=1, replica_groups=mesh['y'=4,'x'=4,'w'=4,'v'=2,'c'=2] {'y','x','v'}, dimensions={0} | all-to-all | bytes 1572864 | tf_op jit(solution)/shard_map/all_to_all | solution.py:34
  57.9 10.6 %shard_map.42 = (bf16[1024,4096]{1,0:T(8,128)(2,1)}, f32[32,40,256]{2,1,0:T(8,128)S(1)}, f32[8,4096]{1,0:T(8,128)S(1)}) custom-call(bf16[1024,384]{1,0:T(8,128)(2,1)S(1)} %bitcast.28, bf16[1024,384]{1,0:T(8,128)(2,1)S(1)} %get-tuple-element.30.a_ref, bf16[1024,384]{1,0:T(8,128)(2,1)S(1)} %get-tuple-element.31.b_ref, ...), custom_call_target="tpu_custom_call" | custom-call | flops 5368709120 | bytes 13369344 | tf_op jit(solution)/shard_map/pallas_call | solution.py:210
  69.4 5.8 %all-to-all-start.2 = ((f16[32,40,256]{2,1,0:T(8,128)(2,1)}), f16[32,40,256]{2,1,0:T(8,128)(2,1)}, u32[]{:S(2)}, u32[]{:S(2)}) async-start(f16[32,40,256]{2,1,0:T(8,128)(2,1)} %convert_element_type.42), calls=%async_computation.2 | async-start | bytes 1310720 | tf_op jit(solution)/shard_map/all_to_all | solution.py:34
  76.4 4.5 %shard_map.43 = f32[2048,256]{1,0:T(8,128)} custom-call(s32[1]{0:T(128)} %bitcast.5.core_ref, bf16[1024,4096]{1,0:T(8,128)(2,1)} %get-tuple-element.36.mix_ref, bf16[1024,384]{1,0:T(8,128)(2,1)S(1)} %bitcast.29, bf16[1024,384]{1,0:T(8,128)(2,1)S(1)} %collective-permute-done.c_ref.a_ref, bf16[1024,384]{1,0:T(8,128)(2,1)S(1)} %copy-done.2, ...), custom_call_target="tpu_custom_call" | custom-call | flops 1073741824 | bytes 8388608 | tf_op jit(solution)/shard_map/pallas_call | solution.py:253
  80.9 5.1 %all-to-all-done.2 = f16[32,40,256]{2,1,0:T(8,128)(2,1)} async-done(((f16[32,40,256]{2,1,0:T(8,128)(2,1)}), f16[32,40,256]{2,1,0:T(8,128)(2,1)}, u32[]{:S(2)}, u32[]{:S(2)}) %all-to-all-start.2) | async-done | bytes 655392 | tf_op jit(solution)/shard_map/all_to_all | solution.py:34
  86.0 3.9 %collective-permute-start.8 = (f32[2048,256]{1,0:T(8,128)}, f32[2048,256]{1,0:T(8,128)}, u32[]{:S(2)}, u32[]{:S(2)}) collective-permute-start(f32[2048,256]{1,0:T(8,128)} %shard_map.43), channel_id=1, source_target_pairs={{0,1},{1,0},{2,3},{3,2},{4,5},{5,4},{6,7},{7,6},{8,9},{9,8},{10,11... | collective-permute-start | bytes 6291464 | tf_op jit(solution)/shard_map/ppermute | solution.py:26
  91.3 4.4 %collective-permute-start.5 = (f32[40,256]{1,0:T(8,128)S(1)}, f32[40,256]{1,0:T(8,128)S(1)}, u32[]{:S(2)}, u32[]{:S(2)}) collective-permute-start(f32[40,256]{1,0:T(8,128)S(1)} %maximum_bitcast_fusion.refs_0_), channel_id=1, source_target_pairs={{0,8},{4,12},{8,0},{12,4},{1,9},{5,13},{9,1},{13,5},{2,10},{6,14},... | collective-permute-start | bytes 122888 | tf_op jit(solution)/shard_map/ppermute | solution.py:30
  96.0 3.3 %collective-permute-start.7 = (f32[40,256]{1,0:T(8,128)S(1)}, f32[40,256]{1,0:T(8,128)S(1)}, u32[]{:S(2)}, u32[]{:S(2)}) collective-permute-start(f32[40,256]{1,0:T(8,128)S(1)} %maximum_bitcast_fusion.refs_0_), channel_id=1, source_target_pairs={{0,12},{4,0},{8,4},{12,8},{1,13},{5,1},{9,5},{13,9},{2,14},{6,2},{... | collective-permute-start | bytes 122888 | tf_op jit(solution)/shard_map/ppermute | solution.py:30
  99.3 1.5 %collective-permute-done.6.refs_2_ = f32[40,256]{1,0:T(8,128)S(1)} collective-permute-done((f32[40,256]{1,0:T(8,128)S(1)}, f32[40,256]{1,0:T(8,128)S(1)}, u32[]{:S(2)}, u32[]{:S(2)}) %collective-permute-start.6) | collective-permute-done | bytes 40992 | tf_op jit(solution)/shard_map/ppermute | solution.py:30
  101.7 4.1 %all-to-all-start.3 = ((f16[32,32,256]{2,1,0:T(8,128)(2,1)}), f16[32,32,256]{2,1,0:T(8,128)(2,1)S(1)}, u32[]{:S(2)}, u32[]{:S(2)}) async-start(f16[32,32,256]{2,1,0:T(8,128)(2,1)} %broadcast_in_dim.11), calls=%async_computation.3 | async-start | bytes 1048576 | tf_op jit(solution)/shard_map/all_to_all | solution.py:34
  105.8 1.4 %collective-permute-start.10 = (f32[8,256]{1,0:T(8,128)S(1)}, f32[8,256]{1,0:T(8,128)S(1)}, u32[]{:S(2)}, u32[]{:S(2)}) collective-permute-start(f32[8,256]{1,0:T(8,128)S(1)} %get-tuple-element.42), channel_id=1, source_target_pairs={{0,1},{1,0},{2,3},{3,2},{4,5},{5,4},{6,7},{7,6},{8,9},{9,8},{10,11... | collective-permute-start | bytes 24584 | tf_op jit(solution)/shard_map/ppermute | solution.py:26
  107.2 4.9 %shard_map.45 = f32[2048,256]{1,0:T(8,128)} custom-call(s32[1]{0:T(128)} %bitcast.5.core_ref, bf16[1024,4096]{1,0:T(8,128)(2,1)} %get-tuple-element.36.mix_ref, bf16[1024,384]{1,0:T(8,128)(2,1)S(1)} %bitcast.30, bf16[1024,384]{1,0:T(8,128)(2,1)S(1)} %get-tuple-element.30.a_ref, bf16[1024,384]{1,0:T(8,128)(2,1)S(1)} %get-tuple-element.31.b_ref, ...), custom_call_target="tpu_custom_call" | custom-call | flops 1073741824 | bytes 8388608 | tf_op jit(solution)/shard_map/pallas_call | solution.py:253
  112.1 4.8 %all-to-all-done.3 = f16[32,32,256]{2,1,0:T(8,128)(2,1)S(1)} async-done(((f16[32,32,256]{2,1,0:T(8,128)(2,1)}), f16[32,32,256]{2,1,0:T(8,128)(2,1)S(1)}, u32[]{:S(2)}, u32[]{:S(2)}) %all-to-all-start.3) | async-done | bytes 524320 | tf_op jit(solution)/shard_map/all_to_all | solution.py:34
  116.8 2.2 %collective-permute-start.9 = (f16[32,32,256]{2,1,0:T(8,128)(2,1)S(1)}, f16[32,32,256]{2,1,0:T(8,128)(2,1)S(1)}, u32[]{:S(2)}, u32[]{:S(2)}) collective-permute-start(f16[32,32,256]{2,1,0:T(8,128)(2,1)S(1)} %all-to-all-done.3), channel_id=1, source_target_pairs={{0,1},{1,0},{2,3},{3,2},{4,5},{5,4},{6,7},{7,6},{8,9},{9,8},{10,11... | collective-permute-start | bytes 1572872 | tf_op jit(solution)/shard_map/ppermute | solution.py:26
  119.2 1.4 %collective-permute-done.9 = f16[32,32,256]{2,1,0:T(8,128)(2,1)S(1)} collective-permute-done((f16[32,32,256]{2,1,0:T(8,128)(2,1)S(1)}, f16[32,32,256]{2,1,0:T(8,128)(2,1)S(1)}, u32[]{:S(2)}, u32[]{:S(2)}) %collective-permute-start.9) | collective-permute-done | bytes 524320 | tf_op jit(solution)/shard_map/ppermute | solution.py:26
  (40 shorter events, 12.4 us)
Async XLA Ops:
  2.0 5.2 %collective-permute-start = (bf16[1024,384]{1,0:T(8,128)(2,1)S(1)}, bf16[1024,384]{1,0:T(8,128)(2,1)S(1)}, u32[]{:S(2)}, u32[]{:S(2)}) collective-permute-start(bf16[1024,384]{1,0:T(8,128)(2,1)S(1)} %get-tuple-element.31.b_ref), channel_id=1, source_target_pairs={{0,1},{1,0},{2,3},{3,2},{4,5},{5,4},{6,7},{7,6},{8,9},{9,8},{10,11... | collective-permute-start | bytes 2359304 | tf_op jit(solution)/shard_map/ppermute | solution.py:26
  8.2 20.9 %all-to-all-start = ((bf16[32,32,384]{2,1,0:T(8,128)(2,1)}), bf16[32,32,384]{2,1,0:T(8,128)(2,1)}, u32[]{:S(2)}, u32[]{:S(2)}) async-start(bf16[32,32,384]{2,1,0:T(8,128)(2,1)} %bitcast.1), calls=%async_computation | async-start | bytes 1572864 | tf_op jit(solution)/shard_map/all_to_all | solution.py:34
  15.2 2.7 %collective-permute-start.4 = (bf16[1024,384]{1,0:T(8,128)(2,1)S(1)}, bf16[1024,384]{1,0:T(8,128)(2,1)S(1)}, u32[]{:S(2)}, u32[]{:S(2)}) collective-permute-start(bf16[1024,384]{1,0:T(8,128)(2,1)S(1)} %get-tuple-element.30.a_ref), channel_id=1, source_target_pairs={{0,1},{1,0},{2,3},{3,2},{4,5},{5,4},{6,7},{7,6},{8,9},{9,8},{10,11... | collective-permute-start | bytes 2359304 | tf_op jit(solution)/shard_map/ppermute | solution.py:26
  18.1 0.9 copy-start
  29.2 28.7 %copy-start.1 = (bf16[1024,384]{1,0:T(8,128)(2,1)S(1)}, bf16[1024,384]{1,0:T(8,128)(2,1)}, u32[]{:S(2)}) copy-start(bf16[1024,384]{1,0:T(8,128)(2,1)} %copy-done) | copy-start | bytes 2359300
  30.0 9.7 %collective-permute-start.1 = (bf16[32,384]{1,0:T(8,128)(2,1)S(1)}, bf16[32,384]{1,0:T(8,128)(2,1)S(1)}, u32[]{:S(2)}, u32[]{:S(2)}) collective-permute-start(bf16[32,384]{1,0:T(8,128)(2,1)S(1)} %constant_dynamic-slice_fusion), channel_id=1, source_target_pairs={{0,4},{4,8},{8,12},{12,0},{1,5},{5,9},{9,13},{13,1},{2,6},{6,10},{... | collective-permute-start | bytes 73736 | tf_op jit(solution)/shard_map/ppermute | solution.py:30
  33.1 6.6 %collective-permute-start.2 = (bf16[32,384]{1,0:T(8,128)(2,1)S(1)}, bf16[32,384]{1,0:T(8,128)(2,1)S(1)}, u32[]{:S(2)}, u32[]{:S(2)}) collective-permute-start(bf16[32,384]{1,0:T(8,128)(2,1)S(1)} %constant_dynamic-slice_fusion), channel_id=1, source_target_pairs={{0,12},{4,0},{8,4},{12,8},{1,13},{5,1},{9,5},{13,9},{2,14},{6,2},{... | collective-permute-start | bytes 73736 | tf_op jit(solution)/shard_map/ppermute | solution.py:30
  35.3 6.8 %collective-permute-start.3 = (bf16[32,384]{1,0:T(8,128)(2,1)S(1)}, bf16[32,384]{1,0:T(8,128)(2,1)S(1)}, u32[]{:S(2)}, u32[]{:S(2)}) collective-permute-start(bf16[32,384]{1,0:T(8,128)(2,1)S(1)} %constant_dynamic-slice_fusion), channel_id=1, source_target_pairs={{0,8},{4,12},{8,0},{12,4},{1,9},{5,13},{9,1},{13,5},{2,10},{6,14},... | collective-permute-start | bytes 73736 | tf_op jit(solution)/shard_map/ppermute | solution.py:30
  69.4 16.6 %all-to-all-start.2 = ((f16[32,40,256]{2,1,0:T(8,128)(2,1)}), f16[32,40,256]{2,1,0:T(8,128)(2,1)}, u32[]{:S(2)}, u32[]{:S(2)}) async-start(f16[32,40,256]{2,1,0:T(8,128)(2,1)} %convert_element_type.42), calls=%async_computation.2 | async-start | bytes 1310720 | tf_op jit(solution)/shard_map/all_to_all | solution.py:34
  75.3 1.1 copy-start.2
  86.0 21.2 %collective-permute-start.8 = (f32[2048,256]{1,0:T(8,128)}, f32[2048,256]{1,0:T(8,128)}, u32[]{:S(2)}, u32[]{:S(2)}) collective-permute-start(f32[2048,256]{1,0:T(8,128)} %shard_map.43), channel_id=1, source_target_pairs={{0,1},{1,0},{2,3},{3,2},{4,5},{5,4},{6,7},{7,6},{8,9},{9,8},{10,11... | collective-permute-start | bytes 6291464 | tf_op jit(solution)/shard_map/ppermute | solution.py:26
  91.3 8.0 %collective-permute-start.5 = (f32[40,256]{1,0:T(8,128)S(1)}, f32[40,256]{1,0:T(8,128)S(1)}, u32[]{:S(2)}, u32[]{:S(2)}) collective-permute-start(f32[40,256]{1,0:T(8,128)S(1)} %maximum_bitcast_fusion.refs_0_), channel_id=1, source_target_pairs={{0,8},{4,12},{8,0},{12,4},{1,9},{5,13},{9,1},{13,5},{2,10},{6,14},... | collective-permute-start | bytes 122888 | tf_op jit(solution)/shard_map/ppermute | solution.py:30
  95.7 5.1 %collective-permute-start.6 = (f32[40,256]{1,0:T(8,128)S(1)}, f32[40,256]{1,0:T(8,128)S(1)}, u32[]{:S(2)}, u32[]{:S(2)}) collective-permute-start(f32[40,256]{1,0:T(8,128)S(1)} %maximum_bitcast_fusion.refs_0_), channel_id=1, source_target_pairs={{0,4},{4,8},{8,12},{12,0},{1,5},{5,9},{9,13},{13,1},{2,6},{6,10},{... | collective-permute-start | bytes 122888 | tf_op jit(solution)/shard_map/ppermute | solution.py:30
  96.0 4.8 %collective-permute-start.7 = (f32[40,256]{1,0:T(8,128)S(1)}, f32[40,256]{1,0:T(8,128)S(1)}, u32[]{:S(2)}, u32[]{:S(2)}) collective-permute-start(f32[40,256]{1,0:T(8,128)S(1)} %maximum_bitcast_fusion.refs_0_), channel_id=1, source_target_pairs={{0,12},{4,0},{8,4},{12,8},{1,13},{5,1},{9,5},{13,9},{2,14},{6,2},{... | collective-permute-start | bytes 122888 | tf_op jit(solution)/shard_map/ppermute | solution.py:30
  101.7 15.2 %all-to-all-start.3 = ((f16[32,32,256]{2,1,0:T(8,128)(2,1)}), f16[32,32,256]{2,1,0:T(8,128)(2,1)S(1)}, u32[]{:S(2)}, u32[]{:S(2)}) async-start(f16[32,32,256]{2,1,0:T(8,128)(2,1)} %broadcast_in_dim.11), calls=%async_computation.3 | async-start | bytes 1048576 | tf_op jit(solution)/shard_map/all_to_all | solution.py:34
  105.8 13.2 %collective-permute-start.10 = (f32[8,256]{1,0:T(8,128)S(1)}, f32[8,256]{1,0:T(8,128)S(1)}, u32[]{:S(2)}, u32[]{:S(2)}) collective-permute-start(f32[8,256]{1,0:T(8,128)S(1)} %get-tuple-element.42), channel_id=1, source_target_pairs={{0,1},{1,0},{2,3},{3,2},{4,5},{5,4},{6,7},{7,6},{8,9},{9,8},{10,11... | collective-permute-start | bytes 24584 | tf_op jit(solution)/shard_map/ppermute | solution.py:26
  116.8 3.7 %collective-permute-start.9 = (f16[32,32,256]{2,1,0:T(8,128)(2,1)S(1)}, f16[32,32,256]{2,1,0:T(8,128)(2,1)S(1)}, u32[]{:S(2)}, u32[]{:S(2)}) collective-permute-start(f16[32,32,256]{2,1,0:T(8,128)(2,1)S(1)} %all-to-all-done.3), channel_id=1, source_target_pairs={{0,1},{1,0},{2,3},{3,2},{4,5},{5,4},{6,7},{7,6},{8,9},{9,8},{10,11... | collective-permute-start | bytes 1572872 | tf_op jit(solution)/shard_map/ppermute | solution.py:26

commit v6 on v5

--- a/solution.py
+++ b/solution.py
@@ -13,11 +13,12 @@
 D = 256
 COLS = 64
 WIDE = D + 2 * COLS
-PLANE = ("y", "x", "v")
+PLANE = ("x", "v", "y")
 ALL = ("y", "x", "w", "v", "c")
 NY, NX, NW, NV, NC = 4, 4, 4, 2, 2
 NP = NY * NX * NV
-TILE_OWNER = 256
+TILE_OWNER = 512
+CHUNK = 512
 SCALE_ROWS = 8
 SMALL = 4 * 2**20
 
@@ -61,40 +62,38 @@
     return lax.optimization_barrier(values)
 
 
-def split_kernel(block_ref, here_ref, there_ref, sems):
-    rows = here_ref.shape[0]
+def part_kernel(block_ref, part_ref, sem, *, mine):
+    rows = part_ref.shape[0]
     core = lax.axis_index("c")
-    copies = [
-        pltpu.make_async_copy(
-            block_ref.at[pl.ds(pl.multiple_of(index * rows, rows), rows)], target, sems.at[slot]
-        )
-        for slot, (index, target) in enumerate(((1 - core, there_ref), (core, here_ref)))
-    ]
-    for copy in copies:
-        copy.start()
-    for copy in copies:
-        copy.wait()
-
-
-def split(block):
-    half = jax.ShapeDtypeStruct((block.shape[0] // NC, block.shape[1]), block.dtype)
-    return pl.pallas_call(
-        split_kernel,
+    first = pl.multiple_of((core if mine else 1 - core) * rows, rows)
+    copy = pltpu.make_async_copy(block_ref.at[pl.ds(first, rows)], part_ref, sem)
+    copy.start()
+    copy.wait()
+
+
+def part(block, mine):
+    return pl.pallas_call(
+        functools.partial(part_kernel, mine=mine),
         in_specs=[pl.BlockSpec(memory_space=pl.ANY)],
-        out_specs=[pl.BlockSpec(memory_space=pltpu.VMEM)] * 2,
-        out_shape=[half, half],
-        scratch_shapes=[pltpu.SemaphoreType.DMA((2,))],
+        out_specs=pl.BlockSpec(memory_space=pltpu.VMEM),
+        out_shape=jax.ShapeDtypeStruct((block.shape[0] // NC, block.shape[1]), block.dtype),
+        scratch_shapes=[pltpu.SemaphoreType.DMA],
         compiler_params=pltpu.CompilerParams(vmem_limit_bytes=SMALL),
     )(in_hbm(block))
 
 
 def broadcast_half(block, owner):
-    here, there = split(block)
+    there, here = part(block, False), part(block, True)
     level = owner // NC % (NW * NV)
-    start = (owner // (NC * NW * NV) * NV + level % NV) * (here.shape[0] // NP)
+    chip = owner // (NC * NW * NV)
+    at = {"y": (chip // NX, NY), "x": (chip % NX, NX), "v": (level % NV, NV)}
+    start = 0
+    for axis in PLANE:
+        start = start * at[axis][1] + at[axis][0]
+    start = start * (here.shape[0] // NP)
     here, other, level, start = tie(here, swap(there), level, start)
     half = jnp.where(owner % NC == lax.axis_index("c"), here, other)
-    piece = pick(exchange(half), NP, start)
+    (piece,) = tie(pick(exchange(half), NP, start))
     parts = (here, there, other, swap(here))
     piece = along_w(piece, level // NV)
     squares = jnp.concatenate([squared(part) for part in parts])[None, :]
@@ -169,23 +168,25 @@
             own_sq[span, :] = jnp.sum(feat * feat, axis=1, keepdims=True) * (0.5 / D) + math.log(2.0 * math.sqrt(COLS))
 
     units = choose(j, (a_ref, b_ref, c_ref, d_ref))
-    feat = units[:, :D]
-    swapped = jnp.concatenate([units[:, D + COLS :], units[:, D : D + COLS]], axis=1)
-    col = jnp.zeros(col_ref.shape, jnp.float32)
     contract_last = (((1,), (1,)), ((), ()))
+    chunks = [slice(i, i + CHUNK) for i in range(0, units.shape[0], CHUNK)]
+    feats = [units[chunk, :D] for chunk in chunks]
+    swapped = [jnp.concatenate([units[chunk, D + COLS :], units[chunk, D : D + COLS]], axis=1) for chunk in chunks]
+    cols = [jnp.zeros((8, CHUNK), jnp.float32) for _ in chunks]
     for span in spans:
-        cross = lax.dot_general(own_ref[span, :D], feat, contract_last, preferred_element_type=jnp.float32)
-        weight = lax.dot_general(own_ref[span, D:], swapped, contract_last, preferred_element_type=jnp.float32)
-        mixed = weight * jnp.exp(cross * (1.0 / D) - sq_ref[...] - own_sq[span, :])
-        mixed_b = mixed.astype(jnp.bfloat16)
-        mix_ref[span, :] = mixed_b
-        total[span, :] += jnp.dot(mixed_b, feat, preferred_element_type=jnp.float32)
-        col = col + jnp.sum(mixed.reshape(-1, *col.shape), axis=0)
-        lanes = mixed[:, :128]
-        for start in range(128, mixed.shape[1], 128):
-            lanes = lanes + mixed[:, start : start + 128]
-        row_sum[span, :] += lanes
-    col_ref[...] = col
+        lanes = row_sum[span, :]
+        for k, chunk in enumerate(chunks):
+            cross = lax.dot_general(own_ref[span, :D], feats[k], contract_last, preferred_element_type=jnp.float32)
+            weight = lax.dot_general(own_ref[span, D:], swapped[k], contract_last, preferred_element_type=jnp.float32)
+            mixed = weight * jnp.exp(cross * (1.0 / D) - sq_ref[:, chunk] - own_sq[span, :])
+            mix_ref[span, chunk] = mixed.astype(jnp.bfloat16)
+            cols[k] = cols[k] + jnp.sum(mixed.reshape(-1, 8, CHUNK), axis=0)
+            for start in range(0, CHUNK, 128):
+                lanes = lanes + mixed[:, start : start + 128]
+        row_sum[span, :] = lanes
+        total[span, :] += jnp.dot(mix_ref[span, :], units[:, :D], preferred_element_type=jnp.float32)
+    for k, chunk in enumerate(chunks):
+        col_ref[:, chunk] = cols[k]
 
     @pl.when(j == steps - 1)
     def _():
@@ -275,28 +276,27 @@
     )(core, in_hbm(mixed), own, *parts, col, *more)
 
 
-def place_kernel(mine_ref, other_ref, out_ref, sems):
-    rows = mine_ref.shape[0]
+def place_kernel(half_ref, *rest, mine):
+    out_ref, sem = rest[-2:]
+    rows = half_ref.shape[0]
     core = lax.axis_index("c")
-    copies = [
-        pltpu.make_async_copy(source, out_ref.at[pl.ds(pl.multiple_of(index * rows, rows), rows)], sems.at[slot])
-        for slot, (index, source) in enumerate(((core, mine_ref), (1 - core, other_ref)))
-    ]
-    for copy in copies:
-        copy.start()
-    for copy in copies:
-        copy.wait()
-
-
-def place(mine, other):
-    return pl.pallas_call(
-        place_kernel,
-        in_specs=[pl.BlockSpec(memory_space=pltpu.VMEM)] * 2,
+    first = pl.multiple_of((core if mine else 1 - core) * rows, rows)
+    copy = pltpu.make_async_copy(half_ref, out_ref.at[pl.ds(first, rows)], sem)
+    copy.start()
+    copy.wait()
+
+
+def place(half, out=None):
+    mine = out is None
+    return pl.pallas_call(
+        functools.partial(place_kernel, mine=mine),
+        in_specs=[pl.BlockSpec(memory_space=pltpu.VMEM)] + [pl.BlockSpec(memory_space=pl.ANY)] * (not mine),
         out_specs=pl.BlockSpec(memory_space=pl.ANY),
-        out_shape=jax.ShapeDtypeStruct((NC * mine.shape[0], mine.shape[1]), mine.dtype),
-        scratch_shapes=[pltpu.SemaphoreType.DMA((2,))],
+        out_shape=pltpu.HBM((NC * half.shape[0], half.shape[1]), half.dtype),
+        scratch_shapes=[pltpu.SemaphoreType.DMA],
+        input_output_aliases={} if mine else {1: 0},
         compiler_params=pltpu.CompilerParams(vmem_limit_bytes=SMALL),
-    )(mine, other)
+    )(half, *([] if mine else [out]))
 
 
 def local(unit_data, owner):
@@ -315,7 +315,7 @@
     mine, local_grad = tie(mine, local_grad)
     other = swap(mine)
     factor = 1.0 / math.sqrt(rows * NP * NW * NC)
-    owner_grad = place(unscale(mine, power, factor), unscale(other, power_other, factor))
+    owner_grad = place(unscale(other, power_other, factor), place(unscale(mine, power, factor)))
     return (owner_grad, local_grad)
 
 

time: 123 us -> 118 us (0.959)
  waiting for transfers between devices: 28.1 us -> 21.1 us
  starting transfers between devices: 46 us -> 48 us
    all_to_all x3, waiting for transfers between devices: 20 us -> 15.5 us  [exchange(): return lax.all_to_all(v, PLANE, 0, 0, tiled=True)]
    ppermute x5, starting transfers between devices: 11.6 us -> 14.4 us  [swap(): return lax.ppermute(v, 'c', [(0, 1), (1, 0)])]
    ppermute x5, waiting for transfers between devices: 4.11 us -> 1.94 us  [swap(): return lax.ppermute(v, 'c', [(0, 1), (1, 0)])]
    pallas_call x2 -> x4, Pallas kernels: 2.74 us -> 4.27 us  [the longest x2 2.29 us: part(): pl.pallas_call(functools.partial(part_kernel, mine=mine), in_specs=[pl.Bl...]
  transfers between devices with their start and end apart: 14 -> 14, of which waited for: 8 -> 7; matrix products, arithmetic and copies ran while one was open for 3% -> 3% of each run, Pallas kernels for 8% -> 10%
where the time goes in v6:
time: 118 us
  starting transfers between devices  48 us (41%)
  Pallas kernels  23.8 us (20%)
  waiting for transfers between devices  21.1 us (18%)
  blocking collectives  15 us (13%)
  other arithmetic  4.34 us (4%)
  local copies, waits for them, and re-layouts  3.77 us (3%)
  between operations  1.75 us (1%)
    ppermute x6, starting transfers between devices, shift(): return lax.ppermute(v, 'w', [(i, (i + k) % NW) for i in range(NW)])  17.7 us
    all_to_all x3, starting transfers between devices, exchange(): return lax.all_to_all(v, PLANE, 0, 0, tiled=True)  15.8 us
    all_to_all x3, waiting for transfers between devices, exchange(): return lax.all_to_all(v, PLANE, 0, 0, tiled=True)  15.5 us
    all_to_all x1, blocking collectives, exchange(): return lax.all_to_all(v, PLANE, 0, 0, tiled=True)  15 us
    ppermute x5, starting transfers between devices, swap(): return lax.ppermute(v, 'c', [(0, 1), (1, 0)])  14.4 us
    pallas_call x1, Pallas kernels, mix(): pl.pallas_call(functools.partial(mix_kernel, steps=steps), grid=(steps,),...  10.1 us
    pallas_call x2, Pallas kernels, local_terms(): pl.pallas_call(functools.partial(local_kernel, scale=scale), grid_spec=pl...  9.34 us
    ppermute x6, waiting for transfers between devices, shift(): return lax.ppermute(v, 'w', [(i, (i + k) % NW) for i in range(NW)])  3.61 us
  transfers between devices with their start and end apart: 14, of which 7 were waited for; matrix products, arithmetic and copies ran while one was open for 3% of the time, Pallas kernels for 10%

profile of v6, /device:TPU:1, one launch (start us, length us, event | category | flops | bytes accessed | tf_op | source)
XLA Modules:
  0.0 117.7 jit_solution(2013726210639430555)
XLA Ops:
  0.6 1.2 shard_map.42.b_ref
  1.8 3.3 %collective-permute-start = (bf16[1024,384]{1,0:T(8,128)(2,1)S(1)}, bf16[1024,384]{1,0:T(8,128)(2,1)S(1)}, u32[]{:S(2)}, u32[]{:S(2)}) collective-permute-start(bf16[1024,384]{1,0:T(8,128)(2,1)S(1)} %shard_map.42.b_ref), channel_id=1, source_target_pairs={{0,1},{1,0},{2,3},{3,2},{4,5},{5,4},{6,7},{7,6},{8,9},{9,8},{10,11... | collective-permute-start | bytes 2359304 | tf_op jit(solution)/shard_map/ppermute | solution.py:27
  8.0 6.8 %all-to-all-start = ((bf16[32,32,384]{2,1,0:T(8,128)(2,1)}), bf16[32,32,384]{2,1,0:T(8,128)(2,1)}, u32[]{:S(2)}, u32[]{:S(2)}) async-start(bf16[32,32,384]{2,1,0:T(8,128)(2,1)} %bitcast.1), calls=%async_computation | async-start | bytes 1572864 | tf_op jit(solution)/shard_map/all_to_all | solution.py:35
  16.1 1.5 %collective-permute-done.4.d_ref.b_ref = bf16[1024,384]{1,0:T(8,128)(2,1)S(1)} collective-permute-done((bf16[1024,384]{1,0:T(8,128)(2,1)S(1)}, bf16[1024,384]{1,0:T(8,128)(2,1)S(1)}, u32[]{:S(2)}, u32[]{:S(2)}) %collective-permute-start.4) | collective-permute-done | bytes 786464 | tf_op jit(solution)/shard_map/ppermute | solution.py:27
  18.8 9.0 %all-to-all-done = bf16[32,32,384]{2,1,0:T(8,128)(2,1)} async-done(((bf16[32,32,384]{2,1,0:T(8,128)(2,1)}), bf16[32,32,384]{2,1,0:T(8,128)(2,1)}, u32[]{:S(2)}, u32[]{:S(2)}) %all-to-all-start) | async-done | bytes 786464 | tf_op jit(solution)/shard_map/all_to_all | solution.py:35
  28.6 3.1 %collective-permute-start.1 = (bf16[32,384]{1,0:T(8,128)(2,1)S(1)}, bf16[32,384]{1,0:T(8,128)(2,1)S(1)}, u32[]{:S(2)}, u32[]{:S(2)}) collective-permute-start(bf16[32,384]{1,0:T(8,128)(2,1)S(1)} %constant_dynamic-slice_fusion), channel_id=1, source_target_pairs={{0,4},{4,8},{8,12},{12,0},{1,5},{5,9},{9,13},{13,1},{2,6},{6,10},{... | collective-permute-start | bytes 73736 | tf_op jit(solution)/shard_map/ppermute | solution.py:31
  31.7 2.2 %collective-permute-start.2 = (bf16[32,384]{1,0:T(8,128)(2,1)S(1)}, bf16[32,384]{1,0:T(8,128)(2,1)S(1)}, u32[]{:S(2)}, u32[]{:S(2)}) collective-permute-start(bf16[32,384]{1,0:T(8,128)(2,1)S(1)} %constant_dynamic-slice_fusion), channel_id=1, source_target_pairs={{0,12},{4,0},{8,4},{12,8},{1,13},{5,1},{9,5},{13,9},{2,14},{6,2},{... | collective-permute-start | bytes 73736 | tf_op jit(solution)/shard_map/ppermute | solution.py:31
  33.9 4.4 %collective-permute-start.3 = (bf16[32,384]{1,0:T(8,128)(2,1)S(1)}, bf16[32,384]{1,0:T(8,128)(2,1)S(1)}, u32[]{:S(2)}, u32[]{:S(2)}) collective-permute-start(bf16[32,384]{1,0:T(8,128)(2,1)S(1)} %constant_dynamic-slice_fusion), channel_id=1, source_target_pairs={{0,8},{4,12},{8,0},{12,4},{1,9},{5,13},{9,1},{13,5},{2,10},{6,14},... | collective-permute-start | bytes 73736 | tf_op jit(solution)/shard_map/ppermute | solution.py:31
  38.3 2.2 %collective-permute-done.3 = bf16[32,384]{1,0:T(8,128)(2,1)S(1)} collective-permute-done((bf16[32,384]{1,0:T(8,128)(2,1)S(1)}, bf16[32,384]{1,0:T(8,128)(2,1)S(1)}, u32[]{:S(2)}, u32[]{:S(2)}) %collective-permute-start.3) | collective-permute-done | bytes 24608 | tf_op jit(solution)/shard_map/ppermute | solution.py:31
  40.6 15.0 %all_to_all.27 = bf16[32,32,384]{2,1,0:T(8,128)(2,1)S(1)} all-to-all(bf16[32,32,384]{2,1,0:T(8,128)(2,1)S(1)} %broadcast_in_dim.9), channel_id=1, replica_groups=mesh['y'=4,'x'=4,'w'=4,'v'=2,'c'=2] {'x','v','y'}, dimensions={0} | all-to-all | bytes 1572864 | tf_op jit(solution)/shard_map/all_to_all | solution.py:35
  55.6 10.1 %shard_map.43 = (bf16[1024,4096]{1,0:T(8,128)(2,1)}, f32[32,40,256]{2,1,0:T(8,128)S(1)}, f32[8,4096]{1,0:T(8,128)S(1)}) custom-call(bf16[1024,384]{1,0:T(8,128)(2,1)S(1)} %bitcast.28, bf16[1024,384]{1,0:T(8,128)(2,1)S(1)} %shard_map.41.a_ref, bf16[1024,384]{1,0:T(8,128)(2,1)S(1)} %shard_map.42.b_ref, bf16[1024,384]{1,0:T(8,128)(2,1)S(1)} %collective-permute-done.c_ref.a_ref, ...), custom_call_target="tpu_custom_call" | custom-call | flops 5368709120 | bytes 13369344 | tf_op jit(solution)/shard_map/pallas_call | solution.py:211
  66.7 4.6 %all-to-all-start.2 = ((f16[32,40,256]{2,1,0:T(8,128)(2,1)}), f16[32,40,256]{2,1,0:T(8,128)(2,1)}, u32[]{:S(2)}, u32[]{:S(2)}) async-start(f16[32,40,256]{2,1,0:T(8,128)(2,1)} %convert_element_type.42), calls=%async_computation.2 | async-start | bytes 1310720 | tf_op jit(solution)/shard_map/all_to_all | solution.py:35
  72.5 4.5 %shard_map.44 = f32[2048,256]{1,0:T(8,128)} custom-call(s32[1]{0:T(128)} %bitcast.5.core_ref, bf16[1024,4096]{1,0:T(8,128)(2,1)} %get-tuple-element.32.mix_ref, bf16[1024,384]{1,0:T(8,128)(2,1)S(1)} %bitcast.29, bf16[1024,384]{1,0:T(8,128)(2,1)S(1)} %collective-permute-done.c_ref.a_ref, bf16[1024,384]{1,0:T(8,128)(2,1)S(1)} %copy-done.2, ...), custom_call_target="tpu_custom_call" | custom-call | flops 1073741824 | bytes 8388608 | tf_op jit(solution)/shard_map/pallas_call | solution.py:254
  76.9 4.0 %all-to-all-done.2 = f16[32,40,256]{2,1,0:T(8,128)(2,1)} async-done(((f16[32,40,256]{2,1,0:T(8,128)(2,1)}), f16[32,40,256]{2,1,0:T(8,128)(2,1)}, u32[]{:S(2)}, u32[]{:S(2)}) %all-to-all-start.2) | async-done | bytes 655392 | tf_op jit(solution)/shard_map/all_to_all | solution.py:35
  80.9 5.3 %collective-permute-start.8 = (f32[2048,256]{1,0:T(8,128)}, f32[2048,256]{1,0:T(8,128)}, u32[]{:S(2)}, u32[]{:S(2)}) collective-permute-start(f32[2048,256]{1,0:T(8,128)} %shard_map.44), channel_id=1, source_target_pairs={{0,1},{1,0},{2,3},{3,2},{4,5},{5,4},{6,7},{7,6},{8,9},{9,8},{10,11... | collective-permute-start | bytes 6291464 | tf_op jit(solution)/shard_map/ppermute | solution.py:27
  86.2 1.2 %bitcast_convert_fusion = f32[32,5,8,256]{3,2,1,0:T(8,128)S(1)} fusion(f16[32,40,256]{2,1,0:T(8,128)(2,1)} %all-to-all-done.2), kind=kLoop, calls=%fused_computation.9 | loop fusion | flops 327680 | bytes 1966080 | tf_op jit(solution)/shard_map/convert_element_type | solution.py:115
  87.6 4.5 %collective-permute-start.5 = (f32[40,256]{1,0:T(8,128)S(1)}, f32[40,256]{1,0:T(8,128)S(1)}, u32[]{:S(2)}, u32[]{:S(2)}) collective-permute-start(f32[40,256]{1,0:T(8,128)S(1)} %maximum_bitcast_fusion.refs_0_), channel_id=1, source_target_pairs={{0,8},{4,12},{8,0},{12,4},{1,9},{5,13},{9,1},{13,5},{2,10},{6,14},... | collective-permute-start | bytes 122888 | tf_op jit(solution)/shard_map/ppermute | solution.py:31
  92.1 3.6 %collective-permute-start.7 = (f32[40,256]{1,0:T(8,128)S(1)}, f32[40,256]{1,0:T(8,128)S(1)}, u32[]{:S(2)}, u32[]{:S(2)}) collective-permute-start(f32[40,256]{1,0:T(8,128)S(1)} %maximum_bitcast_fusion.refs_0_), channel_id=1, source_target_pairs={{0,12},{4,0},{8,4},{12,8},{1,13},{5,1},{9,5},{13,9},{2,14},{6,2},{... | collective-permute-start | bytes 122888 | tf_op jit(solution)/shard_map/ppermute | solution.py:31
  95.7 1.4 %collective-permute-done.6.refs_2_ = f32[40,256]{1,0:T(8,128)S(1)} collective-permute-done((f32[40,256]{1,0:T(8,128)S(1)}, f32[40,256]{1,0:T(8,128)S(1)}, u32[]{:S(2)}, u32[]{:S(2)}) %collective-permute-start.6) | collective-permute-done | bytes 40992 | tf_op jit(solution)/shard_map/ppermute | solution.py:31
  98.0 4.4 %all-to-all-start.3 = ((f16[32,32,256]{2,1,0:T(8,128)(2,1)}), f16[32,32,256]{2,1,0:T(8,128)(2,1)S(1)}, u32[]{:S(2)}, u32[]{:S(2)}) async-start(f16[32,32,256]{2,1,0:T(8,128)(2,1)} %broadcast_in_dim.11), calls=%async_computation.3 | async-start | bytes 1048576 | tf_op jit(solution)/shard_map/all_to_all | solution.py:35
  102.4 1.9 %collective-permute-start.10 = (f32[8,256]{1,0:T(8,128)S(1)}, f32[8,256]{1,0:T(8,128)S(1)}, u32[]{:S(2)}, u32[]{:S(2)}) collective-permute-start(f32[8,256]{1,0:T(8,128)S(1)} %get-tuple-element.38), channel_id=1, source_target_pairs={{0,1},{1,0},{2,3},{3,2},{4,5},{5,4},{6,7},{7,6},{8,9},{9,8},{10,11... | collective-permute-start | bytes 24584 | tf_op jit(solution)/shard_map/ppermute | solution.py:27
  104.3 4.9 %shard_map.46 = f32[2048,256]{1,0:T(8,128)} custom-call(s32[1]{0:T(128)} %bitcast.5.core_ref, bf16[1024,4096]{1,0:T(8,128)(2,1)} %get-tuple-element.32.mix_ref, bf16[1024,384]{1,0:T(8,128)(2,1)S(1)} %bitcast.30, bf16[1024,384]{1,0:T(8,128)(2,1)S(1)} %shard_map.41.a_ref, bf16[1024,384]{1,0:T(8,128)(2,1)S(1)} %shard_map.42.b_ref, ...), custom_call_target="tpu_custom_call" | custom-call | flops 1073741824 | bytes 8388608 | tf_op jit(solution)/shard_map/pallas_call | solution.py:254
  109.2 2.5 %all-to-all-done.3 = f16[32,32,256]{2,1,0:T(8,128)(2,1)S(1)} async-done(((f16[32,32,256]{2,1,0:T(8,128)(2,1)}), f16[32,32,256]{2,1,0:T(8,128)(2,1)S(1)}, u32[]{:S(2)}, u32[]{:S(2)}) %all-to-all-start.3) | async-done | bytes 524320 | tf_op jit(solution)/shard_map/all_to_all | solution.py:35
  111.7 3.2 %collective-permute-start.9 = (f16[32,32,256]{2,1,0:T(8,128)(2,1)S(1)}, f16[32,32,256]{2,1,0:T(8,128)(2,1)S(1)}, u32[]{:S(2)}, u32[]{:S(2)}) collective-permute-start(f16[32,32,256]{2,1,0:T(8,128)(2,1)S(1)} %all-to-all-done.3), channel_id=1, source_target_pairs={{0,1},{1,0},{2,3},{3,2},{4,5},{5,4},{6,7},{7,6},{8,9},{9,8},{10,11... | collective-permute-start | bytes 1572872 | tf_op jit(solution)/shard_map/ppermute | solution.py:27
  (42 shorter events, 11.2 us)
Async XLA Ops:
  1.8 5.2 %collective-permute-start = (bf16[1024,384]{1,0:T(8,128)(2,1)S(1)}, bf16[1024,384]{1,0:T(8,128)(2,1)S(1)}, u32[]{:S(2)}, u32[]{:S(2)}) collective-permute-start(bf16[1024,384]{1,0:T(8,128)(2,1)S(1)} %shard_map.42.b_ref), channel_id=1, source_target_pairs={{0,1},{1,0},{2,3},{3,2},{4,5},{5,4},{6,7},{7,6},{8,9},{9,8},{10,11... | collective-permute-start | bytes 2359304 | tf_op jit(solution)/shard_map/ppermute | solution.py:27
  8.0 19.7 %all-to-all-start = ((bf16[32,32,384]{2,1,0:T(8,128)(2,1)}), bf16[32,32,384]{2,1,0:T(8,128)(2,1)}, u32[]{:S(2)}, u32[]{:S(2)}) async-start(bf16[32,32,384]{2,1,0:T(8,128)(2,1)} %bitcast.1), calls=%async_computation | async-start | bytes 1572864 | tf_op jit(solution)/shard_map/all_to_all | solution.py:35
  15.0 2.6 %collective-permute-start.4 = (bf16[1024,384]{1,0:T(8,128)(2,1)S(1)}, bf16[1024,384]{1,0:T(8,128)(2,1)S(1)}, u32[]{:S(2)}, u32[]{:S(2)}) collective-permute-start(bf16[1024,384]{1,0:T(8,128)(2,1)S(1)} %shard_map.41.a_ref), channel_id=1, source_target_pairs={{0,1},{1,0},{2,3},{3,2},{4,5},{5,4},{6,7},{7,6},{8,9},{9,8},{10,11... | collective-permute-start | bytes 2359304 | tf_op jit(solution)/shard_map/ppermute | solution.py:27
  17.9 0.9 copy-start
  27.7 27.8 %copy-start.1 = (bf16[1024,384]{1,0:T(8,128)(2,1)S(1)}, bf16[1024,384]{1,0:T(8,128)(2,1)}, u32[]{:S(2)}) copy-start(bf16[1024,384]{1,0:T(8,128)(2,1)} %copy-done) | copy-start | bytes 2359300
  28.6 9.7 %collective-permute-start.1 = (bf16[32,384]{1,0:T(8,128)(2,1)S(1)}, bf16[32,384]{1,0:T(8,128)(2,1)S(1)}, u32[]{:S(2)}, u32[]{:S(2)}) collective-permute-start(bf16[32,384]{1,0:T(8,128)(2,1)S(1)} %constant_dynamic-slice_fusion), channel_id=1, source_target_pairs={{0,4},{4,8},{8,12},{12,0},{1,5},{5,9},{9,13},{13,1},{2,6},{6,10},{... | collective-permute-start | bytes 73736 | tf_op jit(solution)/shard_map/ppermute | solution.py:31
  31.7 6.6 %collective-permute-start.2 = (bf16[32,384]{1,0:T(8,128)(2,1)S(1)}, bf16[32,384]{1,0:T(8,128)(2,1)S(1)}, u32[]{:S(2)}, u32[]{:S(2)}) collective-permute-start(bf16[32,384]{1,0:T(8,128)(2,1)S(1)} %constant_dynamic-slice_fusion), channel_id=1, source_target_pairs={{0,12},{4,0},{8,4},{12,8},{1,13},{5,1},{9,5},{13,9},{2,14},{6,2},{... | collective-permute-start | bytes 73736 | tf_op jit(solution)/shard_map/ppermute | solution.py:31
  33.9 6.6 %collective-permute-start.3 = (bf16[32,384]{1,0:T(8,128)(2,1)S(1)}, bf16[32,384]{1,0:T(8,128)(2,1)S(1)}, u32[]{:S(2)}, u32[]{:S(2)}) collective-permute-start(bf16[32,384]{1,0:T(8,128)(2,1)S(1)} %constant_dynamic-slice_fusion), channel_id=1, source_target_pairs={{0,8},{4,12},{8,0},{12,4},{1,9},{5,13},{9,1},{13,5},{2,10},{6,14},... | collective-permute-start | bytes 73736 | tf_op jit(solution)/shard_map/ppermute | solution.py:31
  66.7 14.2 %all-to-all-start.2 = ((f16[32,40,256]{2,1,0:T(8,128)(2,1)}), f16[32,40,256]{2,1,0:T(8,128)(2,1)}, u32[]{:S(2)}, u32[]{:S(2)}) async-start(f16[32,40,256]{2,1,0:T(8,128)(2,1)} %convert_element_type.42), calls=%async_computation.2 | async-start | bytes 1310720 | tf_op jit(solution)/shard_map/all_to_all | solution.py:35
  71.3 1.1 copy-start.2
  80.9 23.4 %collective-permute-start.8 = (f32[2048,256]{1,0:T(8,128)}, f32[2048,256]{1,0:T(8,128)}, u32[]{:S(2)}, u32[]{:S(2)}) collective-permute-start(f32[2048,256]{1,0:T(8,128)} %shard_map.44), channel_id=1, source_target_pairs={{0,1},{1,0},{2,3},{3,2},{4,5},{5,4},{6,7},{7,6},{8,9},{9,8},{10,11... | collective-permute-start | bytes 6291464 | tf_op jit(solution)/shard_map/ppermute | solution.py:27
  87.6 8.1 %collective-permute-start.5 = (f32[40,256]{1,0:T(8,128)S(1)}, f32[40,256]{1,0:T(8,128)S(1)}, u32[]{:S(2)}, u32[]{:S(2)}) collective-permute-start(f32[40,256]{1,0:T(8,128)S(1)} %maximum_bitcast_fusion.refs_0_), channel_id=1, source_target_pairs={{0,8},{4,12},{8,0},{12,4},{1,9},{5,13},{9,1},{13,5},{2,10},{6,14},... | collective-permute-start | bytes 122888 | tf_op jit(solution)/shard_map/ppermute | solution.py:31
  92.1 5.0 %collective-permute-start.6 = (f32[40,256]{1,0:T(8,128)S(1)}, f32[40,256]{1,0:T(8,128)S(1)}, u32[]{:S(2)}, u32[]{:S(2)}) collective-permute-start(f32[40,256]{1,0:T(8,128)S(1)} %maximum_bitcast_fusion.refs_0_), channel_id=1, source_target_pairs={{0,4},{4,8},{8,12},{12,0},{1,5},{5,9},{9,13},{13,1},{2,6},{6,10},{... | collective-permute-start | bytes 122888 | tf_op jit(solution)/shard_map/ppermute | solution.py:31
  92.1 5.0 %collective-permute-start.7 = (f32[40,256]{1,0:T(8,128)S(1)}, f32[40,256]{1,0:T(8,128)S(1)}, u32[]{:S(2)}, u32[]{:S(2)}) collective-permute-start(f32[40,256]{1,0:T(8,128)S(1)} %maximum_bitcast_fusion.refs_0_), channel_id=1, source_target_pairs={{0,12},{4,0},{8,4},{12,8},{1,13},{5,1},{9,5},{13,9},{2,14},{6,2},{... | collective-permute-start | bytes 122888 | tf_op jit(solution)/shard_map/ppermute | solution.py:31
  98.0 13.7 %all-to-all-start.3 = ((f16[32,32,256]{2,1,0:T(8,128)(2,1)}), f16[32,32,256]{2,1,0:T(8,128)(2,1)S(1)}, u32[]{:S(2)}, u32[]{:S(2)}) async-start(f16[32,32,256]{2,1,0:T(8,128)(2,1)} %broadcast_in_dim.11), calls=%async_computation.3 | async-start | bytes 1048576 | tf_op jit(solution)/shard_map/all_to_all | solution.py:35
  102.4 12.5 %collective-permute-start.10 = (f32[8,256]{1,0:T(8,128)S(1)}, f32[8,256]{1,0:T(8,128)S(1)}, u32[]{:S(2)}, u32[]{:S(2)}) collective-permute-start(f32[8,256]{1,0:T(8,128)S(1)} %get-tuple-element.38), channel_id=1, source_target_pairs={{0,1},{1,0},{2,3},{3,2},{4,5},{5,4},{6,7},{7,6},{8,9},{9,8},{10,11... | collective-permute-start | bytes 24584 | tf_op jit(solution)/shard_map/ppermute | solution.py:27
  111.7 4.7 %collective-permute-start.9 = (f16[32,32,256]{2,1,0:T(8,128)(2,1)S(1)}, f16[32,32,256]{2,1,0:T(8,128)(2,1)S(1)}, u32[]{:S(2)}, u32[]{:S(2)}) collective-permute-start(f16[32,32,256]{2,1,0:T(8,128)(2,1)S(1)} %all-to-all-done.3), channel_id=1, source_target_pairs={{0,1},{1,0},{2,3},{3,2},{4,5},{5,4},{6,7},{7,6},{8,9},{9,8},{10,11... | collective-permute-start | bytes 1572872 | tf_op jit(solution)/shard_map/ppermute | solution.py:27

commit v7 on v6

--- a/solution.py
+++ b/solution.py
@@ -20,6 +20,7 @@
 TILE_OWNER = 512
 CHUNK = 512
 SCALE_ROWS = 8
+LANES = 128
 SMALL = 4 * 2**20
 
 
@@ -112,26 +113,29 @@
 
 
 def sum_pieces(v):
-    groups = v.reshape(v.shape[0], -1, SCALE_ROWS, D).astype(jnp.float32)
+    groups = v.reshape(v.shape[0], -1, SCALE_ROWS, LANES).astype(jnp.float32)
     powers = groups[:, -1]
     piece = jnp.sum(groups[:, :-1] * jnp.exp2(powers)[:, None], axis=0)
-    return jnp.concatenate([piece, jnp.max(powers, axis=0)[None]], axis=0).reshape(-1, D)
+    return jnp.concatenate([piece, jnp.max(powers, axis=0)[None]], axis=0).reshape(-1, LANES)
 
 
 def join_kernel(*refs):
     parts, piece_ref, power_ref = refs[:-2], refs[-2], refs[-1]
-    rows = piece_ref.shape[0]
+    rows = parts[0].shape[0] - SCALE_ROWS
     piece = (parts[0][:rows] + parts[1][:rows]) + (parts[2][:rows] + parts[3][:rows])
     power = jnp.maximum(
         jnp.maximum(parts[0][rows:], parts[1][rows:]), jnp.maximum(parts[2][rows:], parts[3][rows:])
     ) + math.log2(NP * NW)
     factor = jnp.exp(power * -math.log(2.0))
-    piece_ref[...] = (piece.reshape(-1, SCALE_ROWS, D) * factor[None]).reshape(rows, D)
-    power_ref[...] = power
+    piece = (piece.reshape(-1, SCALE_ROWS, LANES) * factor[None]).reshape(rows, LANES)
+    height = piece_ref.shape[0]
+    for k in range(D // LANES):
+        piece_ref[:, k * LANES : (k + 1) * LANES] = piece[k * height : (k + 1) * height]
+        power_ref[:, k * LANES : (k + 1) * LANES] = power
 
 
 def join(*parts):
-    rows = parts[0].shape[0] - SCALE_ROWS
+    rows = (parts[0].shape[0] - SCALE_ROWS) * LANES // D
     return pl.pallas_call(
         join_kernel,
         out_shape=[
@@ -199,27 +203,29 @@
         power, factor = scaling(top)
         piece_rows = rows // NP
         for p in range(NP):
-            term_ref[p, :piece_rows] = total[p * piece_rows : (p + 1) * piece_rows, :] * factor
-            term_ref[p, piece_rows:] = jnp.broadcast_to(power, (SCALE_ROWS, D))
+            scaled = total[p * piece_rows : (p + 1) * piece_rows, :] * factor
+            for k in range(D // LANES):
+                term_ref[p, k * piece_rows : (k + 1) * piece_rows] = scaled[:, k * LANES : (k + 1) * LANES]
+            term_ref[p, D // LANES * piece_rows :] = jnp.broadcast_to(power, (SCALE_ROWS, LANES))
 
 
 def mix(own, parts, unit_sq):
     rows, tile = own.shape[0], parts[0].shape[0]
     steps = len(parts)
     count = steps * tile
-    packed_rows = rows // NP + SCALE_ROWS
+    packed_rows = D // LANES * rows // NP + SCALE_ROWS
     return pl.pallas_call(
         functools.partial(mix_kernel, steps=steps),
         grid=(steps,),
         in_specs=[pl.BlockSpec(memory_space=pltpu.VMEM)] * (1 + steps) + [pl.BlockSpec((1, tile), lambda j: (0, j))],
         out_specs=[
             pl.BlockSpec((rows, tile), lambda j: (0, j)),
-            pl.BlockSpec((NP, packed_rows, D), lambda j: (0, 0, 0)),
+            pl.BlockSpec((NP, packed_rows, LANES), lambda j: (0, 0, 0)),
             pl.BlockSpec((8, tile), lambda j: (0, j)),
         ],
         out_shape=[
             pltpu.HBM((rows, count), jnp.bfloat16),
-            jax.ShapeDtypeStruct((NP, packed_rows, D), jnp.float32),
+            jax.ShapeDtypeStruct((NP, packed_rows, LANES), jnp.float32),
             jax.ShapeDtypeStruct((8, count), jnp.float32),
         ],
         scratch_shapes=[pltpu.VMEM((rows, D), jnp.float32), pltpu.VMEM((rows, 1), jnp.float32), pltpu.VMEM((rows, 128), jnp.float32)],
@@ -276,27 +282,23 @@
     )(core, in_hbm(mixed), own, *parts, col, *more)
 
 
-def place_kernel(half_ref, *rest, mine):
-    out_ref, sem = rest[-2:]
+def place_kernel(half_ref, out_ref, sem):
     rows = half_ref.shape[0]
-    core = lax.axis_index("c")
-    first = pl.multiple_of((core if mine else 1 - core) * rows, rows)
+    first = pl.multiple_of(lax.axis_index("c") * rows, rows)
     copy = pltpu.make_async_copy(half_ref, out_ref.at[pl.ds(first, rows)], sem)
     copy.start()
     copy.wait()
 
 
-def place(half, out=None):
-    mine = out is None
-    return pl.pallas_call(
-        functools.partial(place_kernel, mine=mine),
-        in_specs=[pl.BlockSpec(memory_space=pltpu.VMEM)] + [pl.BlockSpec(memory_space=pl.ANY)] * (not mine),
+def place(half):
+    return pl.pallas_call(
+        place_kernel,
+        in_specs=[pl.BlockSpec(memory_space=pltpu.VMEM)],
         out_specs=pl.BlockSpec(memory_space=pl.ANY),
         out_shape=pltpu.HBM((NC * half.shape[0], half.shape[1]), half.dtype),
         scratch_shapes=[pltpu.SemaphoreType.DMA],
-        input_output_aliases={} if mine else {1: 0},
         compiler_params=pltpu.CompilerParams(vmem_limit_bytes=SMALL),
-    )(half, *([] if mine else [out]))
+    )(half)
 
 
 def local(unit_data, owner):
@@ -315,7 +317,10 @@
     mine, local_grad = tie(mine, local_grad)
     other = swap(mine)
     factor = 1.0 / math.sqrt(rows * NP * NW * NC)
-    owner_grad = place(unscale(other, power_other, factor), place(unscale(mine, power, factor)))
+    first = (1 - lax.axis_index("c")) * (rows // NC)
+    owner_grad = lax.dynamic_update_slice(
+        place(unscale(mine, power, factor)), unscale(other, power_other, factor), (first, 0), allow_negative_indices=False
+    )
     return (owner_grad, local_grad)
 
 

time: 118 us -> 117 us (level)
  no operation moved by 1% of the time
where the time goes in v7:
time: 117 us
  starting transfers between devices  48.2 us (41%)
  Pallas kernels  22.8 us (19%)
  waiting for transfers between devices  20 us (17%)
  blocking collectives  15 us (13%)
  other arithmetic  5.19 us (4%)
  local copies, waits for them, and re-layouts  3.77 us (3%)
  between operations  1.58 us (1%)
    ppermute x6, starting transfers between devices, shift(): return lax.ppermute(v, 'w', [(i, (i + k) % NW) for i in range(NW)])  17.7 us
    all_to_all x3, starting transfers between devices, exchange(): return lax.all_to_all(v, PLANE, 0, 0, tiled=True)  15.3 us
    ppermute x5, starting transfers between devices, swap(): return lax.ppermute(v, 'c', [(0, 1), (1, 0)])  15.2 us
    all_to_all x1, blocking collectives, exchange(): return lax.all_to_all(v, PLANE, 0, 0, tiled=True)  15 us
    all_to_all x3, waiting for transfers between devices, exchange(): return lax.all_to_all(v, PLANE, 0, 0, tiled=True)  14.5 us
    pallas_call x1, Pallas kernels, mix(): pl.pallas_call(functools.partial(mix_kernel, steps=steps), grid=(steps,),...  10.1 us
    pallas_call x2, Pallas kernels, local_terms(): pl.pallas_call(functools.partial(local_kernel, scale=scale), grid_spec=pl...  9.34 us
    ppermute x6, waiting for transfers between devices, shift(): return lax.ppermute(v, 'w', [(i, (i + k) % NW) for i in range(NW)])  3.56 us
  transfers between devices with their start and end apart: 14, of which 7 were waited for; matrix products, arithmetic and copies ran while one was open for 3% of the time, Pallas kernels for 10%

profile of v7, /device:TPU:1, one launch (start us, length us, event | category | flops | bytes accessed | tf_op | source)
XLA Modules:
  0.0 116.6 jit_solution(10015724931567671831)
XLA Ops:
  0.6 1.2 shard_map.42.b_ref
  1.8 3.3 %collective-permute-start = (bf16[1024,384]{1,0:T(8,128)(2,1)S(1)}, bf16[1024,384]{1,0:T(8,128)(2,1)S(1)}, u32[]{:S(2)}, u32[]{:S(2)}) collective-permute-start(bf16[1024,384]{1,0:T(8,128)(2,1)S(1)} %shard_map.42.b_ref), channel_id=1, source_target_pairs={{0,1},{1,0},{2,3},{3,2},{4,5},{5,4},{6,7},{7,6},{8,9},{9,8},{10,11... | collective-permute-start | bytes 2359304 | tf_op jit(solution)/shard_map/ppermute | solution.py:28
  8.0 6.8 %all-to-all-start = ((bf16[32,32,384]{2,1,0:T(8,128)(2,1)}), bf16[32,32,384]{2,1,0:T(8,128)(2,1)}, u32[]{:S(2)}, u32[]{:S(2)}) async-start(bf16[32,32,384]{2,1,0:T(8,128)(2,1)} %bitcast.1), calls=%async_computation | async-start | bytes 1572864 | tf_op jit(solution)/shard_map/all_to_all | solution.py:36
  16.1 1.5 %collective-permute-done.4.d_ref.b_ref = bf16[1024,384]{1,0:T(8,128)(2,1)S(1)} collective-permute-done((bf16[1024,384]{1,0:T(8,128)(2,1)S(1)}, bf16[1024,384]{1,0:T(8,128)(2,1)S(1)}, u32[]{:S(2)}, u32[]{:S(2)}) %collective-permute-start.4) | collective-permute-done | bytes 786464 | tf_op jit(solution)/shard_map/ppermute | solution.py:28
  18.8 9.0 %all-to-all-done = bf16[32,32,384]{2,1,0:T(8,128)(2,1)} async-done(((bf16[32,32,384]{2,1,0:T(8,128)(2,1)}), bf16[32,32,384]{2,1,0:T(8,128)(2,1)}, u32[]{:S(2)}, u32[]{:S(2)}) %all-to-all-start) | async-done | bytes 786464 | tf_op jit(solution)/shard_map/all_to_all | solution.py:36
  28.6 3.1 %collective-permute-start.1 = (bf16[32,384]{1,0:T(8,128)(2,1)S(1)}, bf16[32,384]{1,0:T(8,128)(2,1)S(1)}, u32[]{:S(2)}, u32[]{:S(2)}) collective-permute-start(bf16[32,384]{1,0:T(8,128)(2,1)S(1)} %constant_dynamic-slice_fusion), channel_id=1, source_target_pairs={{0,4},{4,8},{8,12},{12,0},{1,5},{5,9},{9,13},{13,1},{2,6},{6,10},{... | collective-permute-start | bytes 73736 | tf_op jit(solution)/shard_map/ppermute | solution.py:32
  31.7 2.2 %collective-permute-start.2 = (bf16[32,384]{1,0:T(8,128)(2,1)S(1)}, bf16[32,384]{1,0:T(8,128)(2,1)S(1)}, u32[]{:S(2)}, u32[]{:S(2)}) collective-permute-start(bf16[32,384]{1,0:T(8,128)(2,1)S(1)} %constant_dynamic-slice_fusion), channel_id=1, source_target_pairs={{0,12},{4,0},{8,4},{12,8},{1,13},{5,1},{9,5},{13,9},{2,14},{6,2},{... | collective-permute-start | bytes 73736 | tf_op jit(solution)/shard_map/ppermute | solution.py:32
  33.9 4.4 %collective-permute-start.3 = (bf16[32,384]{1,0:T(8,128)(2,1)S(1)}, bf16[32,384]{1,0:T(8,128)(2,1)S(1)}, u32[]{:S(2)}, u32[]{:S(2)}) collective-permute-start(bf16[32,384]{1,0:T(8,128)(2,1)S(1)} %constant_dynamic-slice_fusion), channel_id=1, source_target_pairs={{0,8},{4,12},{8,0},{12,4},{1,9},{5,13},{9,1},{13,5},{2,10},{6,14},... | collective-permute-start | bytes 73736 | tf_op jit(solution)/shard_map/ppermute | solution.py:32
  38.3 2.2 %collective-permute-done.3 = bf16[32,384]{1,0:T(8,128)(2,1)S(1)} collective-permute-done((bf16[32,384]{1,0:T(8,128)(2,1)S(1)}, bf16[32,384]{1,0:T(8,128)(2,1)S(1)}, u32[]{:S(2)}, u32[]{:S(2)}) %collective-permute-start.3) | collective-permute-done | bytes 24608 | tf_op jit(solution)/shard_map/ppermute | solution.py:32
  40.6 15.0 %all_to_all.27 = bf16[32,32,384]{2,1,0:T(8,128)(2,1)S(1)} all-to-all(bf16[32,32,384]{2,1,0:T(8,128)(2,1)S(1)} %broadcast_in_dim.9), channel_id=1, replica_groups=mesh['y'=4,'x'=4,'w'=4,'v'=2,'c'=2] {'x','v','y'}, dimensions={0} | all-to-all | bytes 1572864 | tf_op jit(solution)/shard_map/all_to_all | solution.py:36
  55.6 10.1 %shard_map.43 = (bf16[1024,4096]{1,0:T(8,128)(2,1)}, f32[32,72,128]{2,1,0:T(8,128)S(1)}, f32[8,4096]{1,0:T(8,128)S(1)}) custom-call(bf16[1024,384]{1,0:T(8,128)(2,1)S(1)} %bitcast.27, bf16[1024,384]{1,0:T(8,128)(2,1)S(1)} %shard_map.41.a_ref, bf16[1024,384]{1,0:T(8,128)(2,1)S(1)} %shard_map.42.b_ref, bf16[1024,384]{1,0:T(8,128)(2,1)S(1)} %collective-permute-done.c_ref.a_ref, ...), custom_call_target="tpu_custom_call" | custom-call | flops 5368709120 | bytes 13369344 | tf_op jit(solution)/shard_map/pallas_call | solution.py:217
  66.7 4.6 %all-to-all-start.2 = ((f16[32,72,128]{2,1,0:T(8,128)(2,1)}), f16[32,72,128]{2,1,0:T(8,128)(2,1)}, u32[]{:S(2)}, u32[]{:S(2)}) async-start(f16[32,72,128]{2,1,0:T(8,128)(2,1)} %convert_element_type.42), calls=%async_computation.2 | async-start | bytes 1179648 | tf_op jit(solution)/shard_map/all_to_all | solution.py:36
  72.4 4.5 %shard_map.44 = f32[2048,256]{1,0:T(8,128)} custom-call(s32[1]{0:T(128)} %bitcast.5.core_ref, bf16[1024,4096]{1,0:T(8,128)(2,1)} %get-tuple-element.32.mix_ref, bf16[1024,384]{1,0:T(8,128)(2,1)S(1)} %bitcast.28, bf16[1024,384]{1,0:T(8,128)(2,1)S(1)} %collective-permute-done.c_ref.a_ref, bf16[1024,384]{1,0:T(8,128)(2,1)S(1)} %copy-done.2, ...), custom_call_target="tpu_custom_call" | custom-call | flops 1073741824 | bytes 8388608 | tf_op jit(solution)/shard_map/pallas_call | solution.py:260
  76.9 3.7 %all-to-all-done.2 = f16[32,72,128]{2,1,0:T(8,128)(2,1)} async-done(((f16[32,72,128]{2,1,0:T(8,128)(2,1)}), f16[32,72,128]{2,1,0:T(8,128)(2,1)}, u32[]{:S(2)}, u32[]{:S(2)}) %all-to-all-start.2) | async-done | bytes 589856 | tf_op jit(solution)/shard_map/all_to_all | solution.py:36
  80.6 5.4 %collective-permute-start.8 = (f32[2048,256]{1,0:T(8,128)}, f32[2048,256]{1,0:T(8,128)}, u32[]{:S(2)}, u32[]{:S(2)}) collective-permute-start(f32[2048,256]{1,0:T(8,128)} %shard_map.44), channel_id=1, source_target_pairs={{0,1},{1,0},{2,3},{3,2},{4,5},{5,4},{6,7},{7,6},{8,9},{9,8},{10,11... | collective-permute-start | bytes 6291464 | tf_op jit(solution)/shard_map/ppermute | solution.py:28
  85.9 1.1 bitcast_convert_fusion
  87.2 4.5 %collective-permute-start.5 = (f32[72,128]{1,0:T(8,128)S(1)}, f32[72,128]{1,0:T(8,128)S(1)}, u32[]{:S(2)}, u32[]{:S(2)}) collective-permute-start(f32[72,128]{1,0:T(8,128)S(1)} %maximum_bitcast_fusion.refs_0_), channel_id=1, source_target_pairs={{0,8},{4,12},{8,0},{12,4},{1,9},{5,13},{9,1},{13,5},{2,10},{6,14},... | collective-permute-start | bytes 110600 | tf_op jit(solution)/shard_map/ppermute | solution.py:32
  91.7 3.6 %collective-permute-start.7 = (f32[72,128]{1,0:T(8,128)S(1)}, f32[72,128]{1,0:T(8,128)S(1)}, u32[]{:S(2)}, u32[]{:S(2)}) collective-permute-start(f32[72,128]{1,0:T(8,128)S(1)} %maximum_bitcast_fusion.refs_0_), channel_id=1, source_target_pairs={{0,12},{4,0},{8,4},{12,8},{1,13},{5,1},{9,5},{13,9},{2,14},{6,2},{... | collective-permute-start | bytes 110600 | tf_op jit(solution)/shard_map/ppermute | solution.py:32
  95.3 1.4 %collective-permute-done.6.refs_2_ = f32[72,128]{1,0:T(8,128)S(1)} collective-permute-done((f32[72,128]{1,0:T(8,128)S(1)}, f32[72,128]{1,0:T(8,128)S(1)}, u32[]{:S(2)}, u32[]{:S(2)}) %collective-permute-start.6) | collective-permute-done | bytes 36896 | tf_op jit(solution)/shard_map/ppermute | solution.py:32
  97.5 3.9 %all-to-all-start.3 = ((f16[32,32,256]{2,1,0:T(8,128)(2,1)}), f16[32,32,256]{2,1,0:T(8,128)(2,1)S(1)}, u32[]{:S(2)}, u32[]{:S(2)}) async-start(f16[32,32,256]{2,1,0:T(8,128)(2,1)} %broadcast_in_dim.11), calls=%async_computation.3 | async-start | bytes 1048576 | tf_op jit(solution)/shard_map/all_to_all | solution.py:36
  101.4 2.3 %collective-permute-start.10 = (f32[8,256]{1,0:T(8,128)S(1)}, f32[8,256]{1,0:T(8,128)S(1)}, u32[]{:S(2)}, u32[]{:S(2)}) collective-permute-start(f32[8,256]{1,0:T(8,128)S(1)} %get-tuple-element.38), channel_id=1, source_target_pairs={{0,1},{1,0},{2,3},{3,2},{4,5},{5,4},{6,7},{7,6},{8,9},{9,8},{10,11... | collective-permute-start | bytes 24584 | tf_op jit(solution)/shard_map/ppermute | solution.py:28
  103.7 4.9 %shard_map.46 = f32[2048,256]{1,0:T(8,128)} custom-call(s32[1]{0:T(128)} %bitcast.5.core_ref, bf16[1024,4096]{1,0:T(8,128)(2,1)} %get-tuple-element.32.mix_ref, bf16[1024,384]{1,0:T(8,128)(2,1)S(1)} %bitcast.29, bf16[1024,384]{1,0:T(8,128)(2,1)S(1)} %shard_map.41.a_ref, bf16[1024,384]{1,0:T(8,128)(2,1)S(1)} %shard_map.42.b_ref, ...), custom_call_target="tpu_custom_call" | custom-call | flops 1073741824 | bytes 8388608 | tf_op jit(solution)/shard_map/pallas_call | solution.py:260
  108.6 1.9 %all-to-all-done.3 = f16[32,32,256]{2,1,0:T(8,128)(2,1)S(1)} async-done(((f16[32,32,256]{2,1,0:T(8,128)(2,1)}), f16[32,32,256]{2,1,0:T(8,128)(2,1)S(1)}, u32[]{:S(2)}, u32[]{:S(2)}) %all-to-all-start.3) | async-done | bytes 524320 | tf_op jit(solution)/shard_map/all_to_all | solution.py:36
  110.4 3.5 %collective-permute-start.9 = (f16[32,32,256]{2,1,0:T(8,128)(2,1)S(1)}, f16[32,32,256]{2,1,0:T(8,128)(2,1)S(1)}, u32[]{:S(2)}, u32[]{:S(2)}) collective-permute-start(f16[32,32,256]{2,1,0:T(8,128)(2,1)S(1)} %all-to-all-done.3), channel_id=1, source_target_pairs={{0,1},{1,0},{2,3},{3,2},{4,5},{5,4},{6,7},{7,6},{8,9},{9,8},{10,11... | collective-permute-start | bytes 1572872 | tf_op jit(solution)/shard_map/ppermute | solution.py:28
  (41 shorter events, 11.1 us)
Async XLA Ops:
  1.8 5.2 %collective-permute-start = (bf16[1024,384]{1,0:T(8,128)(2,1)S(1)}, bf16[1024,384]{1,0:T(8,128)(2,1)S(1)}, u32[]{:S(2)}, u32[]{:S(2)}) collective-permute-start(bf16[1024,384]{1,0:T(8,128)(2,1)S(1)} %shard_map.42.b_ref), channel_id=1, source_target_pairs={{0,1},{1,0},{2,3},{3,2},{4,5},{5,4},{6,7},{7,6},{8,9},{9,8},{10,11... | collective-permute-start | bytes 2359304 | tf_op jit(solution)/shard_map/ppermute | solution.py:28
  8.0 19.7 %all-to-all-start = ((bf16[32,32,384]{2,1,0:T(8,128)(2,1)}), bf16[32,32,384]{2,1,0:T(8,128)(2,1)}, u32[]{:S(2)}, u32[]{:S(2)}) async-start(bf16[32,32,384]{2,1,0:T(8,128)(2,1)} %bitcast.1), calls=%async_computation | async-start | bytes 1572864 | tf_op jit(solution)/shard_map/all_to_all | solution.py:36
  15.0 2.6 %collective-permute-start.4 = (bf16[1024,384]{1,0:T(8,128)(2,1)S(1)}, bf16[1024,384]{1,0:T(8,128)(2,1)S(1)}, u32[]{:S(2)}, u32[]{:S(2)}) collective-permute-start(bf16[1024,384]{1,0:T(8,128)(2,1)S(1)} %shard_map.41.a_ref), channel_id=1, source_target_pairs={{0,1},{1,0},{2,3},{3,2},{4,5},{5,4},{6,7},{7,6},{8,9},{9,8},{10,11... | collective-permute-start | bytes 2359304 | tf_op jit(solution)/shard_map/ppermute | solution.py:28
  17.9 0.9 copy-start
  27.7 27.8 %copy-start.1 = (bf16[1024,384]{1,0:T(8,128)(2,1)S(1)}, bf16[1024,384]{1,0:T(8,128)(2,1)}, u32[]{:S(2)}) copy-start(bf16[1024,384]{1,0:T(8,128)(2,1)} %copy-done) | copy-start | bytes 2359300
  28.6 9.7 %collective-permute-start.1 = (bf16[32,384]{1,0:T(8,128)(2,1)S(1)}, bf16[32,384]{1,0:T(8,128)(2,1)S(1)}, u32[]{:S(2)}, u32[]{:S(2)}) collective-permute-start(bf16[32,384]{1,0:T(8,128)(2,1)S(1)} %constant_dynamic-slice_fusion), channel_id=1, source_target_pairs={{0,4},{4,8},{8,12},{12,0},{1,5},{5,9},{9,13},{13,1},{2,6},{6,10},{... | collective-permute-start | bytes 73736 | tf_op jit(solution)/shard_map/ppermute | solution.py:32
  31.7 6.6 %collective-permute-start.2 = (bf16[32,384]{1,0:T(8,128)(2,1)S(1)}, bf16[32,384]{1,0:T(8,128)(2,1)S(1)}, u32[]{:S(2)}, u32[]{:S(2)}) collective-permute-start(bf16[32,384]{1,0:T(8,128)(2,1)S(1)} %constant_dynamic-slice_fusion), channel_id=1, source_target_pairs={{0,12},{4,0},{8,4},{12,8},{1,13},{5,1},{9,5},{13,9},{2,14},{6,2},{... | collective-permute-start | bytes 73736 | tf_op jit(solution)/shard_map/ppermute | solution.py:32
  33.9 6.6 %collective-permute-start.3 = (bf16[32,384]{1,0:T(8,128)(2,1)S(1)}, bf16[32,384]{1,0:T(8,128)(2,1)S(1)}, u32[]{:S(2)}, u32[]{:S(2)}) collective-permute-start(bf16[32,384]{1,0:T(8,128)(2,1)S(1)} %constant_dynamic-slice_fusion), channel_id=1, source_target_pairs={{0,8},{4,12},{8,0},{12,4},{1,9},{5,13},{9,1},{13,5},{2,10},{6,14},... | collective-permute-start | bytes 73736 | tf_op jit(solution)/shard_map/ppermute | solution.py:32
  66.7 13.9 %all-to-all-start.2 = ((f16[32,72,128]{2,1,0:T(8,128)(2,1)}), f16[32,72,128]{2,1,0:T(8,128)(2,1)}, u32[]{:S(2)}, u32[]{:S(2)}) async-start(f16[32,72,128]{2,1,0:T(8,128)(2,1)} %convert_element_type.42), calls=%async_computation.2 | async-start | bytes 1179648 | tf_op jit(solution)/shard_map/all_to_all | solution.py:36
  71.3 1.1 copy-start.2
  80.6 23.2 %collective-permute-start.8 = (f32[2048,256]{1,0:T(8,128)}, f32[2048,256]{1,0:T(8,128)}, u32[]{:S(2)}, u32[]{:S(2)}) collective-permute-start(f32[2048,256]{1,0:T(8,128)} %shard_map.44), channel_id=1, source_target_pairs={{0,1},{1,0},{2,3},{3,2},{4,5},{5,4},{6,7},{7,6},{8,9},{9,8},{10,11... | collective-permute-start | bytes 6291464 | tf_op jit(solution)/shard_map/ppermute | solution.py:28
  87.2 8.1 %collective-permute-start.5 = (f32[72,128]{1,0:T(8,128)S(1)}, f32[72,128]{1,0:T(8,128)S(1)}, u32[]{:S(2)}, u32[]{:S(2)}) collective-permute-start(f32[72,128]{1,0:T(8,128)S(1)} %maximum_bitcast_fusion.refs_0_), channel_id=1, source_target_pairs={{0,8},{4,12},{8,0},{12,4},{1,9},{5,13},{9,1},{13,5},{2,10},{6,14},... | collective-permute-start | bytes 110600 | tf_op jit(solution)/shard_map/ppermute | solution.py:32
  91.7 4.9 %collective-permute-start.6 = (f32[72,128]{1,0:T(8,128)S(1)}, f32[72,128]{1,0:T(8,128)S(1)}, u32[]{:S(2)}, u32[]{:S(2)}) collective-permute-start(f32[72,128]{1,0:T(8,128)S(1)} %maximum_bitcast_fusion.refs_0_), channel_id=1, source_target_pairs={{0,4},{4,8},{8,12},{12,0},{1,5},{5,9},{9,13},{13,1},{2,6},{6,10},{... | collective-permute-start | bytes 110600 | tf_op jit(solution)/shard_map/ppermute | solution.py:32
  91.7 4.9 %collective-permute-start.7 = (f32[72,128]{1,0:T(8,128)S(1)}, f32[72,128]{1,0:T(8,128)S(1)}, u32[]{:S(2)}, u32[]{:S(2)}) collective-permute-start(f32[72,128]{1,0:T(8,128)S(1)} %maximum_bitcast_fusion.refs_0_), channel_id=1, source_target_pairs={{0,12},{4,0},{8,4},{12,8},{1,13},{5,1},{9,5},{13,9},{2,14},{6,2},{... | collective-permute-start | bytes 110600 | tf_op jit(solution)/shard_map/ppermute | solution.py:32
  97.5 12.9 %all-to-all-start.3 = ((f16[32,32,256]{2,1,0:T(8,128)(2,1)}), f16[32,32,256]{2,1,0:T(8,128)(2,1)S(1)}, u32[]{:S(2)}, u32[]{:S(2)}) async-start(f16[32,32,256]{2,1,0:T(8,128)(2,1)} %broadcast_in_dim.11), calls=%async_computation.3 | async-start | bytes 1048576 | tf_op jit(solution)/shard_map/all_to_all | solution.py:36
  101.4 12.5 %collective-permute-start.10 = (f32[8,256]{1,0:T(8,128)S(1)}, f32[8,256]{1,0:T(8,128)S(1)}, u32[]{:S(2)}, u32[]{:S(2)}) collective-permute-start(f32[8,256]{1,0:T(8,128)S(1)} %get-tuple-element.38), channel_id=1, source_target_pairs={{0,1},{1,0},{2,3},{3,2},{4,5},{5,4},{6,7},{7,6},{8,9},{9,8},{10,11... | collective-permute-start | bytes 24584 | tf_op jit(solution)/shard_map/ppermute | solution.py:28
  110.4 5.1 %collective-permute-start.9 = (f16[32,32,256]{2,1,0:T(8,128)(2,1)S(1)}, f16[32,32,256]{2,1,0:T(8,128)(2,1)S(1)}, u32[]{:S(2)}, u32[]{:S(2)}) collective-permute-start(f16[32,32,256]{2,1,0:T(8,128)(2,1)S(1)} %all-to-all-done.3), channel_id=1, source_target_pairs={{0,1},{1,0},{2,3},{3,2},{4,5},{5,4},{6,7},{7,6},{8,9},{9,8},{10,11... | collective-permute-start | bytes 1572872 | tf_op jit(solution)/shard_map/ppermute | solution.py:28

commit v8 on v7

--- a/solution.py
+++ b/solution.py
@@ -230,7 +230,7 @@
         ],
         scratch_shapes=[pltpu.VMEM((rows, D), jnp.float32), pltpu.VMEM((rows, 1), jnp.float32), pltpu.VMEM((rows, 128), jnp.float32)],
         compiler_params=pltpu.CompilerParams(
-            vmem_limit_bytes=24 * 2**20, dimension_semantics=("arbitrary",)
+            vmem_limit_bytes=14 * 2**20, dimension_semantics=("arbitrary",)
         ),
         cost_estimate=pl.CostEstimate(
             flops=2 * rows * count * (WIDE + D),
@@ -274,7 +274,7 @@
         ),
         out_shape=pltpu.HBM((count, D), jnp.float32),
         compiler_params=pltpu.CompilerParams(
-            vmem_limit_bytes=24 * 2**20, dimension_semantics=("arbitrary",)
+            vmem_limit_bytes=14 * 2**20, dimension_semantics=("arbitrary",)
         ),
         cost_estimate=pl.CostEstimate(
             flops=2 * rows * count * D, bytes_accessed=2 * rows * count + 8 * count * D, transcendentals=0

time: 117 us -> 117 us (level)
  no operation moved by 1% of the time
where the time goes in v8:
time: 117 us
  starting transfers between devices  48.2 us (41%)
  Pallas kernels  22.8 us (19%)
  waiting for transfers between devices  20 us (17%)
  blocking collectives  15 us (13%)
  other arithmetic  5.19 us (4%)
  local copies, waits for them, and re-layouts  3.77 us (3%)
  between operations  1.58 us (1%)
    ppermute x6, starting transfers between devices, shift(): return lax.ppermute(v, 'w', [(i, (i + k) % NW) for i in range(NW)])  17.7 us
    all_to_all x3, starting transfers between devices, exchange(): return lax.all_to_all(v, PLANE, 0, 0, tiled=True)  15.3 us
    ppermute x5, starting transfers between devices, swap(): return lax.ppermute(v, 'c', [(0, 1), (1, 0)])  15.2 us
    all_to_all x1, blocking collectives, exchange(): return lax.all_to_all(v, PLANE, 0, 0, tiled=True)  15 us
    all_to_all x3, waiting for transfers between devices, exchange(): return lax.all_to_all(v, PLANE, 0, 0, tiled=True)  14.5 us
    pallas_call x1, Pallas kernels, mix(): pl.pallas_call(functools.partial(mix_kernel, steps=steps), grid=(steps,),...  10.1 us
    pallas_call x2, Pallas kernels, local_terms(): pl.pallas_call(functools.partial(local_kernel, scale=scale), grid_spec=pl...  9.34 us
    ppermute x6, waiting for transfers between devices, shift(): return lax.ppermute(v, 'w', [(i, (i + k) % NW) for i in range(NW)])  3.56 us
  transfers between devices with their start and end apart: 14, of which 7 were waited for; matrix products, arithmetic and copies ran while one was open for 3% of the time, Pallas kernels for 10%

profile of v8, /device:TPU:1, one launch (start us, length us, event | category | flops | bytes accessed | tf_op | source)
XLA Modules:
  0.0 116.6 jit_solution(4492457140931685924)
XLA Ops:
  0.6 1.2 shard_map.42.b_ref
  1.8 3.3 %collective-permute-start = (bf16[1024,384]{1,0:T(8,128)(2,1)S(1)}, bf16[1024,384]{1,0:T(8,128)(2,1)S(1)}, u32[]{:S(2)}, u32[]{:S(2)}) collective-permute-start(bf16[1024,384]{1,0:T(8,128)(2,1)S(1)} %shard_map.42.b_ref), channel_id=1, source_target_pairs={{0,1},{1,0},{2,3},{3,2},{4,5},{5,4},{6,7},{7,6},{8,9},{9,8},{10,11... | collective-permute-start | bytes 2359304 | tf_op jit(solution)/shard_map/ppermute | solution.py:28
  8.0 6.8 %all-to-all-start = ((bf16[32,32,384]{2,1,0:T(8,128)(2,1)}), bf16[32,32,384]{2,1,0:T(8,128)(2,1)}, u32[]{:S(2)}, u32[]{:S(2)}) async-start(bf16[32,32,384]{2,1,0:T(8,128)(2,1)} %bitcast.1), calls=%async_computation | async-start | bytes 1572864 | tf_op jit(solution)/shard_map/all_to_all | solution.py:36
  16.1 1.5 %collective-permute-done.4.d_ref.b_ref = bf16[1024,384]{1,0:T(8,128)(2,1)S(1)} collective-permute-done((bf16[1024,384]{1,0:T(8,128)(2,1)S(1)}, bf16[1024,384]{1,0:T(8,128)(2,1)S(1)}, u32[]{:S(2)}, u32[]{:S(2)}) %collective-permute-start.4) | collective-permute-done | bytes 786464 | tf_op jit(solution)/shard_map/ppermute | solution.py:28
  18.8 9.0 %all-to-all-done = bf16[32,32,384]{2,1,0:T(8,128)(2,1)} async-done(((bf16[32,32,384]{2,1,0:T(8,128)(2,1)}), bf16[32,32,384]{2,1,0:T(8,128)(2,1)}, u32[]{:S(2)}, u32[]{:S(2)}) %all-to-all-start) | async-done | bytes 786464 | tf_op jit(solution)/shard_map/all_to_all | solution.py:36
  28.6 3.1 %collective-permute-start.1 = (bf16[32,384]{1,0:T(8,128)(2,1)S(1)}, bf16[32,384]{1,0:T(8,128)(2,1)S(1)}, u32[]{:S(2)}, u32[]{:S(2)}) collective-permute-start(bf16[32,384]{1,0:T(8,128)(2,1)S(1)} %constant_dynamic-slice_fusion), channel_id=1, source_target_pairs={{0,4},{4,8},{8,12},{12,0},{1,5},{5,9},{9,13},{13,1},{2,6},{6,10},{... | collective-permute-start | bytes 73736 | tf_op jit(solution)/shard_map/ppermute | solution.py:32
  31.7 2.2 %collective-permute-start.2 = (bf16[32,384]{1,0:T(8,128)(2,1)S(1)}, bf16[32,384]{1,0:T(8,128)(2,1)S(1)}, u32[]{:S(2)}, u32[]{:S(2)}) collective-permute-start(bf16[32,384]{1,0:T(8,128)(2,1)S(1)} %constant_dynamic-slice_fusion), channel_id=1, source_target_pairs={{0,12},{4,0},{8,4},{12,8},{1,13},{5,1},{9,5},{13,9},{2,14},{6,2},{... | collective-permute-start | bytes 73736 | tf_op jit(solution)/shard_map/ppermute | solution.py:32
  33.9 4.4 %collective-permute-start.3 = (bf16[32,384]{1,0:T(8,128)(2,1)S(1)}, bf16[32,384]{1,0:T(8,128)(2,1)S(1)}, u32[]{:S(2)}, u32[]{:S(2)}) collective-permute-start(bf16[32,384]{1,0:T(8,128)(2,1)S(1)} %constant_dynamic-slice_fusion), channel_id=1, source_target_pairs={{0,8},{4,12},{8,0},{12,4},{1,9},{5,13},{9,1},{13,5},{2,10},{6,14},... | collective-permute-start | bytes 73736 | tf_op jit(solution)/shard_map/ppermute | solution.py:32
  38.3 2.2 %collective-permute-done.3 = bf16[32,384]{1,0:T(8,128)(2,1)S(1)} collective-permute-done((bf16[32,384]{1,0:T(8,128)(2,1)S(1)}, bf16[32,384]{1,0:T(8,128)(2,1)S(1)}, u32[]{:S(2)}, u32[]{:S(2)}) %collective-permute-start.3) | collective-permute-done | bytes 24608 | tf_op jit(solution)/shard_map/ppermute | solution.py:32
  40.6 15.0 %all_to_all.27 = bf16[32,32,384]{2,1,0:T(8,128)(2,1)S(1)} all-to-all(bf16[32,32,384]{2,1,0:T(8,128)(2,1)S(1)} %broadcast_in_dim.9), channel_id=1, replica_groups=mesh['y'=4,'x'=4,'w'=4,'v'=2,'c'=2] {'x','v','y'}, dimensions={0} | all-to-all | bytes 1572864 | tf_op jit(solution)/shard_map/all_to_all | solution.py:36
  55.6 10.1 %shard_map.43 = (bf16[1024,4096]{1,0:T(8,128)(2,1)}, f32[32,72,128]{2,1,0:T(8,128)S(1)}, f32[8,4096]{1,0:T(8,128)S(1)}) custom-call(bf16[1024,384]{1,0:T(8,128)(2,1)S(1)} %bitcast.27, bf16[1024,384]{1,0:T(8,128)(2,1)S(1)} %shard_map.41.a_ref, bf16[1024,384]{1,0:T(8,128)(2,1)S(1)} %shard_map.42.b_ref, bf16[1024,384]{1,0:T(8,128)(2,1)S(1)} %collective-permute-done.c_ref.a_ref, ...), custom_call_target="tpu_custom_call" | custom-call | flops 5368709120 | bytes 13369344 | tf_op jit(solution)/shard_map/pallas_call | solution.py:217
  66.7 4.6 %all-to-all-start.2 = ((f16[32,72,128]{2,1,0:T(8,128)(2,1)}), f16[32,72,128]{2,1,0:T(8,128)(2,1)}, u32[]{:S(2)}, u32[]{:S(2)}) async-start(f16[32,72,128]{2,1,0:T(8,128)(2,1)} %convert_element_type.42), calls=%async_computation.2 | async-start | bytes 1179648 | tf_op jit(solution)/shard_map/all_to_all | solution.py:36
  72.4 4.5 %shard_map.44 = f32[2048,256]{1,0:T(8,128)} custom-call(s32[1]{0:T(128)} %bitcast.5.core_ref, bf16[1024,4096]{1,0:T(8,128)(2,1)} %get-tuple-element.32.mix_ref, bf16[1024,384]{1,0:T(8,128)(2,1)S(1)} %bitcast.28, bf16[1024,384]{1,0:T(8,128)(2,1)S(1)} %collective-permute-done.c_ref.a_ref, bf16[1024,384]{1,0:T(8,128)(2,1)S(1)} %copy-done.2, ...), custom_call_target="tpu_custom_call" | custom-call | flops 1073741824 | bytes 8388608 | tf_op jit(solution)/shard_map/pallas_call | solution.py:260
  76.9 3.7 %all-to-all-done.2 = f16[32,72,128]{2,1,0:T(8,128)(2,1)} async-done(((f16[32,72,128]{2,1,0:T(8,128)(2,1)}), f16[32,72,128]{2,1,0:T(8,128)(2,1)}, u32[]{:S(2)}, u32[]{:S(2)}) %all-to-all-start.2) | async-done | bytes 589856 | tf_op jit(solution)/shard_map/all_to_all | solution.py:36
  80.6 5.4 %collective-permute-start.8 = (f32[2048,256]{1,0:T(8,128)}, f32[2048,256]{1,0:T(8,128)}, u32[]{:S(2)}, u32[]{:S(2)}) collective-permute-start(f32[2048,256]{1,0:T(8,128)} %shard_map.44), channel_id=1, source_target_pairs={{0,1},{1,0},{2,3},{3,2},{4,5},{5,4},{6,7},{7,6},{8,9},{9,8},{10,11... | collective-permute-start | bytes 6291464 | tf_op jit(solution)/shard_map/ppermute | solution.py:28
  85.9 1.1 bitcast_convert_fusion
  87.2 4.5 %collective-permute-start.5 = (f32[72,128]{1,0:T(8,128)S(1)}, f32[72,128]{1,0:T(8,128)S(1)}, u32[]{:S(2)}, u32[]{:S(2)}) collective-permute-start(f32[72,128]{1,0:T(8,128)S(1)} %maximum_bitcast_fusion.refs_0_), channel_id=1, source_target_pairs={{0,8},{4,12},{8,0},{12,4},{1,9},{5,13},{9,1},{13,5},{2,10},{6,14},... | collective-permute-start | bytes 110600 | tf_op jit(solution)/shard_map/ppermute | solution.py:32
  91.7 3.6 %collective-permute-start.7 = (f32[72,128]{1,0:T(8,128)S(1)}, f32[72,128]{1,0:T(8,128)S(1)}, u32[]{:S(2)}, u32[]{:S(2)}) collective-permute-start(f32[72,128]{1,0:T(8,128)S(1)} %maximum_bitcast_fusion.refs_0_), channel_id=1, source_target_pairs={{0,12},{4,0},{8,4},{12,8},{1,13},{5,1},{9,5},{13,9},{2,14},{6,2},{... | collective-permute-start | bytes 110600 | tf_op jit(solution)/shard_map/ppermute | solution.py:32
  95.3 1.4 %collective-permute-done.6.refs_2_ = f32[72,128]{1,0:T(8,128)S(1)} collective-permute-done((f32[72,128]{1,0:T(8,128)S(1)}, f32[72,128]{1,0:T(8,128)S(1)}, u32[]{:S(2)}, u32[]{:S(2)}) %collective-permute-start.6) | collective-permute-done | bytes 36896 | tf_op jit(solution)/shard_map/ppermute | solution.py:32
  97.5 3.9 %all-to-all-start.3 = ((f16[32,32,256]{2,1,0:T(8,128)(2,1)}), f16[32,32,256]{2,1,0:T(8,128)(2,1)S(1)}, u32[]{:S(2)}, u32[]{:S(2)}) async-start(f16[32,32,256]{2,1,0:T(8,128)(2,1)} %broadcast_in_dim.11), calls=%async_computation.3 | async-start | bytes 1048576 | tf_op jit(solution)/shard_map/all_to_all | solution.py:36
  101.4 2.3 %collective-permute-start.10 = (f32[8,256]{1,0:T(8,128)S(1)}, f32[8,256]{1,0:T(8,128)S(1)}, u32[]{:S(2)}, u32[]{:S(2)}) collective-permute-start(f32[8,256]{1,0:T(8,128)S(1)} %get-tuple-element.38), channel_id=1, source_target_pairs={{0,1},{1,0},{2,3},{3,2},{4,5},{5,4},{6,7},{7,6},{8,9},{9,8},{10,11... | collective-permute-start | bytes 24584 | tf_op jit(solution)/shard_map/ppermute | solution.py:28
  103.7 4.9 %shard_map.46 = f32[2048,256]{1,0:T(8,128)} custom-call(s32[1]{0:T(128)} %bitcast.5.core_ref, bf16[1024,4096]{1,0:T(8,128)(2,1)} %get-tuple-element.32.mix_ref, bf16[1024,384]{1,0:T(8,128)(2,1)S(1)} %bitcast.29, bf16[1024,384]{1,0:T(8,128)(2,1)S(1)} %shard_map.41.a_ref, bf16[1024,384]{1,0:T(8,128)(2,1)S(1)} %shard_map.42.b_ref, ...), custom_call_target="tpu_custom_call" | custom-call | flops 1073741824 | bytes 8388608 | tf_op jit(solution)/shard_map/pallas_call | solution.py:260
  108.6 1.9 %all-to-all-done.3 = f16[32,32,256]{2,1,0:T(8,128)(2,1)S(1)} async-done(((f16[32,32,256]{2,1,0:T(8,128)(2,1)}), f16[32,32,256]{2,1,0:T(8,128)(2,1)S(1)}, u32[]{:S(2)}, u32[]{:S(2)}) %all-to-all-start.3) | async-done | bytes 524320 | tf_op jit(solution)/shard_map/all_to_all | solution.py:36
  110.4 3.5 %collective-permute-start.9 = (f16[32,32,256]{2,1,0:T(8,128)(2,1)S(1)}, f16[32,32,256]{2,1,0:T(8,128)(2,1)S(1)}, u32[]{:S(2)}, u32[]{:S(2)}) collective-permute-start(f16[32,32,256]{2,1,0:T(8,128)(2,1)S(1)} %all-to-all-done.3), channel_id=1, source_target_pairs={{0,1},{1,0},{2,3},{3,2},{4,5},{5,4},{6,7},{7,6},{8,9},{9,8},{10,11... | collective-permute-start | bytes 1572872 | tf_op jit(solution)/shard_map/ppermute | solution.py:28
  (41 shorter events, 11.1 us)
Async XLA Ops:
  1.8 5.2 %collective-permute-start = (bf16[1024,384]{1,0:T(8,128)(2,1)S(1)}, bf16[1024,384]{1,0:T(8,128)(2,1)S(1)}, u32[]{:S(2)}, u32[]{:S(2)}) collective-permute-start(bf16[1024,384]{1,0:T(8,128)(2,1)S(1)} %shard_map.42.b_ref), channel_id=1, source_target_pairs={{0,1},{1,0},{2,3},{3,2},{4,5},{5,4},{6,7},{7,6},{8,9},{9,8},{10,11... | collective-permute-start | bytes 2359304 | tf_op jit(solution)/shard_map/ppermute | solution.py:28
  8.0 19.7 %all-to-all-start = ((bf16[32,32,384]{2,1,0:T(8,128)(2,1)}), bf16[32,32,384]{2,1,0:T(8,128)(2,1)}, u32[]{:S(2)}, u32[]{:S(2)}) async-start(bf16[32,32,384]{2,1,0:T(8,128)(2,1)} %bitcast.1), calls=%async_computation | async-start | bytes 1572864 | tf_op jit(solution)/shard_map/all_to_all | solution.py:36
  15.0 2.6 %collective-permute-start.4 = (bf16[1024,384]{1,0:T(8,128)(2,1)S(1)}, bf16[1024,384]{1,0:T(8,128)(2,1)S(1)}, u32[]{:S(2)}, u32[]{:S(2)}) collective-permute-start(bf16[1024,384]{1,0:T(8,128)(2,1)S(1)} %shard_map.41.a_ref), channel_id=1, source_target_pairs={{0,1},{1,0},{2,3},{3,2},{4,5},{5,4},{6,7},{7,6},{8,9},{9,8},{10,11... | collective-permute-start | bytes 2359304 | tf_op jit(solution)/shard_map/ppermute | solution.py:28
  17.9 0.9 copy-start
  27.7 27.8 %copy-start.1 = (bf16[1024,384]{1,0:T(8,128)(2,1)S(1)}, bf16[1024,384]{1,0:T(8,128)(2,1)}, u32[]{:S(2)}) copy-start(bf16[1024,384]{1,0:T(8,128)(2,1)} %copy-done) | copy-start | bytes 2359300
  28.6 9.7 %collective-permute-start.1 = (bf16[32,384]{1,0:T(8,128)(2,1)S(1)}, bf16[32,384]{1,0:T(8,128)(2,1)S(1)}, u32[]{:S(2)}, u32[]{:S(2)}) collective-permute-start(bf16[32,384]{1,0:T(8,128)(2,1)S(1)} %constant_dynamic-slice_fusion), channel_id=1, source_target_pairs={{0,4},{4,8},{8,12},{12,0},{1,5},{5,9},{9,13},{13,1},{2,6},{6,10},{... | collective-permute-start | bytes 73736 | tf_op jit(solution)/shard_map/ppermute | solution.py:32
  31.7 6.6 %collective-permute-start.2 = (bf16[32,384]{1,0:T(8,128)(2,1)S(1)}, bf16[32,384]{1,0:T(8,128)(2,1)S(1)}, u32[]{:S(2)}, u32[]{:S(2)}) collective-permute-start(bf16[32,384]{1,0:T(8,128)(2,1)S(1)} %constant_dynamic-slice_fusion), channel_id=1, source_target_pairs={{0,12},{4,0},{8,4},{12,8},{1,13},{5,1},{9,5},{13,9},{2,14},{6,2},{... | collective-permute-start | bytes 73736 | tf_op jit(solution)/shard_map/ppermute | solution.py:32
  33.9 6.6 %collective-permute-start.3 = (bf16[32,384]{1,0:T(8,128)(2,1)S(1)}, bf16[32,384]{1,0:T(8,128)(2,1)S(1)}, u32[]{:S(2)}, u32[]{:S(2)}) collective-permute-start(bf16[32,384]{1,0:T(8,128)(2,1)S(1)} %constant_dynamic-slice_fusion), channel_id=1, source_target_pairs={{0,8},{4,12},{8,0},{12,4},{1,9},{5,13},{9,1},{13,5},{2,10},{6,14},... | collective-permute-start | bytes 73736 | tf_op jit(solution)/shard_map/ppermute | solution.py:32
  66.7 13.9 %all-to-all-start.2 = ((f16[32,72,128]{2,1,0:T(8,128)(2,1)}), f16[32,72,128]{2,1,0:T(8,128)(2,1)}, u32[]{:S(2)}, u32[]{:S(2)}) async-start(f16[32,72,128]{2,1,0:T(8,128)(2,1)} %convert_element_type.42), calls=%async_computation.2 | async-start | bytes 1179648 | tf_op jit(solution)/shard_map/all_to_all | solution.py:36
  71.3 1.1 copy-start.2
  80.6 23.2 %collective-permute-start.8 = (f32[2048,256]{1,0:T(8,128)}, f32[2048,256]{1,0:T(8,128)}, u32[]{:S(2)}, u32[]{:S(2)}) collective-permute-start(f32[2048,256]{1,0:T(8,128)} %shard_map.44), channel_id=1, source_target_pairs={{0,1},{1,0},{2,3},{3,2},{4,5},{5,4},{6,7},{7,6},{8,9},{9,8},{10,11... | collective-permute-start | bytes 6291464 | tf_op jit(solution)/shard_map/ppermute | solution.py:28
  87.2 8.1 %collective-permute-start.5 = (f32[72,128]{1,0:T(8,128)S(1)}, f32[72,128]{1,0:T(8,128)S(1)}, u32[]{:S(2)}, u32[]{:S(2)}) collective-permute-start(f32[72,128]{1,0:T(8,128)S(1)} %maximum_bitcast_fusion.refs_0_), channel_id=1, source_target_pairs={{0,8},{4,12},{8,0},{12,4},{1,9},{5,13},{9,1},{13,5},{2,10},{6,14},... | collective-permute-start | bytes 110600 | tf_op jit(solution)/shard_map/ppermute | solution.py:32
  91.7 4.9 %collective-permute-start.6 = (f32[72,128]{1,0:T(8,128)S(1)}, f32[72,128]{1,0:T(8,128)S(1)}, u32[]{:S(2)}, u32[]{:S(2)}) collective-permute-start(f32[72,128]{1,0:T(8,128)S(1)} %maximum_bitcast_fusion.refs_0_), channel_id=1, source_target_pairs={{0,4},{4,8},{8,12},{12,0},{1,5},{5,9},{9,13},{13,1},{2,6},{6,10},{... | collective-permute-start | bytes 110600 | tf_op jit(solution)/shard_map/ppermute | solution.py:32
  91.7 4.9 %collective-permute-start.7 = (f32[72,128]{1,0:T(8,128)S(1)}, f32[72,128]{1,0:T(8,128)S(1)}, u32[]{:S(2)}, u32[]{:S(2)}) collective-permute-start(f32[72,128]{1,0:T(8,128)S(1)} %maximum_bitcast_fusion.refs_0_), channel_id=1, source_target_pairs={{0,12},{4,0},{8,4},{12,8},{1,13},{5,1},{9,5},{13,9},{2,14},{6,2},{... | collective-permute-start | bytes 110600 | tf_op jit(solution)/shard_map/ppermute | solution.py:32
  97.5 12.9 %all-to-all-start.3 = ((f16[32,32,256]{2,1,0:T(8,128)(2,1)}), f16[32,32,256]{2,1,0:T(8,128)(2,1)S(1)}, u32[]{:S(2)}, u32[]{:S(2)}) async-start(f16[32,32,256]{2,1,0:T(8,128)(2,1)} %broadcast_in_dim.11), calls=%async_computation.3 | async-start | bytes 1048576 | tf_op jit(solution)/shard_map/all_to_all | solution.py:36
  101.4 12.5 %collective-permute-start.10 = (f32[8,256]{1,0:T(8,128)S(1)}, f32[8,256]{1,0:T(8,128)S(1)}, u32[]{:S(2)}, u32[]{:S(2)}) collective-permute-start(f32[8,256]{1,0:T(8,128)S(1)} %get-tuple-element.38), channel_id=1, source_target_pairs={{0,1},{1,0},{2,3},{3,2},{4,5},{5,4},{6,7},{7,6},{8,9},{9,8},{10,11... | collective-permute-start | bytes 24584 | tf_op jit(solution)/shard_map/ppermute | solution.py:28
  110.4 5.1 %collective-permute-start.9 = (f16[32,32,256]{2,1,0:T(8,128)(2,1)S(1)}, f16[32,32,256]{2,1,0:T(8,128)(2,1)S(1)}, u32[]{:S(2)}, u32[]{:S(2)}) collective-permute-start(f16[32,32,256]{2,1,0:T(8,128)(2,1)S(1)} %all-to-all-done.3), channel_id=1, source_target_pairs={{0,1},{1,0},{2,3},{3,2},{4,5},{5,4},{6,7},{7,6},{8,9},{9,8},{10,11... | collective-permute-start | bytes 1572872 | tf_op jit(solution)/shard_map/ppermute | solution.py:28

commit v9 on v8

--- a/solution.py
+++ b/solution.py
@@ -94,8 +94,8 @@
     start = start * (here.shape[0] // NP)
     here, other, level, start = tie(here, swap(there), level, start)
     half = jnp.where(owner % NC == lax.axis_index("c"), here, other)
-    (piece,) = tie(pick(exchange(half), NP, start))
-    parts = (here, there, other, swap(here))
+    piece, late = tie(pick(exchange(half), NP, start), here)
+    parts = (here, there, other, swap(late))
     piece = along_w(piece, level // NV)
     squares = jnp.concatenate([squared(part) for part in parts])[None, :]
     piece, squares, *parts = tie(piece, squares, *parts)

time: 117 us -> 120 us (1.026)
  waiting for transfers between devices: 20 us -> 22.4 us
  blocking collectives: 15 us -> 16.3 us
    all_to_all x3, waiting for transfers between devices: 14.5 us -> 18.4 us  [exchange(): return lax.all_to_all(v, PLANE, 0, 0, tiled=True)]
    ppermute x5, waiting for transfers between devices: 1.94 us -> 0.41 us  [swap(): return lax.ppermute(v, 'c', [(0, 1), (1, 0)])]
    all_to_all x1, blocking collectives: 15 us -> 16.3 us  [exchange(): return lax.all_to_all(v, PLANE, 0, 0, tiled=True)]
  transfers between devices with their start and end apart: 14 -> 14, of which waited for: 7 -> 6; matrix products, arithmetic and copies ran while one was open for 3% -> 2% of each run, Pallas kernels for 10% -> 10%
where the time goes in v9:
time: 120 us; the launch traced here: 119 us
  starting transfers between devices  47.8 us (40%)
  Pallas kernels  22.8 us (19%)
  waiting for transfers between devices  22.4 us (19%)
  blocking collectives  16.3 us (14%)
  other arithmetic  5.13 us (4%)
  local copies, waits for them, and re-layouts  2.95 us (2%)
  between operations  1.59 us (1%)
    all_to_all x3, waiting for transfers between devices, exchange(): return lax.all_to_all(v, PLANE, 0, 0, tiled=True)  18.4 us
    ppermute x6, starting transfers between devices, shift(): return lax.ppermute(v, 'w', [(i, (i + k) % NW) for i in range(NW)])  17.7 us
    all_to_all x1, blocking collectives, exchange(): return lax.all_to_all(v, PLANE, 0, 0, tiled=True)  16.3 us
    all_to_all x3, starting transfers between devices, exchange(): return lax.all_to_all(v, PLANE, 0, 0, tiled=True)  15.4 us
    ppermute x5, starting transfers between devices, swap(): return lax.ppermute(v, 'c', [(0, 1), (1, 0)])  14.7 us
    pallas_call x1, Pallas kernels, mix(): pl.pallas_call(functools.partial(mix_kernel, steps=steps), grid=(steps,),...  10.1 us
    pallas_call x2, Pallas kernels, local_terms(): pl.pallas_call(functools.partial(local_kernel, scale=scale), grid_spec=pl...  9.34 us
    ppermute x6, waiting for transfers between devices, shift(): return lax.ppermute(v, 'w', [(i, (i + k) % NW) for i in range(NW)])  3.59 us
  transfers between devices with their start and end apart: 14, of which 6 were waited for; matrix products, arithmetic and copies ran while one was open for 2% of the time, Pallas kernels for 10%

profile of v9, /device:TPU:1, one launch (start us, length us, event | category | flops | bytes accessed | tf_op | source)
XLA Modules:
  0.0 118.9 jit_solution(2531656296406013181)
XLA Ops:
  0.6 1.2 shard_map.42.b_ref
  1.8 3.3 %collective-permute-start = (bf16[1024,384]{1,0:T(8,128)(2,1)S(1)}, bf16[1024,384]{1,0:T(8,128)(2,1)S(1)}, u32[]{:S(2)}, u32[]{:S(2)}) collective-permute-start(bf16[1024,384]{1,0:T(8,128)(2,1)S(1)} %shard_map.42.b_ref), channel_id=1, source_target_pairs={{0,1},{1,0},{2,3},{3,2},{4,5},{5,4},{6,7},{7,6},{8,9},{9,8},{10,11... | collective-permute-start | bytes 2359304 | tf_op jit(solution)/shard_map/ppermute | solution.py:28
  8.0 6.7 %all-to-all-start = ((bf16[32,32,384]{2,1,0:T(8,128)(2,1)}), bf16[32,32,384]{2,1,0:T(8,128)(2,1)S(1)}, u32[]{:S(2)}, u32[]{:S(2)}) async-start(bf16[32,32,384]{2,1,0:T(8,128)(2,1)} %bitcast.1), calls=%async_computation | async-start | bytes 1572864 | tf_op jit(solution)/shard_map/all_to_all | solution.py:36
  14.9 12.7 %all-to-all-done = bf16[32,32,384]{2,1,0:T(8,128)(2,1)S(1)} async-done(((bf16[32,32,384]{2,1,0:T(8,128)(2,1)}), bf16[32,32,384]{2,1,0:T(8,128)(2,1)S(1)}, u32[]{:S(2)}, u32[]{:S(2)}) %all-to-all-start) | async-done | bytes 786464 | tf_op jit(solution)/shard_map/all_to_all | solution.py:36
  27.7 1.6 %collective-permute-start.4 = (bf16[1024,384]{1,0:T(8,128)(2,1)S(1)}, bf16[1024,384]{1,0:T(8,128)(2,1)S(1)}, u32[]{:S(2)}, u32[]{:S(2)}) collective-permute-start(bf16[1024,384]{1,0:T(8,128)(2,1)S(1)} %shard_map.41.a_ref), channel_id=1, source_target_pairs={{0,1},{1,0},{2,3},{3,2},{4,5},{5,4},{6,7},{7,6},{8,9},{9,8},{10,11... | collective-permute-start | bytes 2359304 | tf_op jit(solution)/shard_map/ppermute | solution.py:28
  29.6 3.1 %collective-permute-start.1 = (bf16[32,384]{1,0:T(8,128)(2,1)S(1)}, bf16[32,384]{1,0:T(8,128)(2,1)S(1)}, u32[]{:S(2)}, u32[]{:S(2)}) collective-permute-start(bf16[32,384]{1,0:T(8,128)(2,1)S(1)} %constant_dynamic-slice_fusion), channel_id=1, source_target_pairs={{0,4},{4,8},{8,12},{12,0},{1,5},{5,9},{9,13},{13,1},{2,6},{6,10},{... | collective-permute-start | bytes 73736 | tf_op jit(solution)/shard_map/ppermute | solution.py:32
  32.7 2.2 %collective-permute-start.2 = (bf16[32,384]{1,0:T(8,128)(2,1)S(1)}, bf16[32,384]{1,0:T(8,128)(2,1)S(1)}, u32[]{:S(2)}, u32[]{:S(2)}) collective-permute-start(bf16[32,384]{1,0:T(8,128)(2,1)S(1)} %constant_dynamic-slice_fusion), channel_id=1, source_target_pairs={{0,12},{4,0},{8,4},{12,8},{1,13},{5,1},{9,5},{13,9},{2,14},{6,2},{... | collective-permute-start | bytes 73736 | tf_op jit(solution)/shard_map/ppermute | solution.py:32
  34.9 4.4 %collective-permute-start.3 = (bf16[32,384]{1,0:T(8,128)(2,1)S(1)}, bf16[32,384]{1,0:T(8,128)(2,1)S(1)}, u32[]{:S(2)}, u32[]{:S(2)}) collective-permute-start(bf16[32,384]{1,0:T(8,128)(2,1)S(1)} %constant_dynamic-slice_fusion), channel_id=1, source_target_pairs={{0,8},{4,12},{8,0},{12,4},{1,9},{5,13},{9,1},{13,5},{2,10},{6,14},... | collective-permute-start | bytes 73736 | tf_op jit(solution)/shard_map/ppermute | solution.py:32
  39.3 2.2 %collective-permute-done.3 = bf16[32,384]{1,0:T(8,128)(2,1)S(1)} collective-permute-done((bf16[32,384]{1,0:T(8,128)(2,1)S(1)}, bf16[32,384]{1,0:T(8,128)(2,1)S(1)}, u32[]{:S(2)}, u32[]{:S(2)}) %collective-permute-start.3) | collective-permute-done | bytes 24608 | tf_op jit(solution)/shard_map/ppermute | solution.py:32
  42.7 16.3 %all_to_all.27 = bf16[32,32,384]{2,1,0:T(8,128)(2,1)S(1)} all-to-all(bf16[32,32,384]{2,1,0:T(8,128)(2,1)S(1)} %broadcast_in_dim.9), channel_id=1, replica_groups=mesh['y'=4,'x'=4,'w'=4,'v'=2,'c'=2] {'x','v','y'}, dimensions={0} | all-to-all | bytes 1572864 | tf_op jit(solution)/shard_map/all_to_all | solution.py:36
  59.0 10.1 %shard_map.43 = (bf16[1024,4096]{1,0:T(8,128)(2,1)}, f32[32,72,128]{2,1,0:T(8,128)S(1)}, f32[8,4096]{1,0:T(8,128)S(1)}) custom-call(bf16[1024,384]{1,0:T(8,128)(2,1)S(1)} %bitcast.27, bf16[1024,384]{1,0:T(8,128)(2,1)S(1)} %shard_map.41.a_ref, bf16[1024,384]{1,0:T(8,128)(2,1)S(1)} %shard_map.42.b_ref, bf16[1024,384]{1,0:T(8,128)(2,1)S(1)} %collective-permute-done.c_ref.a_ref, ...), custom_call_target="tpu_custom_call" | custom-call | flops 5368709120 | bytes 13369344 | tf_op jit(solution)/shard_map/pallas_call | solution.py:217
  70.0 4.8 %all-to-all-start.2 = ((f16[32,72,128]{2,1,0:T(8,128)(2,1)}), f16[32,72,128]{2,1,0:T(8,128)(2,1)}, u32[]{:S(2)}, u32[]{:S(2)}) async-start(f16[32,72,128]{2,1,0:T(8,128)(2,1)} %convert_element_type.42), calls=%async_computation.2 | async-start | bytes 1179648 | tf_op jit(solution)/shard_map/all_to_all | solution.py:36
  76.0 4.5 %shard_map.44 = f32[2048,256]{1,0:T(8,128)} custom-call(s32[1]{0:T(128)} %bitcast.5.core_ref, bf16[1024,4096]{1,0:T(8,128)(2,1)} %get-tuple-element.36.mix_ref, bf16[1024,384]{1,0:T(8,128)(2,1)S(1)} %bitcast.28, bf16[1024,384]{1,0:T(8,128)(2,1)S(1)} %collective-permute-done.c_ref.a_ref, bf16[1024,384]{1,0:T(8,128)(2,1)S(1)} %copy-done.2, ...), custom_call_target="tpu_custom_call" | custom-call | flops 1073741824 | bytes 8388608 | tf_op jit(solution)/shard_map/pallas_call | solution.py:260
  80.5 3.7 %all-to-all-done.2 = f16[32,72,128]{2,1,0:T(8,128)(2,1)} async-done(((f16[32,72,128]{2,1,0:T(8,128)(2,1)}), f16[32,72,128]{2,1,0:T(8,128)(2,1)}, u32[]{:S(2)}, u32[]{:S(2)}) %all-to-all-start.2) | async-done | bytes 589856 | tf_op jit(solution)/shard_map/all_to_all | solution.py:36
  84.2 4.1 %collective-permute-start.8 = (f32[2048,256]{1,0:T(8,128)}, f32[2048,256]{1,0:T(8,128)}, u32[]{:S(2)}, u32[]{:S(2)}) collective-permute-start(f32[2048,256]{1,0:T(8,128)} %shard_map.44), channel_id=1, source_target_pairs={{0,1},{1,0},{2,3},{3,2},{4,5},{5,4},{6,7},{7,6},{8,9},{9,8},{10,11... | collective-permute-start | bytes 6291464 | tf_op jit(solution)/shard_map/ppermute | solution.py:28
  88.3 1.1 bitcast_convert_fusion
  89.6 4.5 %collective-permute-start.5 = (f32[72,128]{1,0:T(8,128)S(1)}, f32[72,128]{1,0:T(8,128)S(1)}, u32[]{:S(2)}, u32[]{:S(2)}) collective-permute-start(f32[72,128]{1,0:T(8,128)S(1)} %maximum_bitcast_fusion.refs_0_), channel_id=1, source_target_pairs={{0,8},{4,12},{8,0},{12,4},{1,9},{5,13},{9,1},{13,5},{2,10},{6,14},... | collective-permute-start | bytes 110600 | tf_op jit(solution)/shard_map/ppermute | solution.py:32
  94.1 3.6 %collective-permute-start.7 = (f32[72,128]{1,0:T(8,128)S(1)}, f32[72,128]{1,0:T(8,128)S(1)}, u32[]{:S(2)}, u32[]{:S(2)}) collective-permute-start(f32[72,128]{1,0:T(8,128)S(1)} %maximum_bitcast_fusion.refs_0_), channel_id=1, source_target_pairs={{0,12},{4,0},{8,4},{12,8},{1,13},{5,1},{9,5},{13,9},{2,14},{6,2},{... | collective-permute-start | bytes 110600 | tf_op jit(solution)/shard_map/ppermute | solution.py:32
  97.7 1.4 %collective-permute-done.6.refs_2_ = f32[72,128]{1,0:T(8,128)S(1)} collective-permute-done((f32[72,128]{1,0:T(8,128)S(1)}, f32[72,128]{1,0:T(8,128)S(1)}, u32[]{:S(2)}, u32[]{:S(2)}) %collective-permute-start.6) | collective-permute-done | bytes 36896 | tf_op jit(solution)/shard_map/ppermute | solution.py:32
  99.9 3.9 %all-to-all-start.3 = ((f16[32,32,256]{2,1,0:T(8,128)(2,1)}), f16[32,32,256]{2,1,0:T(8,128)(2,1)S(1)}, u32[]{:S(2)}, u32[]{:S(2)}) async-start(f16[32,32,256]{2,1,0:T(8,128)(2,1)} %broadcast_in_dim.11), calls=%async_computation.3 | async-start | bytes 1048576 | tf_op jit(solution)/shard_map/all_to_all | solution.py:36
  103.8 2.2 %collective-permute-start.10 = (f32[8,256]{1,0:T(8,128)S(1)}, f32[8,256]{1,0:T(8,128)S(1)}, u32[]{:S(2)}, u32[]{:S(2)}) collective-permute-start(f32[8,256]{1,0:T(8,128)S(1)} %get-tuple-element.42), channel_id=1, source_target_pairs={{0,1},{1,0},{2,3},{3,2},{4,5},{5,4},{6,7},{7,6},{8,9},{9,8},{10,11... | collective-permute-start | bytes 24584 | tf_op jit(solution)/shard_map/ppermute | solution.py:28
  106.1 4.9 %shard_map.46 = f32[2048,256]{1,0:T(8,128)} custom-call(s32[1]{0:T(128)} %bitcast.5.core_ref, bf16[1024,4096]{1,0:T(8,128)(2,1)} %get-tuple-element.36.mix_ref, bf16[1024,384]{1,0:T(8,128)(2,1)S(1)} %bitcast.29, bf16[1024,384]{1,0:T(8,128)(2,1)S(1)} %shard_map.41.a_ref, bf16[1024,384]{1,0:T(8,128)(2,1)S(1)} %shard_map.42.b_ref, ...), custom_call_target="tpu_custom_call" | custom-call | flops 1073741824 | bytes 8388608 | tf_op jit(solution)/shard_map/pallas_call | solution.py:260
  110.9 1.9 %all-to-all-done.3 = f16[32,32,256]{2,1,0:T(8,128)(2,1)S(1)} async-done(((f16[32,32,256]{2,1,0:T(8,128)(2,1)}), f16[32,32,256]{2,1,0:T(8,128)(2,1)S(1)}, u32[]{:S(2)}, u32[]{:S(2)}) %all-to-all-start.3) | async-done | bytes 524320 | tf_op jit(solution)/shard_map/all_to_all | solution.py:36
  112.8 3.5 %collective-permute-start.9 = (f16[32,32,256]{2,1,0:T(8,128)(2,1)S(1)}, f16[32,32,256]{2,1,0:T(8,128)(2,1)S(1)}, u32[]{:S(2)}, u32[]{:S(2)}) collective-permute-start(f16[32,32,256]{2,1,0:T(8,128)(2,1)S(1)} %all-to-all-done.3), channel_id=1, source_target_pairs={{0,1},{1,0},{2,3},{3,2},{4,5},{5,4},{6,7},{7,6},{8,9},{9,8},{10,11... | collective-permute-start | bytes 1572872 | tf_op jit(solution)/shard_map/ppermute | solution.py:28
  (41 shorter events, 9.5 us)
Async XLA Ops:
  1.8 5.2 %collective-permute-start = (bf16[1024,384]{1,0:T(8,128)(2,1)S(1)}, bf16[1024,384]{1,0:T(8,128)(2,1)S(1)}, u32[]{:S(2)}, u32[]{:S(2)}) collective-permute-start(bf16[1024,384]{1,0:T(8,128)(2,1)S(1)} %shard_map.42.b_ref), channel_id=1, source_target_pairs={{0,1},{1,0},{2,3},{3,2},{4,5},{5,4},{6,7},{7,6},{8,9},{9,8},{10,11... | collective-permute-start | bytes 2359304 | tf_op jit(solution)/shard_map/ppermute | solution.py:28
  8.0 19.6 %all-to-all-start = ((bf16[32,32,384]{2,1,0:T(8,128)(2,1)}), bf16[32,32,384]{2,1,0:T(8,128)(2,1)S(1)}, u32[]{:S(2)}, u32[]{:S(2)}) async-start(bf16[32,32,384]{2,1,0:T(8,128)(2,1)} %bitcast.1), calls=%async_computation | async-start | bytes 1572864 | tf_op jit(solution)/shard_map/all_to_all | solution.py:36
  27.7 13.9 %collective-permute-start.4 = (bf16[1024,384]{1,0:T(8,128)(2,1)S(1)}, bf16[1024,384]{1,0:T(8,128)(2,1)S(1)}, u32[]{:S(2)}, u32[]{:S(2)}) collective-permute-start(bf16[1024,384]{1,0:T(8,128)(2,1)S(1)} %shard_map.41.a_ref), channel_id=1, source_target_pairs={{0,1},{1,0},{2,3},{3,2},{4,5},{5,4},{6,7},{7,6},{8,9},{9,8},{10,11... | collective-permute-start | bytes 2359304 | tf_op jit(solution)/shard_map/ppermute | solution.py:28
  29.6 9.7 %collective-permute-start.1 = (bf16[32,384]{1,0:T(8,128)(2,1)S(1)}, bf16[32,384]{1,0:T(8,128)(2,1)S(1)}, u32[]{:S(2)}, u32[]{:S(2)}) collective-permute-start(bf16[32,384]{1,0:T(8,128)(2,1)S(1)} %constant_dynamic-slice_fusion), channel_id=1, source_target_pairs={{0,4},{4,8},{8,12},{12,0},{1,5},{5,9},{9,13},{13,1},{2,6},{6,10},{... | collective-permute-start | bytes 73736 | tf_op jit(solution)/shard_map/ppermute | solution.py:32
  32.7 6.6 %collective-permute-start.2 = (bf16[32,384]{1,0:T(8,128)(2,1)S(1)}, bf16[32,384]{1,0:T(8,128)(2,1)S(1)}, u32[]{:S(2)}, u32[]{:S(2)}) collective-permute-start(bf16[32,384]{1,0:T(8,128)(2,1)S(1)} %constant_dynamic-slice_fusion), channel_id=1, source_target_pairs={{0,12},{4,0},{8,4},{12,8},{1,13},{5,1},{9,5},{13,9},{2,14},{6,2},{... | collective-permute-start | bytes 73736 | tf_op jit(solution)/shard_map/ppermute | solution.py:32
  34.9 6.6 %collective-permute-start.3 = (bf16[32,384]{1,0:T(8,128)(2,1)S(1)}, bf16[32,384]{1,0:T(8,128)(2,1)S(1)}, u32[]{:S(2)}, u32[]{:S(2)}) collective-permute-start(bf16[32,384]{1,0:T(8,128)(2,1)S(1)} %constant_dynamic-slice_fusion), channel_id=1, source_target_pairs={{0,8},{4,12},{8,0},{12,4},{1,9},{5,13},{9,1},{13,5},{2,10},{6,14},... | collective-permute-start | bytes 73736 | tf_op jit(solution)/shard_map/ppermute | solution.py:32
  41.8 0.9 copy-start
  42.6 16.3 %copy-start.1 = (bf16[1024,384]{1,0:T(8,128)(2,1)S(1)}, bf16[1024,384]{1,0:T(8,128)(2,1)}, u32[]{:S(2)}) copy-start(bf16[1024,384]{1,0:T(8,128)(2,1)} %copy-done) | copy-start | bytes 2359300
  70.0 14.2 %all-to-all-start.2 = ((f16[32,72,128]{2,1,0:T(8,128)(2,1)}), f16[32,72,128]{2,1,0:T(8,128)(2,1)}, u32[]{:S(2)}, u32[]{:S(2)}) async-start(f16[32,72,128]{2,1,0:T(8,128)(2,1)} %convert_element_type.42), calls=%async_computation.2 | async-start | bytes 1179648 | tf_op jit(solution)/shard_map/all_to_all | solution.py:36
  74.9 1.1 copy-start.2
  84.2 21.8 %collective-permute-start.8 = (f32[2048,256]{1,0:T(8,128)}, f32[2048,256]{1,0:T(8,128)}, u32[]{:S(2)}, u32[]{:S(2)}) collective-permute-start(f32[2048,256]{1,0:T(8,128)} %shard_map.44), channel_id=1, source_target_pairs={{0,1},{1,0},{2,3},{3,2},{4,5},{5,4},{6,7},{7,6},{8,9},{9,8},{10,11... | collective-permute-start | bytes 6291464 | tf_op jit(solution)/shard_map/ppermute | solution.py:28
  89.6 8.1 %collective-permute-start.5 = (f32[72,128]{1,0:T(8,128)S(1)}, f32[72,128]{1,0:T(8,128)S(1)}, u32[]{:S(2)}, u32[]{:S(2)}) collective-permute-start(f32[72,128]{1,0:T(8,128)S(1)} %maximum_bitcast_fusion.refs_0_), channel_id=1, source_target_pairs={{0,8},{4,12},{8,0},{12,4},{1,9},{5,13},{9,1},{13,5},{2,10},{6,14},... | collective-permute-start | bytes 110600 | tf_op jit(solution)/shard_map/ppermute | solution.py:32
  94.1 4.9 %collective-permute-start.6 = (f32[72,128]{1,0:T(8,128)S(1)}, f32[72,128]{1,0:T(8,128)S(1)}, u32[]{:S(2)}, u32[]{:S(2)}) collective-permute-start(f32[72,128]{1,0:T(8,128)S(1)} %maximum_bitcast_fusion.refs_0_), channel_id=1, source_target_pairs={{0,4},{4,8},{8,12},{12,0},{1,5},{5,9},{9,13},{13,1},{2,6},{6,10},{... | collective-permute-start | bytes 110600 | tf_op jit(solution)/shard_map/ppermute | solution.py:32
  94.1 4.9 %collective-permute-start.7 = (f32[72,128]{1,0:T(8,128)S(1)}, f32[72,128]{1,0:T(8,128)S(1)}, u32[]{:S(2)}, u32[]{:S(2)}) collective-permute-start(f32[72,128]{1,0:T(8,128)S(1)} %maximum_bitcast_fusion.refs_0_), channel_id=1, source_target_pairs={{0,12},{4,0},{8,4},{12,8},{1,13},{5,1},{9,5},{13,9},{2,14},{6,2},{... | collective-permute-start | bytes 110600 | tf_op jit(solution)/shard_map/ppermute | solution.py:32
  99.9 12.9 %all-to-all-start.3 = ((f16[32,32,256]{2,1,0:T(8,128)(2,1)}), f16[32,32,256]{2,1,0:T(8,128)(2,1)S(1)}, u32[]{:S(2)}, u32[]{:S(2)}) async-start(f16[32,32,256]{2,1,0:T(8,128)(2,1)} %broadcast_in_dim.11), calls=%async_computation.3 | async-start | bytes 1048576 | tf_op jit(solution)/shard_map/all_to_all | solution.py:36
  103.8 12.5 %collective-permute-start.10 = (f32[8,256]{1,0:T(8,128)S(1)}, f32[8,256]{1,0:T(8,128)S(1)}, u32[]{:S(2)}, u32[]{:S(2)}) collective-permute-start(f32[8,256]{1,0:T(8,128)S(1)} %get-tuple-element.42), channel_id=1, source_target_pairs={{0,1},{1,0},{2,3},{3,2},{4,5},{5,4},{6,7},{7,6},{8,9},{9,8},{10,11... | collective-permute-start | bytes 24584 | tf_op jit(solution)/shard_map/ppermute | solution.py:28
  112.8 5.0 %collective-permute-start.9 = (f16[32,32,256]{2,1,0:T(8,128)(2,1)S(1)}, f16[32,32,256]{2,1,0:T(8,128)(2,1)S(1)}, u32[]{:S(2)}, u32[]{:S(2)}) collective-permute-start(f16[32,32,256]{2,1,0:T(8,128)(2,1)S(1)} %all-to-all-done.3), channel_id=1, source_target_pairs={{0,1},{1,0},{2,3},{3,2},{4,5},{5,4},{6,7},{7,6},{8,9},{9,8},{10,11... | collective-permute-start | bytes 1572872 | tf_op jit(solution)/shard_map/ppermute | solution.py:28
